TPU v7x, 256 devices: a whole 4x4x8 slice. The times are simulated.
256 devices in a mesh: cent: 16 (over y, z_lo), pts: 16 (over x, z_hi, core).
Axes of the slice: x: 4, y: 4, z: 8 (z_hi: 2, z_lo: 4; z = z_hi * 4 + z_lo), core: 2. Of those that a mesh axis runs over, the one named last changes fastest.
Arguments:
- points: bfloat16 [32768, 1024], P('pts'), may hold values from -30 to 30
- center_one: bfloat16 [16384, 1024], P('cent'), may hold values from -9 to 9
- center_two: bfloat16 [4096, 1024], P('pts'), may hold values from -28 to 28
Outputs:
- level_one: bfloat16 [16384, 1024], P(('cent', 'pts'))
- level_two: bfloat16 [4096, 1024], P('pts')
All inputs are finite; a program needn't handle non-finite values.
Results may differ from a plain program's by a relative error of at most 0.0051.
Values may be sent and summed in bfloat16 or wider, within the bound.
No kernel may reach another device: no remote copies, remote signals or barrier semaphores. Data moves between devices by JAX's collectives and lax.ppermute only.
A program may use at most 64 MiB of HBM per device.

v0:
```python
import jax
import jax.numpy as jnp
from jax import lax
from jax.sharding import PartitionSpec as P

sharpness_coefficient = 100.0


def normalize_rows(values):
    return (values * lax.rsqrt(jnp.mean(values * values, axis=1, keepdims=True) + 1e-05)).astype(
        jnp.bfloat16
    )


def flipped_scaled_matrix(weights, queries):
    return lax.dot_general(
        weights, queries, (((0,), (0,)), ((), ())), preferred_element_type=jnp.float32
    )


def shards(points, center_one, center_two):
    embedding_dimension = points.shape[1]
    normalizing_multiplier = sharpness_coefficient / embedding_dimension
    logits = (
        jnp.dot(points, center_one.T, preferred_element_type=jnp.float32) * normalizing_multiplier
    )
    local_peak = jnp.max(logits, axis=1)
    powers = jnp.exp(logits - local_peak[:, None])
    row_peak = lax.pmax(local_peak, "cent")
    row_total = lax.psum(jnp.sum(powers * jnp.exp(local_peak - row_peak)[:, None], axis=1), "cent")
    weight_one = (powers * (jnp.exp(local_peak - row_peak) / row_total)[:, None]).astype(
        jnp.bfloat16
    )
    owned_rows = center_one.shape[0] // lax.axis_size("pts")
    first_row = lax.axis_index("pts") * owned_rows
    summed = lax.psum(flipped_scaled_matrix(weight_one, points), "pts")
    gathered = normalize_rows(summed + center_one.astype(jnp.float32))
    level_one = lax.dynamic_slice_in_dim(gathered, first_row, owned_rows, 0)
    logits_two = (
        jnp.dot(gathered, center_two.T, preferred_element_type=jnp.float32) * normalizing_multiplier
    )
    local_two = jnp.max(logits_two, axis=1)
    powers_two = jnp.exp(logits_two - local_two[:, None])
    second_level_peak = lax.pmax(local_two, "pts")
    total_two = lax.psum(
        jnp.sum(powers_two * jnp.exp(local_two - second_level_peak)[:, None], axis=1), "pts"
    )
    weight_two = (
        powers_two * (jnp.exp(local_two - second_level_peak) / total_two)[:, None]
    ).astype(jnp.bfloat16)
    owner_terms = lax.psum(flipped_scaled_matrix(weight_two, gathered), "cent")
    level_two = normalize_rows(owner_terms + center_two.astype(jnp.float32))
    return (level_one, level_two)


def solution(mesh):
    in_specs = (P("pts", None), P("cent", None), P("pts", None))
    out_specs = (P(("cent", "pts"), None), P("pts", None))
    return jax.shard_map(shards, mesh=mesh, in_specs=in_specs, out_specs=out_specs, check_vma=False)
```

profile of v0, /device:TPU:32, one launch (start us, length us, event | category | flops | bytes accessed | tf_op | source)
XLA Modules:
  0.0 617.4 jit_solution(4374070316027389)
XLA Ops:
  7.2 0.0 all-reduce.3.cloned.1.call-start
  7.2 10.6 %multiply_reduce_fusion.1 = (f32[2048]{0:T(1024)S(1)}, f32[2048,1024]{0,1:T(8,128)}) fusion(bf16[2048,1024]{1,0:T(8,128)(2,1)} %param.3, bf16[1024,1024]{1,0:T(8,128)(2,1)} %param.4), kind=kOutput, calls=%fused_computation.3 | convolution fusion | flops 4299159552 | bytes 14688256 | tf_op jit(solution)/shard_map/dot_general | solution.py:25
  17.8 40.5 %pmax.14 = f32[2048]{0:T(1024)S(1)} all-reduce(f32[2048]{0:T(1024)S(1)} %get-tuple-element.2), channel_id=1, replica_groups=mesh['cent'=16,'pts'=16] {'cent'}, use_global_device_ids=true, to_apply=%region_1.0 | all-reduce | flops 2048 | bytes 16384 | tf_op jit(solution)/shard_map/pmax | solution.py:29
  58.4 5.0 multiply_reduce_fusion
  63.4 44.1 %psum.28 = f32[2048]{0:T(1024)S(1)} all-reduce(f32[2048]{0:T(1024)S(1)} %multiply_reduce_fusion), channel_id=1, replica_groups=mesh['cent'=16,'pts'=16] {'cent'}, use_global_device_ids=true, to_apply=%region_3.0 | all-reduce | flops 2048 | bytes 16384 | tf_op jit(solution)/shard_map/psum | solution.py:30
  107.5 11.1 %fusion = f32[1024,1024]{1,0:T(8,128)} fusion(bf16[2048,1024]{1,0:T(8,128)(2,1)} %param.3, f32[2048,1024]{0,1:T(8,128)} %get-tuple-element.3, f32[2048]{0:T(1024)S(1)} %div.18, f32[2048]{0:T(1024)S(1)} %get-tuple-element.2), kind=kOutput, calls=%fused_computation.4 | convolution fusion | flops 4303355904 | bytes 16793600 | tf_op jit(solution)/shard_map/dot_general | solution.py:16
  118.6 0.0 all-reduce.3.cloned.1.call-update
  118.6 0.0 all-reduce.5.cloned.1.call-start
  118.7 224.8 %all-reduce.3.cloned.1.call-done = f32[1024,1024]{1,0:T(8,128)} async-done(((f32[1024,1024]{1,0:T(8,128)}), f32[1024,1024]{1,0:T(8,128)}) %all-reduce.3.cloned.1.call-update) | async-done | bytes 4194320 | tf_op jit(solution)/shard_map/psum | solution.py:36
  343.5 3.0 multiply_reduce_fusion.2
  346.5 0.5 copy-done
  346.9 0.7 copy-done.2
  347.6 0.5 multiply_convert_fusion.2
  348.1 0.5 copy-done.3
  348.7 0.7 fusion.8
  349.4 47.5 %pmax.15 = f32[1024]{0:T(1024)S(1)} all-reduce(f32[1024]{0:T(1024)S(1)} %get-tuple-element.4), channel_id=1, replica_groups=mesh['cent'=16,'pts'=16] {'pts'}, use_global_device_ids=true, to_apply=%region_7.0 | all-reduce | flops 1024 | bytes 8192 | tf_op jit(solution)/shard_map/pmax | solution.py:44
  397.0 0.2 multiply_reduce_fusion.4
  397.2 42.8 %psum.30 = f32[1024]{0:T(1024)S(1)} all-reduce(f32[1024]{0:T(1024)S(1)} %multiply_reduce_fusion.4), channel_id=1, replica_groups=mesh['cent'=16,'pts'=16] {'pts'}, use_global_device_ids=true, to_apply=%region_9.0 | all-reduce | flops 1024 | bytes 8192 | tf_op jit(solution)/shard_map/psum | solution.py:45
  439.9 1.7 fusion.4
  441.7 0.0 all-reduce.5.cloned.1.call-update
  441.7 0.7 constant_dynamic-slice_fusion
  442.4 164.3 %all-reduce.5.cloned.1.call-done = f32[256,1024]{1,0:T(8,128)} async-done(((f32[256,1024]{1,0:T(8,128)}), f32[256,1024]{1,0:T(8,128)}) %all-reduce.5.cloned.1.call-update) | async-done | bytes 1048592 | tf_op jit(solution)/shard_map/psum | solution.py:51
  606.7 1.6 multiply_reduce_fusion.3
  608.3 2.3 multiply_convert_fusion.3
  (11 shorter events, 0.1 us)
Async XLA Ops:
  7.2 336.3 %all-reduce.3.cloned.1.call-start = ((), (), s32[]{:S(2)}) async-start(), calls=%async_computation | async-start | bytes 8388608 | tf_op jit(solution)/shard_map/psum | solution.py:36
  118.6 224.9 %copy-start.1 = (bf16[1024,1024]{1,0:T(8,128)(2,1)S(1)}, bf16[1024,1024]{1,0:T(8,128)(2,1)}, u32[]{:S(2)}) copy-start(bf16[1024,1024]{1,0:T(8,128)(2,1)} %param.4) | copy-start | bytes 6291460
  118.6 488.1 %all-reduce.5.cloned.1.call-start = ((), (), s32[]{:S(2)}) async-start(), calls=%async_computation.1 | async-start | bytes 2097152 | tf_op jit(solution)/shard_map/psum | solution.py:51
  343.5 3.4 copy-start
  343.5 4.1 copy-start.2
  347.6 1.0 copy-start.3
Sparse Core Ops, SparseCore 0:
  118.7 224.6 all-reduce.2
  441.8 164.8 all-reduce.4
where the time goes:
time: 618 us; the launch traced here: 617 us
  waiting for transfers between devices  389 us (63%)
  blocking collectives  175 us (28%)
  matrix products  24.2 us (4%)
  between operations  14.1 us (2%)
  other arithmetic  12.6 us (2%)
    psum x1, waiting for transfers between devices, shards(): summed = lax.psum(flipped_scaled_matrix(weight_one, points), 'pts')  225 us
    psum x1, waiting for transfers between devices, shards(): owner_terms = lax.psum(flipped_scaled_matrix(weight_two, gathered), 'cent')  164 us
    pmax x1, blocking collectives, shards(): second_level_peak = lax.pmax(local_two, 'pts')  47.5 us
    psum x1, blocking collectives, shards(): lax.psum(jnp.sum(powers * jnp.exp(local_peak - row_peak)[:, None], axis=1...  44.1 us
    psum x1, blocking collectives, shards(): lax.psum(jnp.sum(powers_two * jnp.exp(local_two - second_level_peak)[:, N...  42.8 us
    pmax x1, blocking collectives, shards(): row_peak = lax.pmax(local_peak, 'cent')  40.5 us
    dot_general x2, matrix products, flipped_scaled_matrix(): lax.dot_general(weights, queries, (((0,), (0,)), ((), ())), preferred_ele...  12.8 us
  transfers between devices with their start and end apart: 2, of which 2 were waited for; matrix products, arithmetic and copies ran while one was open for 0% of the time, Pallas kernels for 0%

commit v1 on v0

v1 whole, which is shorter than its diff:
```python
import jax
import jax.numpy as jnp
from jax import lax
from jax.sharding import Mesh
from jax.sharding import PartitionSpec as P

sharpness_coefficient = 100.0
AXES = ("y", "zl", "x", "zh", "core")


def shifted(value, axis, step):
    size = lax.axis_size(axis)
    return lax.ppermute(value, axis, [(i, (i + step) % size) for i in range(size)])


def from_others(value, axis):
    return [shifted(value, axis, k) for k in range(1, lax.axis_size(axis))]


def merge(parts):
    peak = parts[0][0]
    for part in parts[1:]:
        peak = jnp.maximum(peak, part[0])
    total = sum(part[1] * jnp.exp(part[0] - peak) for part in parts)
    return jnp.stack([peak, total])


def normalize_rows(values):
    return (values * lax.rsqrt(jnp.mean(values * values, axis=-1, keepdims=True) + 1e-05)).astype(
        jnp.bfloat16
    )


def logits_of(centers, rows, scale):
    return (
        lax.dot_general(centers, rows, (((1,), (1,)), ((), ())), preferred_element_type=jnp.float32)
        * scale
    )


def softmax_parts(logits):
    peak = jnp.max(logits, axis=0)
    powers = jnp.exp(logits - peak[None, :])
    return powers, jnp.stack([peak, jnp.sum(powers, axis=0)])


def rescale(local, whole):
    return jnp.exp(local[0] - whole[0]) / whole[1]


def reduce_scatter(blocks, axis):
    size = lax.axis_size(axis)
    me = lax.axis_index(axis)
    take = lambda i: lax.dynamic_index_in_dim(blocks, lax.rem(i, size), 0, keepdims=False)
    got = [shifted(take(me + k).astype(jnp.bfloat16), axis, k) for k in range(1, size)]
    total = take(me)
    for part in got:
        total = total + part.astype(jnp.float32)
    return total


def shards(points, center_one, center_two):
    depth = points.shape[1]
    scale = sharpness_coefficient / depth
    nx, nh, nc = lax.axis_size("x"), lax.axis_size("zh"), lax.axis_size("core")
    ix, ih, ic = lax.axis_index("x"), lax.axis_index("zh"), lax.axis_index("core")
    held = center_one.shape[0]
    owned = held // (nx * nh * nc)

    some_two = jnp.concatenate([center_two] + from_others(center_two, "x"))
    some_two = jnp.concatenate([some_two] + from_others(some_two, "core"))

    powers, local = softmax_parts(logits_of(center_one, points, scale))
    whole = merge([local] + from_others(local, "y"))
    whole = merge([whole] + from_others(whole, "zl"))
    weight = (powers * rescale(local, whole)[None, :]).astype(jnp.bfloat16)
    sums = jnp.dot(weight, points, preferred_element_type=jnp.float32)
    sums = sums.reshape(nx, nh, nc, owned, depth)

    part = reduce_scatter(jnp.moveaxis(sums, 2, 0), "core")
    part = reduce_scatter(part, "x")
    other = shifted(part.astype(jnp.bfloat16), "zh", 1)
    mine = center_one.reshape(nx, nh, nc, owned, depth)
    mine = lax.dynamic_index_in_dim(mine, ic, 2, keepdims=False)
    mine = lax.dynamic_index_in_dim(mine, ix, 0, keepdims=False)
    rows = normalize_rows(part + other.astype(jnp.float32) + mine.astype(jnp.float32))
    level_one = lax.dynamic_index_in_dim(rows, ih, 0, keepdims=False)
    rows = rows.reshape(nh * owned, depth)

    _, own = softmax_parts(logits_of(some_two, rows, scale))
    own = merge([own, shifted(own, "zh", 1)])
    own = jnp.concatenate([own] + from_others(own, "x"), axis=1)
    whole_two = jnp.concatenate([own] + from_others(own, "core"), axis=1)

    rows = jnp.concatenate([rows] + from_others(rows, "x"))
    rows = jnp.concatenate([rows] + from_others(rows, "core"))
    logits = logits_of(center_two, rows, scale)
    weight = (jnp.exp(logits - whole_two[0][None, :]) * (1.0 / whole_two[1])[None, :]).astype(jnp.bfloat16)
    sums = jnp.dot(weight, rows, preferred_element_type=jnp.float32)

    ny, nl = lax.axis_size("y"), lax.axis_size("zl")
    iy, il = lax.axis_index("y"), lax.axis_index("zl")
    sums = sums.reshape(ny, nl, -1, depth)
    part = reduce_scatter(reduce_scatter(sums, "y"), "zl")
    mine = center_two.reshape(ny, nl, -1, depth)
    mine = lax.dynamic_index_in_dim(mine, iy, 0, keepdims=False)
    mine = lax.dynamic_index_in_dim(mine, il, 0, keepdims=False)
    done = normalize_rows(part + mine.astype(jnp.float32))
    for axis in ("zl", "y"):
        size, me = lax.axis_size(axis), lax.axis_index(axis)
        parts = jnp.stack([done] + from_others(done, axis))
        order = lax.rem(me - jnp.arange(size) + size, size)
        done = jnp.take(parts, order, axis=0)
        done = done.reshape((-1,) + done.shape[2:])
    return level_one, done


def solution(mesh):
    fine = Mesh(mesh.devices.reshape(4, 4, 4, 2, 2), AXES)
    cent, pts = ("y", "zl"), ("x", "zh", "core")
    in_specs = (P(pts, None), P(cent, None), P(pts, None))
    out_specs = (P(cent + pts, None), P(pts, None))
    return jax.shard_map(shards, mesh=fine, in_specs=in_specs, out_specs=out_specs, check_vma=False)
```

time: 618 us -> 174 us (0.28)
  waiting for transfers between devices: 389 us -> 72.3 us
  blocking collectives: 175 us -> 0 us
  starting transfers between devices: 0.08 us -> 56.6 us
  between operations: 14.1 us -> 1.02 us
  local copies, waits for them, and re-layouts: 2.36 us -> 10.2 us
    psum x2 -> x0, waiting for transfers between devices: 389 us -> none  [the longest x1 225 us: shards(): summed = lax.psum(flipped_scaled_matrix(weight_one, points), 'pts')]
    pmax x2 -> x0, blocking collectives: 88 us -> none  [the longest x1 47.5 us: shards(): second_level_peak = lax.pmax(local_two, 'pts')]
    psum x2 -> x0, blocking collectives: 86.9 us -> none  [the longest x1 44.1 us: shards(): lax.psum(jnp.sum(powers * jnp.exp(local_peak - row_peak)[:, None], axis=1...]
    ppermute x0 -> x36, waiting for transfers between devices: none -> 72.3 us  [shifted(): lax.ppermute(value, axis, [(i, (i + step) % size) for i in range(size)])]
    ppermute x0 -> x36, starting transfers between devices: none -> 56.6 us  [shifted(): lax.ppermute(value, axis, [(i, (i + step) % size) for i in range(size)])]
    reduce_sum x4, other arithmetic: 9.77 us -> 3.07 us  [the longest x2 1.7 us: softmax_parts(): return (powers, jnp.stack([peak, jnp.sum(powers, axis=0)]))]
  transfers between devices with their start and end apart: 2 -> 36, of which waited for: 2 -> 26; matrix products, arithmetic and copies ran while one was open for 0% -> 7% of each run, Pallas kernels for 0% -> 0%
where the time goes in v1:
time: 174 us; the launch traced here: 173 us
  waiting for transfers between devices  72.3 us (42%)
  starting transfers between devices  56.6 us (33%)
  matrix products  21.1 us (12%)
  other arithmetic  11.8 us (7%)
  local copies, waits for them, and re-layouts  10.2 us (6%)
    ppermute x36, waiting for transfers between devices, shifted(): lax.ppermute(value, axis, [(i, (i + step) % size) for i in range(size)])  72.3 us
    ppermute x36, starting transfers between devices, shifted(): lax.ppermute(value, axis, [(i, (i + step) % size) for i in range(size)])  56.6 us
    dot_general x2, matrix products, logits_of(): lax.dot_general(centers, rows, (((1,), (1,)), ((), ())), preferred_elemen...  8.32 us
    dot_general x1, matrix products, shards(): sums = jnp.dot(weight, points, preferred_element_type=jnp.float32)  8.23 us
    unnamed x29, local copies, waits for them, and re-layouts  7.43 us
    dot_general x1, matrix products, shards(): sums = jnp.dot(weight, rows, preferred_element_type=jnp.float32)  4.54 us
  transfers between devices with their start and end apart: 36, of which 26 were waited for; matrix products, arithmetic and copies ran while one was open for 7% of the time, Pallas kernels for 0%

profile of v1, /device:TPU:32, one launch (start us, length us, event | category | flops | bytes accessed | tf_op | source)
XLA Modules:
  0.0 172.9 jit_solution(17077964051462121100)
XLA Ops:
  0.6 7.0 %multiply_reduce_fusion = (f32[2048]{0:T(1024)S(1)}, f32[1024,2048]{1,0:T(8,128)S(1)}) fusion(bf16[1024,1024]{1,0:T(8,128)(2,1)} %param.4, bf16[2048,1024]{1,0:T(8,128)(2,1)} %param.3), kind=kOutput, calls=%fused_computation.4 | convolution fusion | flops 4299159552 | bytes 14688256 | tf_op jit(solution)/shard_map/dot_general | solution.py:36
  12.6 2.9 %collective-permute-start.1 = (f32[2,2048]{1,0:T(2,128)S(1)}, f32[2,2048]{1,0:T(2,128)S(1)}, u32[]{:S(2)}, u32[]{:S(2)}) collective-permute-start(f32[2,2048]{1,0:T(2,128)S(1)} %pad_maximum_fusion.4), channel_id=1, source_target_pairs={{0,128},{64,192},{128,0},{192,64},{1,129},{65,193},{129,1},{193,65... | collective-permute-start | bytes 49160 | tf_op jit(solution)/shard_map/ppermute | solution.py:13
  26.7 8.2 %fusion.1 = f32[1024,1024]{1,0:T(8,128)S(1)} fusion(bf16[2048,1024]{1,0:T(8,128)(2,1)} %param.3, f32[1024,2048]{1,0:T(8,128)} %copy-done, f32[2048]{0:T(1024)S(1)} %bitcast.129, f32[2048]{0:T(1024)S(1)} %get-tuple-element.23), kind=kOutput, calls=%fused_computation.6 | convolution fusion | flops 4303355904 | bytes 16793600 | tf_op jit(solution)/shard_map/dot_general | solution.py:77
  38.7 2.7 %collective-permute-start.16 = (bf16[256,1024]{1,0:T(8,128)(2,1)S(1)}, bf16[256,1024]{1,0:T(8,128)(2,1)S(1)}, u32[]{:S(2)}, u32[]{:S(2)}) collective-permute-start(bf16[256,1024]{1,0:T(8,128)(2,1)S(1)} %copy-done.2), channel_id=1, source_target_pairs={{0,8},{4,12},{8,0},{12,4},{1,9},{5,13},{9,1},{13,5},{2,10},{6,14},... | collective-permute-start | bytes 1572872 | tf_op jit(solution)/shard_map/ppermute | solution.py:13
  42.9 2.4 %bitcast_add_fusion = f32[4,2,64,1024]{3,2,1,0:T(8,128)S(1)} fusion(bf16[4,2,64,1024]{3,2,1,0:T(8,128)(2,1)} %collective-permute-done.6, f32[4,2,2,64,1024]{4,3,2,1,0:T(8,128)} %bitcast.110, s32[]{:T(128)S(6)} %select_n.124), kind=kLoop, calls=%fused_computation.12 | loop fusion | flops 1048576 | bytes 5242884 | tf_op jit(solution)/shard_map/add | solution.py:58
  46.9 6.3 %collective-permute-done.15 = bf16[256,1024]{1,0:T(8,128)(2,1)} collective-permute-done((bf16[256,1024]{1,0:T(8,128)(2,1)S(1)}, bf16[256,1024]{1,0:T(8,128)(2,1)}, u32[]{:S(2)}, u32[]{:S(2)}) %collective-permute-start.15) | collective-permute-done | bytes 524320 | tf_op jit(solution)/shard_map/ppermute | solution.py:13
  54.8 10.6 %collective-permute-done.16 = bf16[256,1024]{1,0:T(8,128)(2,1)S(1)} collective-permute-done((bf16[256,1024]{1,0:T(8,128)(2,1)S(1)}, bf16[256,1024]{1,0:T(8,128)(2,1)S(1)}, u32[]{:S(2)}, u32[]{:S(2)}) %collective-permute-start.16) | collective-permute-done | bytes 524320 | tf_op jit(solution)/shard_map/ppermute | solution.py:13
  66.3 2.6 %pad_maximum_fusion = bf16[1024,1024]{1,0:T(8,128)(2,1)} fusion(bf16[256,1024]{1,0:T(8,128)(2,1)S(1)} %collective-permute-done.17, bf16[256,1024]{1,0:T(8,128)(2,1)S(1)} %collective-permute-done.16, bf16[256,1024]{1,0:T(8,128)(2,1)} %collective-permute-done.15, bf16[256,1024]{1,0:T(8,128)(2,1)S(1)} %copy-done.2), kind=kLoop, calls=%fused_computation.11 | loop fusion | flops 8388608 | bytes 4194304 | tf_op jit(solution)/shard_map/concatenate | solution.py:70
  69.5 6.6 %collective-permute-done.8 = bf16[2,64,1024]{2,1,0:T(8,128)(2,1)S(1)} collective-permute-done((bf16[2,64,1024]{2,1,0:T(8,128)(2,1)S(1)}, bf16[2,64,1024]{2,1,0:T(8,128)(2,1)S(1)}, u32[]{:S(2)}, u32[]{:S(2)}) %collective-permute-start.8) | collective-permute-done | bytes 262176 | tf_op jit(solution)/shard_map/ppermute | solution.py:13
  77.1 6.3 %collective-permute-start.10 = (bf16[2,64,1024]{2,1,0:T(8,128)(2,1)}, bf16[2,64,1024]{2,1,0:T(8,128)(2,1)S(1)}, u32[]{:S(2)}, u32[]{:S(2)}) collective-permute-start(bf16[2,64,1024]{2,1,0:T(8,128)(2,1)} %get-tuple-element.4), channel_id=1, source_target_pairs={{0,2},{2,0},{1,3},{3,1},{4,6},{6,4},{5,7},{7,5},{8,10},{10,8},{9,1... | collective-permute-start | bytes 786440 | tf_op jit(solution)/shard_map/ppermute | solution.py:13
  84.6 10.8 %collective-permute-done.10 = bf16[2,64,1024]{2,1,0:T(8,128)(2,1)S(1)} collective-permute-done((bf16[2,64,1024]{2,1,0:T(8,128)(2,1)}, bf16[2,64,1024]{2,1,0:T(8,128)(2,1)S(1)}, u32[]{:S(2)}, u32[]{:S(2)}) %collective-permute-start.10) | collective-permute-done | bytes 262176 | tf_op jit(solution)/shard_map/ppermute | solution.py:13
  98.8 3.1 %collective-permute-start.12 = (bf16[128,1024]{1,0:T(8,128)(2,1)S(1)}, bf16[128,1024]{1,0:T(8,128)(2,1)S(1)}, u32[]{:S(2)}, u32[]{:S(2)}) collective-permute-start(bf16[128,1024]{1,0:T(8,128)(2,1)S(1)} %bitcast.104), channel_id=1, source_target_pairs={{0,8},{4,12},{8,0},{12,4},{1,9},{5,13},{9,1},{13,5},{2,10},{6,14},... | collective-permute-start | bytes 786440 | tf_op jit(solution)/shard_map/ppermute | solution.py:13
  102.9 3.8 %collective-permute-done.11 = bf16[128,1024]{1,0:T(8,128)(2,1)S(1)} collective-permute-done((bf16[128,1024]{1,0:T(8,128)(2,1)S(1)}, bf16[128,1024]{1,0:T(8,128)(2,1)S(1)}, u32[]{:S(2)}, u32[]{:S(2)}) %collective-permute-start.11) | collective-permute-done | bytes 262176 | tf_op jit(solution)/shard_map/ppermute | solution.py:13
  106.7 6.4 %collective-permute-done.12 = bf16[128,1024]{1,0:T(8,128)(2,1)S(1)} collective-permute-done((bf16[128,1024]{1,0:T(8,128)(2,1)S(1)}, bf16[128,1024]{1,0:T(8,128)(2,1)S(1)}, u32[]{:S(2)}, u32[]{:S(2)}) %collective-permute-start.12) | collective-permute-done | bytes 262176 | tf_op jit(solution)/shard_map/ppermute | solution.py:13
  115.1 5.4 %collective-permute-start.19 = (f32[2,128]{1,0:T(2,128)S(1)}, f32[2,128]{1,0:T(2,128)S(1)}, u32[]{:S(2)}, u32[]{:S(2)}) collective-permute-start(f32[2,128]{1,0:T(2,128)S(1)} %pad_maximum_fusion.7), channel_id=1, source_target_pairs={{0,2},{2,0},{1,3},{3,1},{4,6},{6,4},{5,7},{7,5},{8,10},{10,8},{9,1... | collective-permute-start | bytes 3080 | tf_op jit(solution)/shard_map/ppermute | solution.py:13
  120.5 2.1 %collective-permute-done.19 = f32[2,128]{1,0:T(2,128)S(1)} collective-permute-done((f32[2,128]{1,0:T(2,128)S(1)}, f32[2,128]{1,0:T(2,128)S(1)}, u32[]{:S(2)}, u32[]{:S(2)}) %collective-permute-start.19) | collective-permute-done | bytes 1056 | tf_op jit(solution)/shard_map/ppermute | solution.py:13
  122.8 3.6 %collective-permute-start.21 = (f32[2,128]{1,0:T(2,128)S(1)}, f32[2,128]{1,0:T(2,128)S(1)}, u32[]{:S(2)}, u32[]{:S(2)}) collective-permute-start(f32[2,128]{1,0:T(2,128)S(1)} %get-tuple-element.21), channel_id=1, source_target_pairs={{0,8},{4,12},{8,0},{12,4},{1,9},{5,13},{9,1},{13,5},{2,10},{6,14},... | collective-permute-start | bytes 3080 | tf_op jit(solution)/shard_map/ppermute | solution.py:13
  132.9 4.5 %fusion.10 = f32[256,1024]{1,0:T(8,128)S(1)} fusion(bf16[1024,1024]{1,0:T(8,128)(2,1)} %copy-done.8, bf16[256,1024]{1,0:T(8,128)(2,1)S(1)} %copy-done.2, f32[1024]{0:T(1024)S(1)} %bitcast.132, f32[1024]{0:T(1024)S(1)} %bitcast.131), kind=kOutput, calls=%fused_computation.22 | convolution fusion | flops 1074790400 | bytes 3678208 | tf_op jit(solution)/shard_map/dot_general | solution.py:99
  137.8 3.8 %collective-permute-start.25 = (bf16[4,16,1024]{2,1,0:T(8,128)(2,1)S(1)}, bf16[4,16,1024]{2,1,0:T(8,128)(2,1)S(1)}, u32[]{:S(2)}, u32[]{:S(2)}) collective-permute-start(bf16[4,16,1024]{2,1,0:T(8,128)(2,1)S(1)} %get-tuple-element.13), channel_id=1, source_target_pairs={{0,128},{64,192},{128,0},{192,64},{1,129},{65,193},{129,1},{193,65... | collective-permute-start | bytes 393224 | tf_op jit(solution)/shard_map/ppermute | solution.py:13
  142.1 2.3 %collective-permute-done.24 = bf16[4,16,1024]{2,1,0:T(8,128)(2,1)S(1)} collective-permute-done((bf16[4,16,1024]{2,1,0:T(8,128)(2,1)S(1)}, bf16[4,16,1024]{2,1,0:T(8,128)(2,1)S(1)}, u32[]{:S(2)}, u32[]{:S(2)}) %collective-permute-start.24) | collective-permute-done | bytes 131104 | tf_op jit(solution)/shard_map/ppermute | solution.py:13
  144.4 3.6 %collective-permute-done.25 = bf16[4,16,1024]{2,1,0:T(8,128)(2,1)S(1)} collective-permute-done((bf16[4,16,1024]{2,1,0:T(8,128)(2,1)S(1)}, bf16[4,16,1024]{2,1,0:T(8,128)(2,1)S(1)}, u32[]{:S(2)}, u32[]{:S(2)}) %collective-permute-start.25) | collective-permute-done | bytes 131104 | tf_op jit(solution)/shard_map/ppermute | solution.py:13
  163.2 3.2 %collective-permute-start.34 = (bf16[64,1024]{1,0:T(8,128)(2,1)S(1)}, bf16[64,1024]{1,0:T(8,128)(2,1)S(1)}, u32[]{:S(2)}, u32[]{:S(2)}) collective-permute-start(bf16[64,1024]{1,0:T(8,128)(2,1)S(1)} %bitcast_select_fusion.1), channel_id=1, source_target_pairs={{0,128},{64,192},{128,0},{192,64},{1,129},{65,193},{129,1},{193,65... | collective-permute-start | bytes 393224 | tf_op jit(solution)/shard_map/ppermute | solution.py:13
  166.5 2.1 %collective-permute-done.33 = bf16[64,1024]{1,0:T(8,128)(2,1)S(1)} collective-permute-done((bf16[64,1024]{1,0:T(8,128)(2,1)S(1)}, bf16[64,1024]{1,0:T(8,128)(2,1)S(1)}, u32[]{:S(2)}, u32[]{:S(2)}) %collective-permute-start.33) | collective-permute-done | bytes 131104 | tf_op jit(solution)/shard_map/ppermute | solution.py:13
  168.6 2.1 %collective-permute-done.34 = bf16[64,1024]{1,0:T(8,128)(2,1)S(1)} collective-permute-done((bf16[64,1024]{1,0:T(8,128)(2,1)S(1)}, bf16[64,1024]{1,0:T(8,128)(2,1)S(1)}, u32[]{:S(2)}, u32[]{:S(2)}) %collective-permute-start.34) | collective-permute-done | bytes 131104 | tf_op jit(solution)/shard_map/ppermute | solution.py:13
  (128 shorter events, 59.3 us)
Async XLA Ops:
  11.0 5.9 %collective-permute-start = (f32[2,2048]{1,0:T(2,128)S(1)}, f32[2,2048]{1,0:T(2,128)S(1)}, u32[]{:S(2)}, u32[]{:S(2)}) collective-permute-start(f32[2,2048]{1,0:T(2,128)S(1)} %pad_maximum_fusion.4), channel_id=1, source_target_pairs={{0,64},{64,128},{128,192},{192,0},{1,65},{65,129},{129,193},{193,1... | collective-permute-start | bytes 49160 | tf_op jit(solution)/shard_map/ppermute | solution.py:13
  12.6 5.2 %collective-permute-start.1 = (f32[2,2048]{1,0:T(2,128)S(1)}, f32[2,2048]{1,0:T(2,128)S(1)}, u32[]{:S(2)}, u32[]{:S(2)}) collective-permute-start(f32[2,2048]{1,0:T(2,128)S(1)} %pad_maximum_fusion.4), channel_id=1, source_target_pairs={{0,128},{64,192},{128,0},{192,64},{1,129},{65,193},{129,1},{193,65... | collective-permute-start | bytes 49160 | tf_op jit(solution)/shard_map/ppermute | solution.py:13
  19.4 5.4 %collective-permute-start.3 = (f32[2,2048]{1,0:T(2,128)S(1)}, f32[2,2048]{1,0:T(2,128)S(1)}, u32[]{:S(2)}, u32[]{:S(2)}) collective-permute-start(f32[2,2048]{1,0:T(2,128)S(1)} %pad_maximum_fusion.5), channel_id=1, source_target_pairs={{0,16},{16,32},{32,48},{48,0},{1,17},{17,33},{33,49},{49,1},{2,18}... | collective-permute-start | bytes 49160 | tf_op jit(solution)/shard_map/ppermute | solution.py:13
  37.0 5.9 %collective-permute-start.6 = (bf16[4,2,64,1024]{3,2,1,0:T(8,128)(2,1)S(1)}, bf16[4,2,64,1024]{3,2,1,0:T(8,128)(2,1)}, u32[]{:S(2)}, u32[]{:S(2)}) collective-permute-start(bf16[4,2,64,1024]{3,2,1,0:T(8,128)(2,1)S(1)} %fusion.9), channel_id=1, source_target_pairs={{0,1},{1,0},{2,3},{3,2},{4,5},{5,4},{6,7},{7,6},{8,9},{9,8},{10,11... | collective-permute-start | bytes 3145736 | tf_op jit(solution)/shard_map/ppermute | solution.py:13
  37.1 16.1 %collective-permute-start.15 = (bf16[256,1024]{1,0:T(8,128)(2,1)S(1)}, bf16[256,1024]{1,0:T(8,128)(2,1)}, u32[]{:S(2)}, u32[]{:S(2)}) collective-permute-start(bf16[256,1024]{1,0:T(8,128)(2,1)S(1)} %copy-done.2), channel_id=1, source_target_pairs={{0,4},{4,8},{8,12},{12,0},{1,5},{5,9},{9,13},{13,1},{2,6},{6,10},{... | collective-permute-start | bytes 1572872 | tf_op jit(solution)/shard_map/ppermute | solution.py:13
  38.7 26.7 %collective-permute-start.16 = (bf16[256,1024]{1,0:T(8,128)(2,1)S(1)}, bf16[256,1024]{1,0:T(8,128)(2,1)S(1)}, u32[]{:S(2)}, u32[]{:S(2)}) collective-permute-start(bf16[256,1024]{1,0:T(8,128)(2,1)S(1)} %copy-done.2), channel_id=1, source_target_pairs={{0,8},{4,12},{8,0},{12,4},{1,9},{5,13},{9,1},{13,5},{2,10},{6,14},... | collective-permute-start | bytes 1572872 | tf_op jit(solution)/shard_map/ppermute | solution.py:13
  41.4 24.0 %collective-permute-start.17 = (bf16[256,1024]{1,0:T(8,128)(2,1)S(1)}, bf16[256,1024]{1,0:T(8,128)(2,1)S(1)}, u32[]{:S(2)}, u32[]{:S(2)}) collective-permute-start(bf16[256,1024]{1,0:T(8,128)(2,1)S(1)} %copy-done.2), channel_id=1, source_target_pairs={{0,12},{4,0},{8,4},{12,8},{1,13},{5,1},{9,5},{13,9},{2,14},{6,2},{... | collective-permute-start | bytes 1572872 | tf_op jit(solution)/shard_map/ppermute | solution.py:13
  45.4 24.2 %collective-permute-start.7 = (bf16[2,64,1024]{2,1,0:T(8,128)(2,1)S(1)}, bf16[2,64,1024]{2,1,0:T(8,128)(2,1)S(1)}, u32[]{:S(2)}, u32[]{:S(2)}) collective-permute-start(bf16[2,64,1024]{2,1,0:T(8,128)(2,1)S(1)} %get-tuple-element.8), channel_id=1, source_target_pairs={{0,4},{4,8},{8,12},{12,0},{1,5},{5,9},{9,13},{13,1},{2,6},{6,10},{... | collective-permute-start | bytes 786440 | tf_op jit(solution)/shard_map/ppermute | solution.py:13
  46.0 30.1 %collective-permute-start.8 = (bf16[2,64,1024]{2,1,0:T(8,128)(2,1)S(1)}, bf16[2,64,1024]{2,1,0:T(8,128)(2,1)S(1)}, u32[]{:S(2)}, u32[]{:S(2)}) collective-permute-start(bf16[2,64,1024]{2,1,0:T(8,128)(2,1)S(1)} %get-tuple-element.10), channel_id=1, source_target_pairs={{0,8},{4,12},{8,0},{12,4},{1,9},{5,13},{9,1},{13,5},{2,10},{6,14},... | collective-permute-start | bytes 786440 | tf_op jit(solution)/shard_map/ppermute | solution.py:13
  53.3 22.9 %collective-permute-start.9 = (bf16[2,64,1024]{2,1,0:T(8,128)(2,1)S(1)}, bf16[2,64,1024]{2,1,0:T(8,128)(2,1)S(1)}, u32[]{:S(2)}, u32[]{:S(2)}) collective-permute-start(bf16[2,64,1024]{2,1,0:T(8,128)(2,1)S(1)} %get-tuple-element.9), channel_id=1, source_target_pairs={{0,12},{4,0},{8,4},{12,8},{1,13},{5,1},{9,5},{13,9},{2,14},{6,2},{... | collective-permute-start | bytes 786440 | tf_op jit(solution)/shard_map/ppermute | solution.py:13
  68.9 44.4 %collective-permute-start.18 = (bf16[1024,1024]{1,0:T(8,128)(2,1)}, bf16[1024,1024]{1,0:T(8,128)(2,1)S(1)}, u32[]{:S(2)}, u32[]{:S(2)}) collective-permute-start(bf16[1024,1024]{1,0:T(8,128)(2,1)} %pad_maximum_fusion), channel_id=1, source_target_pairs={{0,1},{1,0},{2,3},{3,2},{4,5},{5,4},{6,7},{7,6},{8,9},{9,8},{10,11... | collective-permute-start | bytes 6291464 | tf_op jit(solution)/shard_map/ppermute | solution.py:13
  77.1 18.3 %collective-permute-start.10 = (bf16[2,64,1024]{2,1,0:T(8,128)(2,1)}, bf16[2,64,1024]{2,1,0:T(8,128)(2,1)S(1)}, u32[]{:S(2)}, u32[]{:S(2)}) collective-permute-start(bf16[2,64,1024]{2,1,0:T(8,128)(2,1)} %get-tuple-element.4), channel_id=1, source_target_pairs={{0,2},{2,0},{1,3},{3,1},{4,6},{6,4},{5,7},{7,5},{8,10},{10,8},{9,1... | collective-permute-start | bytes 786440 | tf_op jit(solution)/shard_map/ppermute | solution.py:13
  97.8 8.9 %collective-permute-start.11 = (bf16[128,1024]{1,0:T(8,128)(2,1)S(1)}, bf16[128,1024]{1,0:T(8,128)(2,1)S(1)}, u32[]{:S(2)}, u32[]{:S(2)}) collective-permute-start(bf16[128,1024]{1,0:T(8,128)(2,1)S(1)} %bitcast.103), channel_id=1, source_target_pairs={{0,4},{4,8},{8,12},{12,0},{1,5},{5,9},{9,13},{13,1},{2,6},{6,10},{... | collective-permute-start | bytes 786440 | tf_op jit(solution)/shard_map/ppermute | solution.py:13
  98.8 14.3 %collective-permute-start.12 = (bf16[128,1024]{1,0:T(8,128)(2,1)S(1)}, bf16[128,1024]{1,0:T(8,128)(2,1)S(1)}, u32[]{:S(2)}, u32[]{:S(2)}) collective-permute-start(bf16[128,1024]{1,0:T(8,128)(2,1)S(1)} %bitcast.104), channel_id=1, source_target_pairs={{0,8},{4,12},{8,0},{12,4},{1,9},{5,13},{9,1},{13,5},{2,10},{6,14},... | collective-permute-start | bytes 786440 | tf_op jit(solution)/shard_map/ppermute | solution.py:13
  101.8 11.2 %collective-permute-start.13 = (bf16[128,1024]{1,0:T(8,128)(2,1)S(1)}, bf16[128,1024]{1,0:T(8,128)(2,1)S(1)}, u32[]{:S(2)}, u32[]{:S(2)}) collective-permute-start(bf16[128,1024]{1,0:T(8,128)(2,1)S(1)} %bitcast.105), channel_id=1, source_target_pairs={{0,12},{4,0},{8,4},{12,8},{1,13},{5,1},{9,5},{13,9},{2,14},{6,2},{... | collective-permute-start | bytes 786440 | tf_op jit(solution)/shard_map/ppermute | solution.py:13
  113.2 18.3 %collective-permute-start.14 = (bf16[512,1024]{1,0:T(8,128)(2,1)S(1)}, bf16[512,1024]{1,0:T(8,128)(2,1)S(1)}, u32[]{:S(2)}, u32[]{:S(2)}) collective-permute-start(bf16[512,1024]{1,0:T(8,128)(2,1)S(1)} %pad_maximum_fusion.1), channel_id=1, source_target_pairs={{0,1},{1,0},{2,3},{3,2},{4,5},{5,4},{6,7},{7,6},{8,9},{9,8},{10,11... | collective-permute-start | bytes 3145736 | tf_op jit(solution)/shard_map/ppermute | solution.py:13
  115.1 7.6 %collective-permute-start.19 = (f32[2,128]{1,0:T(2,128)S(1)}, f32[2,128]{1,0:T(2,128)S(1)}, u32[]{:S(2)}, u32[]{:S(2)}) collective-permute-start(f32[2,128]{1,0:T(2,128)S(1)} %pad_maximum_fusion.7), channel_id=1, source_target_pairs={{0,2},{2,0},{1,3},{3,1},{4,6},{6,4},{5,7},{7,5},{8,10},{10,8},{9,1... | collective-permute-start | bytes 3080 | tf_op jit(solution)/shard_map/ppermute | solution.py:13
  137.5 6.9 %collective-permute-start.24 = (bf16[4,16,1024]{2,1,0:T(8,128)(2,1)S(1)}, bf16[4,16,1024]{2,1,0:T(8,128)(2,1)S(1)}, u32[]{:S(2)}, u32[]{:S(2)}) collective-permute-start(bf16[4,16,1024]{2,1,0:T(8,128)(2,1)S(1)} %get-tuple-element.11), channel_id=1, source_target_pairs={{0,64},{64,128},{128,192},{192,0},{1,65},{65,129},{129,193},{193,1... | collective-permute-start | bytes 393224 | tf_op jit(solution)/shard_map/ppermute | solution.py:13
  137.8 10.2 %collective-permute-start.25 = (bf16[4,16,1024]{2,1,0:T(8,128)(2,1)S(1)}, bf16[4,16,1024]{2,1,0:T(8,128)(2,1)S(1)}, u32[]{:S(2)}, u32[]{:S(2)}) collective-permute-start(bf16[4,16,1024]{2,1,0:T(8,128)(2,1)S(1)} %get-tuple-element.13), channel_id=1, source_target_pairs={{0,128},{64,192},{128,0},{192,64},{1,129},{65,193},{129,1},{193,65... | collective-permute-start | bytes 393224 | tf_op jit(solution)/shard_map/ppermute | solution.py:13
  141.6 6.4 %collective-permute-start.26 = (bf16[4,16,1024]{2,1,0:T(8,128)(2,1)S(1)}, bf16[4,16,1024]{2,1,0:T(8,128)(2,1)S(1)}, u32[]{:S(2)}, u32[]{:S(2)}) collective-permute-start(bf16[4,16,1024]{2,1,0:T(8,128)(2,1)S(1)} %get-tuple-element.12), channel_id=1, source_target_pairs={{0,192},{64,0},{128,64},{192,128},{1,193},{65,1},{129,65},{193,129... | collective-permute-start | bytes 393224 | tf_op jit(solution)/shard_map/ppermute | solution.py:13
  148.5 5.5 %collective-permute-start.29 = (bf16[16,1024]{1,0:T(8,128)(2,1)S(1)}, bf16[16,1024]{1,0:T(8,128)(2,1)S(1)}, u32[]{:S(2)}, u32[]{:S(2)}) collective-permute-start(bf16[16,1024]{1,0:T(8,128)(2,1)S(1)} %get-tuple-element.15), channel_id=1, source_target_pairs={{0,48},{16,0},{32,16},{48,32},{1,49},{17,1},{33,17},{49,33},{2,50}... | collective-permute-start | bytes 98312 | tf_op jit(solution)/shard_map/ppermute | solution.py:13
  154.3 5.3 %collective-permute-start.30 = (bf16[16,1024]{1,0:T(8,128)(2,1)S(1)}, bf16[16,1024]{1,0:T(8,128)(2,1)S(1)}, u32[]{:S(2)}, u32[]{:S(2)}) collective-permute-start(bf16[16,1024]{1,0:T(8,128)(2,1)S(1)} %multiply_convert_fusion.3), channel_id=1, source_target_pairs={{0,16},{16,32},{32,48},{48,0},{1,17},{17,33},{33,49},{49,1},{2,18}... | collective-permute-start | bytes 98312 | tf_op jit(solution)/shard_map/ppermute | solution.py:13
  162.4 6.3 %collective-permute-start.33 = (bf16[64,1024]{1,0:T(8,128)(2,1)S(1)}, bf16[64,1024]{1,0:T(8,128)(2,1)S(1)}, u32[]{:S(2)}, u32[]{:S(2)}) collective-permute-start(bf16[64,1024]{1,0:T(8,128)(2,1)S(1)} %bitcast_select_fusion.1), channel_id=1, source_target_pairs={{0,64},{64,128},{128,192},{192,0},{1,65},{65,129},{129,193},{193,1... | collective-permute-start | bytes 393224 | tf_op jit(solution)/shard_map/ppermute | solution.py:13
  163.2 7.5 %collective-permute-start.34 = (bf16[64,1024]{1,0:T(8,128)(2,1)S(1)}, bf16[64,1024]{1,0:T(8,128)(2,1)S(1)}, u32[]{:S(2)}, u32[]{:S(2)}) collective-permute-start(bf16[64,1024]{1,0:T(8,128)(2,1)S(1)} %bitcast_select_fusion.1), channel_id=1, source_target_pairs={{0,128},{64,192},{128,0},{192,64},{1,129},{65,193},{129,1},{193,65... | collective-permute-start | bytes 393224 | tf_op jit(solution)/shard_map/ppermute | solution.py:13
  (21 other events, 118.5 us)

commit v2 on v0

v2 whole, which is shorter than its diff:
```python
import functools

import jax
import jax.numpy as jnp
from jax import lax
from jax.experimental import pallas as pl
from jax.experimental.pallas import tpu as pltpu
from jax.sharding import Mesh
from jax.sharding import PartitionSpec as P

sharpness_coefficient = 100.0
AXES = ("y", "zl", "x", "zh", "core")
MIB = 1024 * 1024
VMEM = pl.BlockSpec(memory_space=pltpu.VMEM)
HBM = pl.BlockSpec(memory_space=pltpu.HBM)

def swapped(value, axis, mask=1):
    return lax.ppermute(value, axis, [(i, i ^ mask) for i in range(lax.axis_size(axis))])


def from_others(value, axis):
    return [swapped(value, axis, k) for k in range(1, lax.axis_size(axis))]


def kernel_call(body, name, flops, in_specs, out_specs, out_shape, vmem=12, **more):
    return pl.pallas_call(
        body,
        in_specs=in_specs,
        out_specs=out_specs,
        out_shape=out_shape,
        compiler_params=pltpu.CompilerParams(vmem_limit_bytes=vmem * MIB),
        cost_estimate=pl.CostEstimate(flops=flops, bytes_accessed=1024, transcendentals=0),
        name=name,
        **more,
    )


def f32(value):
    return value.astype(jnp.float32)


def bf16(value):
    return value.astype(jnp.bfloat16)


def shape(dims, dtype=jnp.bfloat16):
    return jax.ShapeDtypeStruct(dims, dtype)


def times_rows(left, right):
    return lax.dot_general(left, right, (((1,), (1,)), ((), ())), preferred_element_type=jnp.float32)


def merge(parts):
    peak = functools.reduce(jnp.maximum, [part[0:1] for part in parts])
    return peak, sum(part[1:2] * jnp.exp(part[0:1] - peak) for part in parts)


def normalize(values):
    return bf16(values * lax.rsqrt(jnp.mean(values * values, axis=-1, keepdims=True) + 1e-05))


def merge_kernel(count, *refs):
    peak, total = merge([ref[...] for ref in refs[:count]])
    refs[-1][0:1, :] = peak
    refs[-1][1:2, :] = total


def merge_stats(parts):
    return kernel_call(
        functools.partial(merge_kernel, len(parts)),
        "merge_stats",
        1_000_000,
        [VMEM] * len(parts),
        VMEM,
        shape(parts[0].shape, jnp.float32),
    )(*parts)


def powers_kernel(scale, step, center_ref, point_ref, power_ref, stat_ref):
    for start in range(0, point_ref.shape[0], step):
        columns = slice(start, start + step)
        raw = times_rows(center_ref[...], point_ref[columns, :])
        peak = jnp.max(raw, axis=0, keepdims=True)
        powers = jnp.exp((raw - peak) * scale)
        stat_ref[0:1, columns] = peak * scale
        stat_ref[1:2, columns] = jnp.sum(powers, axis=0, keepdims=True)
        power_ref[:, columns] = bf16(powers)


def level_one_powers(center, points, scale):
    held, depth = center.shape
    count = points.shape[0]
    return kernel_call(
        functools.partial(powers_kernel, scale, 512),
        "level_one_powers",
        2 * held * count * depth,
        [VMEM] * 2,
        [VMEM] * 2,
        [shape((held, count)), shape((2, count), jnp.float32)],
        vmem=20,
    )(center, points)


def sums_kernel(near, other_core, local_ref, *refs):
    stat_refs, power_ref, point_ref, out_ref = refs[:near], refs[near], refs[near + 1], refs[-1]
    nx, nh, _, owned, count = power_ref.shape
    peak, total = merge([ref[...] for ref in stat_refs])
    factor = jnp.exp(local_ref[0:1, :] - peak) / total
    core = lax.axis_index("core") ^ int(other_core)
    for k in range(nx):
        powers = power_ref[lax.axis_index("x") ^ k, :, core].reshape(nh * owned, count)
        weight = bf16(f32(powers) * factor)
        sums = jnp.dot(weight, point_ref[...], preferred_element_type=jnp.float32)
        out_ref[k] = sums.astype(out_ref.dtype).reshape(nh, owned, -1)


def level_one_sums(other_core, local, stats, powers, points, dtype):
    nx, nh, _, owned, count = powers.shape
    depth = points.shape[1]
    return kernel_call(
        functools.partial(sums_kernel, len(stats), other_core),
        "level_one_sums",
        2 * nx * nh * owned * count * depth,
        [VMEM] * (3 + len(stats)),
        VMEM,
        shape((nx, nh, owned, depth), dtype),
    )(local, *stats, powers, points)


def split_kernel(parts, kept_ref, got_ref, *refs):
    size = kept_ref.shape[0]
    for part in range(parts):
        hold_ref, *send_refs = refs[part * size : (part + 1) * size]
        hold_ref[...] = kept_ref[0, part] + f32(got_ref[0, part])
        for k, send_ref in enumerate(send_refs, 1):
            send_ref[...] = bf16(kept_ref[k, part] + f32(got_ref[k, part]))


def total_kernel(hold_ref, *refs):
    refs[-1][...] = bf16(hold_ref[...] + sum(f32(ref[...]) for ref in refs[:-1]))


def axis_sums(kept, got, axis):
    size, parts, *block = kept.shape
    outs = kernel_call(
        functools.partial(split_kernel, parts),
        "split",
        1_000_000,
        [VMEM] * 2,
        [VMEM] * (size * parts),
        ([shape(block, jnp.float32)] + [shape(block)] * (size - 1)) * parts,
    )(kept, got)
    sums = []
    for part in range(parts):
        hold, *sends = outs[part * size : (part + 1) * size]
        arrived = [swapped(send, axis, k) for k, send in enumerate(sends, 1)]
        sums.append(
            kernel_call(total_kernel, "total", 1_000_000, [VMEM] * size, VMEM, shape(block))(hold, *arrived)
        )
    return sums


def rows_kernel(half, part_ref, other_ref, center_hbm, row_ref, center_ref, sem):
    mine = center_hbm.at[lax.axis_index("x"), half, lax.axis_index("core")]
    copy = pltpu.make_async_copy(mine, center_ref, sem)
    copy.start()
    copy.wait()
    row_ref[...] = normalize(f32(part_ref[...]) + f32(other_ref[...]) + f32(center_ref[...]))


def new_rows(half, part, other, centers):
    return kernel_call(
        functools.partial(rows_kernel, half),
        "new_rows",
        1_000_000,
        [VMEM] * 2 + [HBM],
        VMEM,
        shape(part.shape),
        scratch_shapes=[pltpu.VMEM(part.shape, jnp.bfloat16), pltpu.SemaphoreType.DMA],
    )(part, other, centers)


def own_kernel(a_ref, b_ref, out_ref):
    out_ref[...] = jnp.where(lax.axis_index("zh") == 0, a_ref[...], b_ref[...])


def own_rows(a, b):
    return kernel_call(own_kernel, "own_rows", 1_000_000, [VMEM] * 2, VMEM, shape(a.shape))(a, b)


def powers_two_kernel(scale, ny, own_ref, other_ref, *refs):
    piece_refs, (row_ref, power_ref, stat_ref, center_ref) = refs[:-4], refs[-4:]
    held = own_ref.shape[0]
    block = held // ny
    for core, ref in enumerate((own_ref, other_ref)):
        for k in range(ny):
            place = pl.ds(pl.multiple_of((lax.axis_index("y") ^ k) * block, block), block)
            center_ref[core * held + k * block : core * held + (k + 1) * block, :] = ref[place, :]
    around = lax.axis_size("x")
    for i, ref in enumerate(piece_refs):
        size = ref.shape[0]
        first = (lax.axis_index("x") ^ (i % around)) * size + (i // around) * around * size
        row_ref[pl.ds(pl.multiple_of(first, size), size), :] = ref[...]
    raw = times_rows(center_ref[...], row_ref[...])
    peak = jnp.max(raw, axis=0, keepdims=True)
    powers = jnp.exp((raw - peak) * scale)
    stat_ref[0:1, :] = peak * scale
    stat_ref[1:2, :] = jnp.sum(powers, axis=0, keepdims=True)
    power_ref[...] = bf16(powers)


def level_two_powers(own, other, pieces, ny, scale):
    held, depth = own.shape
    count = sum(p.shape[0] for p in pieces)
    return kernel_call(
        functools.partial(powers_two_kernel, scale, ny),
        "level_two_powers",
        4 * held * count * depth,
        [VMEM] * (2 + len(pieces)),
        [VMEM] * 3,
        [shape((count, depth)), shape((2 * held, count)), shape((2, count), jnp.float32)],
        scratch_shapes=[pltpu.VMEM((2 * held, depth), jnp.bfloat16)],
    )(own, other, *pieces)


def sums_two_kernel(first, local_ref, power_ref, row_ref, *refs):
    stat_refs, out_ref = refs[:-1], refs[-1]
    peak, total = merge([ref[...] for ref in stat_refs])
    factor = jnp.exp(local_ref[0:1, :] - peak) / total
    held = power_ref.shape[0] // 2
    weight = bf16(f32(power_ref[first : first + held, :]) * factor)
    sums = jnp.dot(weight, row_ref[...], preferred_element_type=jnp.float32)
    out_ref[...] = sums.astype(out_ref.dtype).reshape(out_ref.shape)


def level_two_sums(other_core, local, stats, powers, rows, ny, dtype):
    held = powers.shape[0] // 2
    count, depth = rows.shape
    return kernel_call(
        functools.partial(sums_two_kernel, held if other_core else 0),
        "level_two_sums",
        2 * held * count * depth,
        [VMEM] * (3 + len(stats)),
        VMEM,
        shape((ny, 1, held // ny, depth), dtype),
    )(local, powers, rows, *stats)


def finish_kernel(center_ref, a_ref, b_ref, c_ref, d_ref, out_ref):
    size = a_ref.shape[0]
    values = (f32(a_ref[...]) + f32(b_ref[...])) + (f32(c_ref[...]) + f32(d_ref[...]))
    start = pl.multiple_of(lax.axis_index("y") * size, size)
    out_ref[...] = normalize(values + f32(center_ref[pl.ds(start, size), :]))


def finish(center, parts):
    return kernel_call(
        finish_kernel, "finish", 1_000_000, [VMEM] * 5, VMEM, shape(parts[0].shape)
    )(center, *parts)


def place_kernel(*refs):
    block_refs, out_ref, sems = refs[:-2], refs[-2], refs[-1]
    size = block_refs[0].shape[0]
    copies = []
    for k, ref in enumerate(block_refs):
        rows = pl.ds(pl.multiple_of((lax.axis_index("y") ^ k) * size, size), size)
        copies.append(pltpu.make_async_copy(ref, out_ref.at[rows, :], sems.at[k]))
    for copy in copies:
        copy.start()
    for copy in copies:
        copy.wait()


def place(blocks, like):
    return kernel_call(
        place_kernel,
        "place",
        1_000_000,
        [VMEM] * len(blocks),
        HBM,
        shape(like.shape),
        scratch_shapes=[pltpu.SemaphoreType.DMA((len(blocks),))],
    )(*blocks)


def shards(points, center_one, center_two):
    held, depth = center_one.shape
    scale = sharpness_coefficient / depth
    ny, nl, nx, nh, nc = (lax.axis_size(a) for a in AXES)
    owned = held // (nx * nh * nc)

    powers, local = level_one_powers(center_one, points, scale)
    near = merge_stats([local] + from_others(local, "y"))
    powers = powers.reshape(nx, nh, nc, owned, -1)
    stats = [near] + from_others(near, "zl")
    sent = level_one_sums(True, local, stats, powers, points, jnp.bfloat16)
    got = swapped(sent, "core")
    kept = level_one_sums(False, local, stats, powers, points, jnp.float32)

    centers = center_one.reshape(nx, nh, nc, owned, depth)
    rows = []
    for half, part in enumerate(axis_sums(kept, got, "x")):
        rows.append(new_rows(half, part, swapped(part, "zh"), centers))
    level_one = own_rows(*rows)

    two_core = swapped(center_two, "core")
    pieces = [piece for half in rows for piece in [half] + from_others(half, "x")]
    rows, powers, local = level_two_powers(center_two, two_core, pieces, ny, scale)
    near = merge_stats([local] + from_others(local, "x"))
    stats = [near, swapped(near, "zh")]
    sent = level_two_sums(True, local, stats, powers, rows, ny, jnp.bfloat16)
    got = swapped(sent, "core")
    kept = level_two_sums(False, local, stats, powers, rows, ny, jnp.float32)

    (part,) = axis_sums(kept, got, "y")
    done = finish(center_two, [part] + from_others(part, "zl"))
    return level_one, place([done] + from_others(done, "y"), center_two)


def solution(mesh):
    fine = Mesh(mesh.devices.reshape(4, 4, 4, 2, 2), AXES)
    cent, pts = ("y", "zl"), ("x", "zh", "core")
    in_specs = (P(pts, None), P(cent, None), P(pts, None))
    out_specs = (P(cent + pts, None), P(pts, None))
    return jax.shard_map(shards, mesh=fine, in_specs=in_specs, out_specs=out_specs, check_vma=False)
```

time: 618 us -> 134 us (0.22)
  waiting for transfers between devices: 389 us -> 50.3 us
  blocking collectives: 175 us -> 0 us
  starting transfers between devices: 0.08 us -> 62.8 us
  matrix products: 24.2 us -> 0 us
  Pallas kernels: 0 us -> 16.2 us
  between operations: 14.1 us -> 1.02 us
  other arithmetic: 12.6 us -> 0 us
    psum x2 -> x0, waiting for transfers between devices: 389 us -> none  [the longest x1 225 us: shards(): summed = lax.psum(flipped_scaled_matrix(weight_one, points), 'pts')]
    pmax x2 -> x0, blocking collectives: 88 us -> none  [the longest x1 47.5 us: shards(): second_level_peak = lax.pmax(local_two, 'pts')]
    psum x2 -> x0, blocking collectives: 86.9 us -> none  [the longest x1 44.1 us: shards(): lax.psum(jnp.sum(powers * jnp.exp(local_peak - row_peak)[:, None], axis=1...]
    ppermute x0 -> x36, starting transfers between devices: none -> 62.8 us  [swapped(): lax.ppermute(value, axis, [(i, i ^ mask) for i in range(lax.axis_size(axi...]
    ppermute x0 -> x36, waiting for transfers between devices: none -> 50.3 us  [swapped(): lax.ppermute(value, axis, [(i, i ^ mask) for i in range(lax.axis_size(axi...]
    dot_general x4 -> x0, matrix products: 24.2 us -> none  [the longest x2 12.8 us: flipped_scaled_matrix(): lax.dot_general(weights, queries, (((0,), (0,)), ((), ())), preferred_ele...]
    pallas_call x0 -> x18, Pallas kernels: none -> 16.2 us  [the longest x1 6.8 us: level_one_powers(): kernel_call(functools.partial(powers_kernel, scale, 512), 'level_one_powe...]
    reduce_sum x4 -> x0, other arithmetic: 9.77 us -> none  [the longest x1 5.05 us: shards(): jnp.sum(powers * jnp.exp(local_peak - row_peak)[:, None], axis=1)]
  transfers between devices with their start and end apart: 2 -> 36, of which waited for: 2 -> 27; matrix products, arithmetic and copies ran while one was open for 0% -> 0% of each run, Pallas kernels for 0% -> 3%
where the time goes in v2:
time: 134 us
  starting transfers between devices  62.8 us (47%)
  waiting for transfers between devices  50.3 us (38%)
  Pallas kernels  16.2 us (12%)
  local copies, waits for them, and re-layouts  3.79 us (3%)
    ppermute x36, starting transfers between devices, swapped(): lax.ppermute(value, axis, [(i, i ^ mask) for i in range(lax.axis_size(axi...  62.8 us
    ppermute x36, waiting for transfers between devices, swapped(): lax.ppermute(value, axis, [(i, i ^ mask) for i in range(lax.axis_size(axi...  50.3 us
    pallas_call x1, Pallas kernels, level_one_powers(): kernel_call(functools.partial(powers_kernel, scale, 512), 'level_one_powe...  6.8 us
    pallas_call x2, Pallas kernels, level_one_sums(): kernel_call(functools.partial(sums_kernel, len(stats), other_core), 'leve...  4.7 us
    unnamed x10, local copies, waits for them, and re-layouts  3.79 us
  transfers between devices with their start and end apart: 36, of which 27 were waited for; matrix products, arithmetic and copies ran while one was open for 0% of the time, Pallas kernels for 3%

profile of v2, /device:TPU:32, one launch (start us, length us, event | category | flops | bytes accessed | tf_op | source)
XLA Modules:
  0.0 134.1 jit_solution(12315457166667443735)
XLA Ops:
  4.4 6.8 %level_one_powers.1 = (bf16[1024,2048]{1,0:T(8,128)(2,1)S(1)}, f32[2,2048]{1,0:T(2,128)S(1)}) custom-call(bf16[1024,1024]{1,0:T(8,128)(2,1)S(1)} %copy-done.2, bf16[2048,1024]{1,0:T(8,128)(2,1)S(1)} %copy-done), custom_call_target="tpu_custom_call" | custom-call | flops 4294967296 | bytes 1024 | tf_op jit(solution)/shard_map/level_one_powers/pallas_call | solution.py:94
  12.9 2.9 %collective-permute-start.1 = (f32[2,2048]{1,0:T(2,128)S(1)}, f32[2,2048]{1,0:T(2,128)S(1)}, u32[]{:S(2)}, u32[]{:S(2)}) collective-permute-start(f32[2,2048]{1,0:T(2,128)S(1)} %get-tuple-element.19.refs_0_.local_ref), channel_id=1, source_target_pairs={{0,128},{64,192},{128,0},{192,64},{1,129},{65,193},{129,1},{193,65... | collective-permute-start | bytes 49160 | tf_op jit(solution)/shard_map/ppermute | solution.py:18
  18.1 2.6 %collective-permute-done.2.refs_3_ = f32[2,2048]{1,0:T(2,128)S(1)} collective-permute-done((f32[2,2048]{1,0:T(2,128)S(1)}, f32[2,2048]{1,0:T(2,128)S(1)}, u32[]{:S(2)}, u32[]{:S(2)}) %collective-permute-start.2) | collective-permute-done | bytes 16416 | tf_op jit(solution)/shard_map/ppermute | solution.py:18
  21.0 3.3 %collective-permute-start.4 = (f32[2,2048]{1,0:T(2,128)S(1)}, f32[2,2048]{1,0:T(2,128)S(1)}, u32[]{:S(2)}, u32[]{:S(2)}) collective-permute-start(f32[2,2048]{1,0:T(2,128)S(1)} %merge_stats.2.refs_0_), channel_id=1, source_target_pairs={{0,32},{16,48},{32,0},{48,16},{1,33},{17,49},{33,1},{49,17},{2,34}... | collective-permute-start | bytes 49160 | tf_op jit(solution)/shard_map/ppermute | solution.py:18
  28.0 2.4 %level_one_sums.3 = bf16[4,2,64,1024]{3,2,1,0:T(8,128)(2,1)S(1)} custom-call(f32[2,2048]{1,0:T(2,128)S(1)} %get-tuple-element.19.refs_0_.local_ref, f32[2,2048]{1,0:T(2,128)S(1)} %merge_stats.2.refs_0_, f32[2,2048]{1,0:T(2,128)S(1)} %collective-permute-done.3.refs_1_, f32[2,2048]{1,0:T(2,128)S(1)} %collective-permute-done.4.refs_2_, ...), custom_call_target="tpu_custom_call" | custom-call | flops 2147483648 | bytes 1024 | tf_op jit(solution)/shard_map/level_one_sums/pallas_call | solution.py:121
  30.9 2.3 %level_one_sums.2.kept_ref = f32[4,2,64,1024]{3,2,1,0:T(8,128)S(1)} custom-call(f32[2,2048]{1,0:T(2,128)S(1)} %get-tuple-element.19.refs_0_.local_ref, f32[2,2048]{1,0:T(2,128)S(1)} %merge_stats.2.refs_0_, f32[2,2048]{1,0:T(2,128)S(1)} %collective-permute-done.3.refs_1_, f32[2,2048]{1,0:T(2,128)S(1)} %collective-permute-done.4.refs_2_, ...), custom_call_target="tpu_custom_call" | custom-call | flops 2147483648 | bytes 1024 | tf_op jit(solution)/shard_map/level_one_sums/pallas_call | solution.py:121
  35.1 2.7 %collective-permute-start.12 = (bf16[64,1024]{1,0:T(8,128)(2,1)S(1)}, bf16[64,1024]{1,0:T(8,128)(2,1)S(1)}, u32[]{:S(2)}, u32[]{:S(2)}) collective-permute-start(bf16[64,1024]{1,0:T(8,128)(2,1)S(1)} %get-tuple-element.27), channel_id=1, source_target_pairs={{0,8},{4,12},{8,0},{12,4},{1,9},{5,13},{9,1},{13,5},{2,10},{6,14},... | collective-permute-start | bytes 393224 | tf_op jit(solution)/shard_map/ppermute | solution.py:18
  39.9 3.0 %collective-permute-start.8 = (bf16[64,1024]{1,0:T(8,128)(2,1)S(1)}, bf16[64,1024]{1,0:T(8,128)(2,1)S(1)}, u32[]{:S(2)}, u32[]{:S(2)}) collective-permute-start(bf16[64,1024]{1,0:T(8,128)(2,1)S(1)} %get-tuple-element.23), channel_id=1, source_target_pairs={{0,8},{4,12},{8,0},{12,4},{1,9},{5,13},{9,1},{13,5},{2,10},{6,14},... | collective-permute-start | bytes 393224 | tf_op jit(solution)/shard_map/ppermute | solution.py:18
  47.0 5.5 %collective-permute-start.14 = (bf16[64,1024]{1,0:T(8,128)(2,1)S(1)}, bf16[64,1024]{1,0:T(8,128)(2,1)S(1)}, u32[]{:S(2)}, u32[]{:S(2)}) collective-permute-start(bf16[64,1024]{1,0:T(8,128)(2,1)S(1)} %total.4.part_ref), channel_id=1, source_target_pairs={{0,2},{2,0},{1,3},{3,1},{4,6},{6,4},{5,7},{7,5},{8,10},{10,8},{9,1... | collective-permute-start | bytes 393224 | tf_op jit(solution)/shard_map/ppermute | solution.py:18
  52.7 5.5 %collective-permute-start.10 = (bf16[64,1024]{1,0:T(8,128)(2,1)S(1)}, bf16[64,1024]{1,0:T(8,128)(2,1)S(1)}, u32[]{:S(2)}, u32[]{:S(2)}) collective-permute-start(bf16[64,1024]{1,0:T(8,128)(2,1)S(1)} %total.3.part_ref), channel_id=1, source_target_pairs={{0,2},{2,0},{1,3},{3,1},{4,6},{6,4},{5,7},{7,5},{8,10},{10,8},{9,1... | collective-permute-start | bytes 393224 | tf_op jit(solution)/shard_map/ppermute | solution.py:18
  60.9 2.8 %collective-permute-start.21 = (bf16[64,1024]{1,0:T(8,128)(2,1)S(1)}, bf16[64,1024]{1,0:T(8,128)(2,1)S(1)}, u32[]{:S(2)}, u32[]{:S(2)}) collective-permute-start(bf16[64,1024]{1,0:T(8,128)(2,1)S(1)} %new_rows.3.b_ref.refs_4_), channel_id=1, source_target_pairs={{0,12},{4,8},{8,4},{12,0},{1,13},{5,9},{9,5},{13,1},{2,14},{6,10},... | collective-permute-start | bytes 393224 | tf_op jit(solution)/shard_map/ppermute | solution.py:18
  65.2 2.5 %collective-permute-start.17 = (bf16[64,1024]{1,0:T(8,128)(2,1)S(1)}, bf16[64,1024]{1,0:T(8,128)(2,1)S(1)}, u32[]{:S(2)}, u32[]{:S(2)}) collective-permute-start(bf16[64,1024]{1,0:T(8,128)(2,1)S(1)} %new_rows.2.a_ref.refs_0_), channel_id=1, source_target_pairs={{0,8},{4,12},{8,0},{12,4},{1,9},{5,13},{9,1},{13,5},{2,10},{6,14},... | collective-permute-start | bytes 393224 | tf_op jit(solution)/shard_map/ppermute | solution.py:18
  75.4 3.9 %collective-permute-start.23 = (f32[2,512]{1,0:T(2,128)S(1)}, f32[2,512]{1,0:T(2,128)S(1)}, u32[]{:S(2)}, u32[]{:S(2)}) collective-permute-start(f32[2,512]{1,0:T(2,128)S(1)} %get-tuple-element.29.refs_0_.local_ref), channel_id=1, source_target_pairs={{0,8},{4,12},{8,0},{12,4},{1,9},{5,13},{9,1},{13,5},{2,10},{6,14},... | collective-permute-start | bytes 12296 | tf_op jit(solution)/shard_map/ppermute | solution.py:18
  81.0 3.2 %collective-permute-done.24.refs_3_ = f32[2,512]{1,0:T(2,128)S(1)} collective-permute-done((f32[2,512]{1,0:T(2,128)S(1)}, f32[2,512]{1,0:T(2,128)S(1)}, u32[]{:S(2)}, u32[]{:S(2)}) %collective-permute-start.24) | collective-permute-done | bytes 4128 | tf_op jit(solution)/shard_map/ppermute | solution.py:18
  84.2 4.3 %collective-permute-start.25 = (f32[2,512]{1,0:T(2,128)S(1)}, f32[2,512]{1,0:T(2,128)S(1)}, u32[]{:S(2)}, u32[]{:S(2)}) collective-permute-start(f32[2,512]{1,0:T(2,128)S(1)} %merge_stats.3.refs_0_), channel_id=1, source_target_pairs={{0,2},{2,0},{1,3},{3,1},{4,6},{6,4},{5,7},{7,5},{8,10},{10,8},{9,1... | collective-permute-start | bytes 12296 | tf_op jit(solution)/shard_map/ppermute | solution.py:18
  88.5 3.3 %collective-permute-done.25.refs_1_ = f32[2,512]{1,0:T(2,128)S(1)} collective-permute-done((f32[2,512]{1,0:T(2,128)S(1)}, f32[2,512]{1,0:T(2,128)S(1)}, u32[]{:S(2)}, u32[]{:S(2)}) %collective-permute-start.25) | collective-permute-done | bytes 4128 | tf_op jit(solution)/shard_map/ppermute | solution.py:18
  96.0 3.1 %collective-permute-start.29 = (bf16[64,1024]{1,0:T(8,128)(2,1)S(1)}, bf16[64,1024]{1,0:T(8,128)(2,1)S(1)}, u32[]{:S(2)}, u32[]{:S(2)}) collective-permute-start(bf16[64,1024]{1,0:T(8,128)(2,1)S(1)} %get-tuple-element.35), channel_id=1, source_target_pairs={{0,192},{64,128},{128,64},{192,0},{1,193},{65,129},{129,65},{193,1... | collective-permute-start | bytes 393224 | tf_op jit(solution)/shard_map/ppermute | solution.py:18
  102.5 2.3 %collective-permute-done.29.refs_2_ = bf16[64,1024]{1,0:T(8,128)(2,1)S(1)} collective-permute-done((bf16[64,1024]{1,0:T(8,128)(2,1)S(1)}, bf16[64,1024]{1,0:T(8,128)(2,1)S(1)}, u32[]{:S(2)}, u32[]{:S(2)}) %collective-permute-start.29) | collective-permute-done | bytes 131104 | tf_op jit(solution)/shard_map/ppermute | solution.py:18
  104.8 4.1 %collective-permute-start.30 = (bf16[64,1024]{1,0:T(8,128)(2,1)S(1)}, bf16[64,1024]{1,0:T(8,128)(2,1)S(1)}, u32[]{:S(2)}, u32[]{:S(2)}) collective-permute-start(bf16[64,1024]{1,0:T(8,128)(2,1)S(1)} %total.5.a_ref), channel_id=1, source_target_pairs={{0,16},{16,0},{32,48},{48,32},{1,17},{17,1},{33,49},{49,33},{2,18}... | collective-permute-start | bytes 393224 | tf_op jit(solution)/shard_map/ppermute | solution.py:18
  110.5 2.8 %collective-permute-done.30.b_ref = bf16[64,1024]{1,0:T(8,128)(2,1)S(1)} collective-permute-done((bf16[64,1024]{1,0:T(8,128)(2,1)S(1)}, bf16[64,1024]{1,0:T(8,128)(2,1)S(1)}, u32[]{:S(2)}, u32[]{:S(2)}) %collective-permute-start.30) | collective-permute-done | bytes 131104 | tf_op jit(solution)/shard_map/ppermute | solution.py:18
  113.3 5.1 %collective-permute-done.31.c_ref = bf16[64,1024]{1,0:T(8,128)(2,1)S(1)} collective-permute-done((bf16[64,1024]{1,0:T(8,128)(2,1)S(1)}, bf16[64,1024]{1,0:T(8,128)(2,1)S(1)}, u32[]{:S(2)}, u32[]{:S(2)}) %collective-permute-start.31) | collective-permute-done | bytes 131104 | tf_op jit(solution)/shard_map/ppermute | solution.py:18
  118.4 3.4 %collective-permute-done.32.d_ref = bf16[64,1024]{1,0:T(8,128)(2,1)S(1)} collective-permute-done((bf16[64,1024]{1,0:T(8,128)(2,1)S(1)}, bf16[64,1024]{1,0:T(8,128)(2,1)S(1)}, u32[]{:S(2)}, u32[]{:S(2)}) %collective-permute-start.32) | collective-permute-done | bytes 131104 | tf_op jit(solution)/shard_map/ppermute | solution.py:18
  122.1 4.3 %collective-permute-start.34 = (bf16[64,1024]{1,0:T(8,128)(2,1)S(1)}, bf16[64,1024]{1,0:T(8,128)(2,1)S(1)}, u32[]{:S(2)}, u32[]{:S(2)}) collective-permute-start(bf16[64,1024]{1,0:T(8,128)(2,1)S(1)} %finish.1.refs_0_), channel_id=1, source_target_pairs={{0,128},{64,192},{128,0},{192,64},{1,129},{65,193},{129,1},{193,65... | collective-permute-start | bytes 393224 | tf_op jit(solution)/shard_map/ppermute | solution.py:18
  128.1 3.4 %collective-permute-done.34.refs_2_ = bf16[64,1024]{1,0:T(8,128)(2,1)S(1)} collective-permute-done((bf16[64,1024]{1,0:T(8,128)(2,1)S(1)}, bf16[64,1024]{1,0:T(8,128)(2,1)S(1)}, u32[]{:S(2)}, u32[]{:S(2)}) %collective-permute-start.34) | collective-permute-done | bytes 131104 | tf_op jit(solution)/shard_map/ppermute | solution.py:18
  (76 shorter events, 47.7 us)
Async XLA Ops:
  30.4 34.7 %collective-permute-start.15 = (bf16[256,1024]{1,0:T(8,128)(2,1)S(1)}, bf16[256,1024]{1,0:T(8,128)(2,1)S(1)}, u32[]{:S(2)}, u32[]{:S(2)}) collective-permute-start(bf16[256,1024]{1,0:T(8,128)(2,1)S(1)} %copy-done.4), channel_id=1, source_target_pairs={{0,1},{1,0},{2,3},{3,2},{4,5},{5,4},{6,7},{7,6},{8,9},{9,8},{10,11... | collective-permute-start | bytes 1572872 | tf_op jit(solution)/shard_map/ppermute | solution.py:18
  33.5 6.4 %collective-permute-start.11 = (bf16[64,1024]{1,0:T(8,128)(2,1)S(1)}, bf16[64,1024]{1,0:T(8,128)(2,1)S(1)}, u32[]{:S(2)}, u32[]{:S(2)}) collective-permute-start(bf16[64,1024]{1,0:T(8,128)(2,1)S(1)} %get-tuple-element.26), channel_id=1, source_target_pairs={{0,4},{4,0},{8,12},{12,8},{1,5},{5,1},{9,13},{13,9},{2,6},{6,2},{1... | collective-permute-start | bytes 393224 | tf_op jit(solution)/shard_map/ppermute | solution.py:18
  35.1 9.9 %collective-permute-start.12 = (bf16[64,1024]{1,0:T(8,128)(2,1)S(1)}, bf16[64,1024]{1,0:T(8,128)(2,1)S(1)}, u32[]{:S(2)}, u32[]{:S(2)}) collective-permute-start(bf16[64,1024]{1,0:T(8,128)(2,1)S(1)} %get-tuple-element.27), channel_id=1, source_target_pairs={{0,8},{4,12},{8,0},{12,4},{1,9},{5,13},{9,1},{13,5},{2,10},{6,14},... | collective-permute-start | bytes 393224 | tf_op jit(solution)/shard_map/ppermute | solution.py:18
  37.8 9.1 %collective-permute-start.13 = (bf16[64,1024]{1,0:T(8,128)(2,1)S(1)}, bf16[64,1024]{1,0:T(8,128)(2,1)S(1)}, u32[]{:S(2)}, u32[]{:S(2)}) collective-permute-start(bf16[64,1024]{1,0:T(8,128)(2,1)S(1)} %get-tuple-element.28), channel_id=1, source_target_pairs={{0,12},{4,8},{8,4},{12,0},{1,13},{5,9},{9,5},{13,1},{2,14},{6,10},... | collective-permute-start | bytes 393224 | tf_op jit(solution)/shard_map/ppermute | solution.py:18
  38.3 14.2 %collective-permute-start.7 = (bf16[64,1024]{1,0:T(8,128)(2,1)S(1)}, bf16[64,1024]{1,0:T(8,128)(2,1)S(1)}, u32[]{:S(2)}, u32[]{:S(2)}) collective-permute-start(bf16[64,1024]{1,0:T(8,128)(2,1)S(1)} %get-tuple-element.22), channel_id=1, source_target_pairs={{0,4},{4,0},{8,12},{12,8},{1,5},{5,1},{9,13},{13,9},{2,6},{6,2},{1... | collective-permute-start | bytes 393224 | tf_op jit(solution)/shard_map/ppermute | solution.py:18
  39.9 12.6 %collective-permute-start.8 = (bf16[64,1024]{1,0:T(8,128)(2,1)S(1)}, bf16[64,1024]{1,0:T(8,128)(2,1)S(1)}, u32[]{:S(2)}, u32[]{:S(2)}) collective-permute-start(bf16[64,1024]{1,0:T(8,128)(2,1)S(1)} %get-tuple-element.23), channel_id=1, source_target_pairs={{0,8},{4,12},{8,0},{12,4},{1,9},{5,13},{9,1},{13,5},{2,10},{6,14},... | collective-permute-start | bytes 393224 | tf_op jit(solution)/shard_map/ppermute | solution.py:18
  44.9 7.7 %collective-permute-start.9 = (bf16[64,1024]{1,0:T(8,128)(2,1)S(1)}, bf16[64,1024]{1,0:T(8,128)(2,1)S(1)}, u32[]{:S(2)}, u32[]{:S(2)}) collective-permute-start(bf16[64,1024]{1,0:T(8,128)(2,1)S(1)} %get-tuple-element.24), channel_id=1, source_target_pairs={{0,12},{4,8},{8,4},{12,0},{1,13},{5,9},{9,5},{13,1},{2,14},{6,10},... | collective-permute-start | bytes 393224 | tf_op jit(solution)/shard_map/ppermute | solution.py:18
  47.0 11.6 %collective-permute-start.14 = (bf16[64,1024]{1,0:T(8,128)(2,1)S(1)}, bf16[64,1024]{1,0:T(8,128)(2,1)S(1)}, u32[]{:S(2)}, u32[]{:S(2)}) collective-permute-start(bf16[64,1024]{1,0:T(8,128)(2,1)S(1)} %total.4.part_ref), channel_id=1, source_target_pairs={{0,2},{2,0},{1,3},{3,1},{4,6},{6,4},{5,7},{7,5},{8,10},{10,8},{9,1... | collective-permute-start | bytes 393224 | tf_op jit(solution)/shard_map/ppermute | solution.py:18
  52.7 12.0 %collective-permute-start.10 = (bf16[64,1024]{1,0:T(8,128)(2,1)S(1)}, bf16[64,1024]{1,0:T(8,128)(2,1)S(1)}, u32[]{:S(2)}, u32[]{:S(2)}) collective-permute-start(bf16[64,1024]{1,0:T(8,128)(2,1)S(1)} %total.3.part_ref), channel_id=1, source_target_pairs={{0,2},{2,0},{1,3},{3,1},{4,6},{6,4},{5,7},{7,5},{8,10},{10,8},{9,1... | collective-permute-start | bytes 393224 | tf_op jit(solution)/shard_map/ppermute | solution.py:18
  58.9 8.8 %collective-permute-start.19 = (bf16[64,1024]{1,0:T(8,128)(2,1)S(1)}, bf16[64,1024]{1,0:T(8,128)(2,1)S(1)}, u32[]{:S(2)}, u32[]{:S(2)}) collective-permute-start(bf16[64,1024]{1,0:T(8,128)(2,1)S(1)} %new_rows.3.b_ref.refs_4_), channel_id=1, source_target_pairs={{0,4},{4,0},{8,12},{12,8},{1,5},{5,1},{9,13},{13,9},{2,6},{6,2},{1... | collective-permute-start | bytes 393224 | tf_op jit(solution)/shard_map/ppermute | solution.py:18
  59.0 10.9 %collective-permute-start.20 = (bf16[64,1024]{1,0:T(8,128)(2,1)S(1)}, bf16[64,1024]{1,0:T(8,128)(2,1)S(1)}, u32[]{:S(2)}, u32[]{:S(2)}) collective-permute-start(bf16[64,1024]{1,0:T(8,128)(2,1)S(1)} %new_rows.3.b_ref.refs_4_), channel_id=1, source_target_pairs={{0,8},{4,12},{8,0},{12,4},{1,9},{5,13},{9,1},{13,5},{2,10},{6,14},... | collective-permute-start | bytes 393224 | tf_op jit(solution)/shard_map/ppermute | solution.py:18
  60.9 9.6 %collective-permute-start.21 = (bf16[64,1024]{1,0:T(8,128)(2,1)S(1)}, bf16[64,1024]{1,0:T(8,128)(2,1)S(1)}, u32[]{:S(2)}, u32[]{:S(2)}) collective-permute-start(bf16[64,1024]{1,0:T(8,128)(2,1)S(1)} %new_rows.3.b_ref.refs_4_), channel_id=1, source_target_pairs={{0,12},{4,8},{8,4},{12,0},{1,13},{5,9},{9,5},{13,1},{2,14},{6,10},... | collective-permute-start | bytes 393224 | tf_op jit(solution)/shard_map/ppermute | solution.py:18
  65.2 7.2 %collective-permute-start.17 = (bf16[64,1024]{1,0:T(8,128)(2,1)S(1)}, bf16[64,1024]{1,0:T(8,128)(2,1)S(1)}, u32[]{:S(2)}, u32[]{:S(2)}) collective-permute-start(bf16[64,1024]{1,0:T(8,128)(2,1)S(1)} %new_rows.2.a_ref.refs_0_), channel_id=1, source_target_pairs={{0,8},{4,12},{8,0},{12,4},{1,9},{5,13},{9,1},{13,5},{2,10},{6,14},... | collective-permute-start | bytes 393224 | tf_op jit(solution)/shard_map/ppermute | solution.py:18
  67.6 6.6 %collective-permute-start.18 = (bf16[64,1024]{1,0:T(8,128)(2,1)S(1)}, bf16[64,1024]{1,0:T(8,128)(2,1)S(1)}, u32[]{:S(2)}, u32[]{:S(2)}) collective-permute-start(bf16[64,1024]{1,0:T(8,128)(2,1)S(1)} %new_rows.2.a_ref.refs_0_), channel_id=1, source_target_pairs={{0,12},{4,8},{8,4},{12,0},{1,13},{5,9},{9,5},{13,1},{2,14},{6,10},... | collective-permute-start | bytes 393224 | tf_op jit(solution)/shard_map/ppermute | solution.py:18
  84.2 7.6 %collective-permute-start.25 = (f32[2,512]{1,0:T(2,128)S(1)}, f32[2,512]{1,0:T(2,128)S(1)}, u32[]{:S(2)}, u32[]{:S(2)}) collective-permute-start(f32[2,512]{1,0:T(2,128)S(1)} %merge_stats.3.refs_0_), channel_id=1, source_target_pairs={{0,2},{2,0},{1,3},{3,1},{4,6},{6,4},{5,7},{7,5},{8,10},{10,8},{9,1... | collective-permute-start | bytes 12296 | tf_op jit(solution)/shard_map/ppermute | solution.py:18
  94.3 6.4 %collective-permute-start.27 = (bf16[64,1024]{1,0:T(8,128)(2,1)S(1)}, bf16[64,1024]{1,0:T(8,128)(2,1)S(1)}, u32[]{:S(2)}, u32[]{:S(2)}) collective-permute-start(bf16[64,1024]{1,0:T(8,128)(2,1)S(1)} %get-tuple-element.33), channel_id=1, source_target_pairs={{0,64},{64,0},{128,192},{192,128},{1,65},{65,1},{129,193},{193,129... | collective-permute-start | bytes 393224 | tf_op jit(solution)/shard_map/ppermute | solution.py:18
  94.4 8.0 %collective-permute-start.28 = (bf16[64,1024]{1,0:T(8,128)(2,1)S(1)}, bf16[64,1024]{1,0:T(8,128)(2,1)S(1)}, u32[]{:S(2)}, u32[]{:S(2)}) collective-permute-start(bf16[64,1024]{1,0:T(8,128)(2,1)S(1)} %get-tuple-element.34), channel_id=1, source_target_pairs={{0,128},{64,192},{128,0},{192,64},{1,129},{65,193},{129,1},{193,65... | collective-permute-start | bytes 393224 | tf_op jit(solution)/shard_map/ppermute | solution.py:18
  96.0 8.7 %collective-permute-start.29 = (bf16[64,1024]{1,0:T(8,128)(2,1)S(1)}, bf16[64,1024]{1,0:T(8,128)(2,1)S(1)}, u32[]{:S(2)}, u32[]{:S(2)}) collective-permute-start(bf16[64,1024]{1,0:T(8,128)(2,1)S(1)} %get-tuple-element.35), channel_id=1, source_target_pairs={{0,192},{64,128},{128,64},{192,0},{1,193},{65,129},{129,65},{193,1... | collective-permute-start | bytes 393224 | tf_op jit(solution)/shard_map/ppermute | solution.py:18
  104.8 8.5 %collective-permute-start.30 = (bf16[64,1024]{1,0:T(8,128)(2,1)S(1)}, bf16[64,1024]{1,0:T(8,128)(2,1)S(1)}, u32[]{:S(2)}, u32[]{:S(2)}) collective-permute-start(bf16[64,1024]{1,0:T(8,128)(2,1)S(1)} %total.5.a_ref), channel_id=1, source_target_pairs={{0,16},{16,0},{32,48},{48,32},{1,17},{17,1},{33,49},{49,33},{2,18}... | collective-permute-start | bytes 393224 | tf_op jit(solution)/shard_map/ppermute | solution.py:18
  108.9 9.5 %collective-permute-start.31 = (bf16[64,1024]{1,0:T(8,128)(2,1)S(1)}, bf16[64,1024]{1,0:T(8,128)(2,1)S(1)}, u32[]{:S(2)}, u32[]{:S(2)}) collective-permute-start(bf16[64,1024]{1,0:T(8,128)(2,1)S(1)} %total.5.a_ref), channel_id=1, source_target_pairs={{0,32},{16,48},{32,0},{48,16},{1,33},{17,49},{33,1},{49,17},{2,34}... | collective-permute-start | bytes 393224 | tf_op jit(solution)/shard_map/ppermute | solution.py:18
  108.9 12.9 %collective-permute-start.32 = (bf16[64,1024]{1,0:T(8,128)(2,1)S(1)}, bf16[64,1024]{1,0:T(8,128)(2,1)S(1)}, u32[]{:S(2)}, u32[]{:S(2)}) collective-permute-start(bf16[64,1024]{1,0:T(8,128)(2,1)S(1)} %total.5.a_ref), channel_id=1, source_target_pairs={{0,48},{16,32},{32,16},{48,0},{1,49},{17,33},{33,17},{49,1},{2,50}... | collective-permute-start | bytes 393224 | tf_op jit(solution)/shard_map/ppermute | solution.py:18
  122.0 6.1 %collective-permute-start.33 = (bf16[64,1024]{1,0:T(8,128)(2,1)S(1)}, bf16[64,1024]{1,0:T(8,128)(2,1)S(1)}, u32[]{:S(2)}, u32[]{:S(2)}) collective-permute-start(bf16[64,1024]{1,0:T(8,128)(2,1)S(1)} %finish.1.refs_0_), channel_id=1, source_target_pairs={{0,64},{64,0},{128,192},{192,128},{1,65},{65,1},{129,193},{193,129... | collective-permute-start | bytes 393224 | tf_op jit(solution)/shard_map/ppermute | solution.py:18
  122.1 9.4 %collective-permute-start.34 = (bf16[64,1024]{1,0:T(8,128)(2,1)S(1)}, bf16[64,1024]{1,0:T(8,128)(2,1)S(1)}, u32[]{:S(2)}, u32[]{:S(2)}) collective-permute-start(bf16[64,1024]{1,0:T(8,128)(2,1)S(1)} %finish.1.refs_0_), channel_id=1, source_target_pairs={{0,128},{64,192},{128,0},{192,64},{1,129},{65,193},{129,1},{193,65... | collective-permute-start | bytes 393224 | tf_op jit(solution)/shard_map/ppermute | solution.py:18
  126.4 6.7 %collective-permute-start.35 = (bf16[64,1024]{1,0:T(8,128)(2,1)S(1)}, bf16[64,1024]{1,0:T(8,128)(2,1)S(1)}, u32[]{:S(2)}, u32[]{:S(2)}) collective-permute-start(bf16[64,1024]{1,0:T(8,128)(2,1)S(1)} %finish.1.refs_0_), channel_id=1, source_target_pairs={{0,192},{64,128},{128,64},{192,0},{1,193},{65,129},{129,65},{193,1... | collective-permute-start | bytes 393224 | tf_op jit(solution)/shard_map/ppermute | solution.py:18
  (17 other events, 88.1 us)

commit v3 on v2

--- a/solution.py
+++ b/solution.py
@@ -18,8 +18,11 @@
     return lax.ppermute(value, axis, [(i, i ^ mask) for i in range(lax.axis_size(axis))])
 
 
-def from_others(value, axis):
-    return [swapped(value, axis, k) for k in range(1, lax.axis_size(axis))]
+OTHERS = {"y": (2, 1, 3), "x": (2, 1, 3), "zl": (3, 2, 1)}
+
+
+def from_others(value, axis, masks=None):
+    return [swapped(value, axis, k) for k in masks or OTHERS[axis]]
 
 
 def kernel_call(body, name, flops, in_specs, out_specs, out_shape, vmem=12, **more):
@@ -154,7 +157,7 @@
     sums = []
     for part in range(parts):
         hold, *sends = outs[part * size : (part + 1) * size]
-        arrived = [swapped(send, axis, k) for k, send in enumerate(sends, 1)]
+        arrived = [swapped(sends[k - 1], axis, k) for k in OTHERS[axis]]
         sums.append(
             kernel_call(total_kernel, "total", 1_000_000, [VMEM] * size, VMEM, shape(block))(hold, *arrived)
         )
@@ -200,7 +203,8 @@
     around = lax.axis_size("x")
     for i, ref in enumerate(piece_refs):
         size = ref.shape[0]
-        first = (lax.axis_index("x") ^ (i % around)) * size + (i // around) * around * size
+        mask = (0, *OTHERS["x"])[i % around]
+        first = (lax.axis_index("x") ^ mask) * size + (i // around) * around * size
         row_ref[pl.ds(pl.multiple_of(first, size), size), :] = ref[...]
     raw = times_rows(center_ref[...], row_ref[...])
     peak = jnp.max(raw, axis=0, keepdims=True)
@@ -264,9 +268,9 @@
     block_refs, out_ref, sems = refs[:-2], refs[-2], refs[-1]
     size = block_refs[0].shape[0]
     copies = []
-    for k, ref in enumerate(block_refs):
+    for i, (k, ref) in enumerate(zip((0, *OTHERS["y"]), block_refs)):
         rows = pl.ds(pl.multiple_of((lax.axis_index("y") ^ k) * size, size), size)
-        copies.append(pltpu.make_async_copy(ref, out_ref.at[rows, :], sems.at[k]))
+        copies.append(pltpu.make_async_copy(ref, out_ref.at[rows, :], sems.at[i]))
     for copy in copies:
         copy.start()
     for copy in copies:
@@ -315,7 +319,7 @@
     kept = level_two_sums(False, local, stats, powers, rows, ny, jnp.float32)
 
     (part,) = axis_sums(kept, got, "y")
-    done = finish(center_two, [part] + from_others(part, "zl"))
+    done = finish(center_two, [part] + from_others(part, "zl", (1, 2, 3)))
     return level_one, place([done] + from_others(done, "y"), center_two)
 
 

time: 134 us -> 129 us (0.963)
  waiting for transfers between devices: 50.3 us -> 42.9 us
  starting transfers between devices: 62.8 us -> 65.2 us
    ppermute x36, waiting for transfers between devices: 50.3 us -> 42.9 us  [swapped(): lax.ppermute(value, axis, [(i, i ^ mask) for i in range(lax.axis_size(axi...]
    ppermute x36, starting transfers between devices: 62.8 us -> 65.2 us  [swapped(): lax.ppermute(value, axis, [(i, i ^ mask) for i in range(lax.axis_size(axi...]
  transfers between devices with their start and end apart: 36 -> 36, of which waited for: 27 -> 22; matrix products, arithmetic and copies ran while one was open for 0% -> 0% of each run, Pallas kernels for 3% -> 3%
where the time goes in v3:
time: 129 us
  starting transfers between devices  65.2 us (51%)
  waiting for transfers between devices  42.9 us (33%)
  Pallas kernels  16.3 us (13%)
  local copies, waits for them, and re-layouts  3.79 us (3%)
    ppermute x36, starting transfers between devices, swapped(): lax.ppermute(value, axis, [(i, i ^ mask) for i in range(lax.axis_size(axi...  65.2 us
    ppermute x36, waiting for transfers between devices, swapped(): lax.ppermute(value, axis, [(i, i ^ mask) for i in range(lax.axis_size(axi...  42.9 us
    pallas_call x1, Pallas kernels, level_one_powers(): kernel_call(functools.partial(powers_kernel, scale, 512), 'level_one_powe...  6.8 us
    pallas_call x2, Pallas kernels, level_one_sums(): kernel_call(functools.partial(sums_kernel, len(stats), other_core), 'leve...  4.7 us
    unnamed x10, local copies, waits for them, and re-layouts  3.79 us
  transfers between devices with their start and end apart: 36, of which 22 were waited for; matrix products, arithmetic and copies ran while one was open for 0% of the time, Pallas kernels for 3%

profile of v3, /device:TPU:32, one launch (start us, length us, event | category | flops | bytes accessed | tf_op | source)
XLA Modules:
  0.0 129.2 jit_solution(6432155349683168565)
XLA Ops:
  0.6 2.2 %copy-done = bf16[2048,1024]{1,0:T(8,128)(2,1)S(1)} copy-done((bf16[2048,1024]{1,0:T(8,128)(2,1)S(1)}, bf16[2048,1024]{1,0:T(8,128)(2,1)}, u32[]{:S(2)}) %copy-start) | copy-done | bytes 4194328
  4.4 6.8 %level_one_powers.1 = (bf16[1024,2048]{1,0:T(8,128)(2,1)S(1)}, f32[2,2048]{1,0:T(2,128)S(1)}) custom-call(bf16[1024,1024]{1,0:T(8,128)(2,1)S(1)} %copy-done.2, bf16[2048,1024]{1,0:T(8,128)(2,1)S(1)} %copy-done), custom_call_target="tpu_custom_call" | custom-call | flops 4294967296 | bytes 1024 | tf_op jit(solution)/shard_map/level_one_powers/pallas_call | solution.py:97
  11.2 3.3 %collective-permute-start = (f32[2,2048]{1,0:T(2,128)S(1)}, f32[2,2048]{1,0:T(2,128)S(1)}, u32[]{:S(2)}, u32[]{:S(2)}) collective-permute-start(f32[2,2048]{1,0:T(2,128)S(1)} %get-tuple-element.19.refs_0_.local_ref), channel_id=1, source_target_pairs={{0,128},{64,192},{128,0},{192,64},{1,129},{65,193},{129,1},{193,65... | collective-permute-start | bytes 49160 | tf_op jit(solution)/shard_map/ppermute | solution.py:18
  20.2 2.0 %collective-permute-start.3 = (f32[2,2048]{1,0:T(2,128)S(1)}, f32[2,2048]{1,0:T(2,128)S(1)}, u32[]{:S(2)}, u32[]{:S(2)}) collective-permute-start(f32[2,2048]{1,0:T(2,128)S(1)} %merge_stats.2.refs_0_), channel_id=1, source_target_pairs={{0,48},{16,32},{32,16},{48,0},{1,49},{17,33},{33,17},{49,1},{2,50}... | collective-permute-start | bytes 49160 | tf_op jit(solution)/shard_map/ppermute | solution.py:18
  27.3 2.4 %level_one_sums.3 = bf16[4,2,64,1024]{3,2,1,0:T(8,128)(2,1)S(1)} custom-call(f32[2,2048]{1,0:T(2,128)S(1)} %get-tuple-element.19.refs_0_.local_ref, f32[2,2048]{1,0:T(2,128)S(1)} %merge_stats.2.refs_0_, f32[2,2048]{1,0:T(2,128)S(1)} %collective-permute-done.3.refs_1_, f32[2,2048]{1,0:T(2,128)S(1)} %collective-permute-done.4.refs_2_, ...), custom_call_target="tpu_custom_call" | custom-call | flops 2147483648 | bytes 1024 | tf_op jit(solution)/shard_map/level_one_sums/pallas_call | solution.py:124
  30.3 2.3 %level_one_sums.2.kept_ref = f32[4,2,64,1024]{3,2,1,0:T(8,128)S(1)} custom-call(f32[2,2048]{1,0:T(2,128)S(1)} %get-tuple-element.19.refs_0_.local_ref, f32[2,2048]{1,0:T(2,128)S(1)} %merge_stats.2.refs_0_, f32[2,2048]{1,0:T(2,128)S(1)} %collective-permute-done.3.refs_1_, f32[2,2048]{1,0:T(2,128)S(1)} %collective-permute-done.4.refs_2_, ...), custom_call_target="tpu_custom_call" | custom-call | flops 2147483648 | bytes 1024 | tf_op jit(solution)/shard_map/level_one_sums/pallas_call | solution.py:124
  32.9 3.1 %collective-permute-start.11 = (bf16[64,1024]{1,0:T(8,128)(2,1)S(1)}, bf16[64,1024]{1,0:T(8,128)(2,1)S(1)}, u32[]{:S(2)}, u32[]{:S(2)}) collective-permute-start(bf16[64,1024]{1,0:T(8,128)(2,1)S(1)} %get-tuple-element.26), channel_id=1, source_target_pairs={{0,8},{4,12},{8,0},{12,4},{1,9},{5,13},{9,1},{13,5},{2,10},{6,14},... | collective-permute-start | bytes 393224 | tf_op jit(solution)/shard_map/ppermute | solution.py:18
  37.1 2.9 %collective-permute-start.7 = (bf16[64,1024]{1,0:T(8,128)(2,1)S(1)}, bf16[64,1024]{1,0:T(8,128)(2,1)S(1)}, u32[]{:S(2)}, u32[]{:S(2)}) collective-permute-start(bf16[64,1024]{1,0:T(8,128)(2,1)S(1)} %get-tuple-element.22), channel_id=1, source_target_pairs={{0,8},{4,12},{8,0},{12,4},{1,9},{5,13},{9,1},{13,5},{2,10},{6,14},... | collective-permute-start | bytes 393224 | tf_op jit(solution)/shard_map/ppermute | solution.py:18
  45.7 6.4 %collective-permute-start.14 = (bf16[64,1024]{1,0:T(8,128)(2,1)S(1)}, bf16[64,1024]{1,0:T(8,128)(2,1)S(1)}, u32[]{:S(2)}, u32[]{:S(2)}) collective-permute-start(bf16[64,1024]{1,0:T(8,128)(2,1)S(1)} %total.4.part_ref), channel_id=1, source_target_pairs={{0,2},{2,0},{1,3},{3,1},{4,6},{6,4},{5,7},{7,5},{8,10},{10,8},{9,1... | collective-permute-start | bytes 393224 | tf_op jit(solution)/shard_map/ppermute | solution.py:18
  52.2 4.1 %collective-permute-start.10 = (bf16[64,1024]{1,0:T(8,128)(2,1)S(1)}, bf16[64,1024]{1,0:T(8,128)(2,1)S(1)}, u32[]{:S(2)}, u32[]{:S(2)}) collective-permute-start(bf16[64,1024]{1,0:T(8,128)(2,1)S(1)} %total.3.part_ref), channel_id=1, source_target_pairs={{0,2},{2,0},{1,3},{3,1},{4,6},{6,4},{5,7},{7,5},{8,10},{10,8},{9,1... | collective-permute-start | bytes 393224 | tf_op jit(solution)/shard_map/ppermute | solution.py:18
  56.6 4.7 %collective-permute-start.19 = (bf16[64,1024]{1,0:T(8,128)(2,1)S(1)}, bf16[64,1024]{1,0:T(8,128)(2,1)S(1)}, u32[]{:S(2)}, u32[]{:S(2)}) collective-permute-start(bf16[64,1024]{1,0:T(8,128)(2,1)S(1)} %new_rows.3.b_ref.refs_4_), channel_id=1, source_target_pairs={{0,8},{4,12},{8,0},{12,4},{1,9},{5,13},{9,1},{13,5},{2,10},{6,14},... | collective-permute-start | bytes 393224 | tf_op jit(solution)/shard_map/ppermute | solution.py:18
  63.6 2.3 %collective-permute-start.16 = (bf16[64,1024]{1,0:T(8,128)(2,1)S(1)}, bf16[64,1024]{1,0:T(8,128)(2,1)S(1)}, u32[]{:S(2)}, u32[]{:S(2)}) collective-permute-start(bf16[64,1024]{1,0:T(8,128)(2,1)S(1)} %new_rows.2.a_ref.refs_0_), channel_id=1, source_target_pairs={{0,8},{4,12},{8,0},{12,4},{1,9},{5,13},{9,1},{13,5},{2,10},{6,14},... | collective-permute-start | bytes 393224 | tf_op jit(solution)/shard_map/ppermute | solution.py:18
  69.2 2.9 %collective-permute-done.21.refs_7_ = bf16[64,1024]{1,0:T(8,128)(2,1)S(1)} collective-permute-done((bf16[64,1024]{1,0:T(8,128)(2,1)S(1)}, bf16[64,1024]{1,0:T(8,128)(2,1)S(1)}, u32[]{:S(2)}, u32[]{:S(2)}) %collective-permute-start.21) | collective-permute-done | bytes 131104 | tf_op jit(solution)/shard_map/ppermute | solution.py:18
  80.3 2.5 %collective-permute-done.24.refs_3_ = f32[2,512]{1,0:T(2,128)S(1)} collective-permute-done((f32[2,512]{1,0:T(2,128)S(1)}, f32[2,512]{1,0:T(2,128)S(1)}, u32[]{:S(2)}, u32[]{:S(2)}) %collective-permute-start.24) | collective-permute-done | bytes 4128 | tf_op jit(solution)/shard_map/ppermute | solution.py:18
  82.8 7.2 %collective-permute-start.25 = (f32[2,512]{1,0:T(2,128)S(1)}, f32[2,512]{1,0:T(2,128)S(1)}, u32[]{:S(2)}, u32[]{:S(2)}) collective-permute-start(f32[2,512]{1,0:T(2,128)S(1)} %merge_stats.3.refs_0_), channel_id=1, source_target_pairs={{0,2},{2,0},{1,3},{3,1},{4,6},{6,4},{5,7},{7,5},{8,10},{10,8},{9,1... | collective-permute-start | bytes 12296 | tf_op jit(solution)/shard_map/ppermute | solution.py:18
  95.4 2.9 %collective-permute-start.29 = (bf16[64,1024]{1,0:T(8,128)(2,1)S(1)}, bf16[64,1024]{1,0:T(8,128)(2,1)S(1)}, u32[]{:S(2)}, u32[]{:S(2)}) collective-permute-start(bf16[64,1024]{1,0:T(8,128)(2,1)S(1)} %get-tuple-element.35), channel_id=1, source_target_pairs={{0,192},{64,128},{128,64},{192,0},{1,193},{65,129},{129,65},{193,1... | collective-permute-start | bytes 393224 | tf_op jit(solution)/shard_map/ppermute | solution.py:18
  98.3 3.8 %collective-permute-done.27.refs_0_ = bf16[64,1024]{1,0:T(8,128)(2,1)S(1)} collective-permute-done((bf16[64,1024]{1,0:T(8,128)(2,1)S(1)}, bf16[64,1024]{1,0:T(8,128)(2,1)S(1)}, u32[]{:S(2)}, u32[]{:S(2)}) %collective-permute-start.27) | collective-permute-done | bytes 131104 | tf_op jit(solution)/shard_map/ppermute | solution.py:18
  102.1 2.0 %collective-permute-done.29.refs_2_ = bf16[64,1024]{1,0:T(8,128)(2,1)S(1)} collective-permute-done((bf16[64,1024]{1,0:T(8,128)(2,1)S(1)}, bf16[64,1024]{1,0:T(8,128)(2,1)S(1)}, u32[]{:S(2)}, u32[]{:S(2)}) %collective-permute-start.29) | collective-permute-done | bytes 131104 | tf_op jit(solution)/shard_map/ppermute | solution.py:18
  104.2 2.5 %collective-permute-start.31 = (bf16[64,1024]{1,0:T(8,128)(2,1)S(1)}, bf16[64,1024]{1,0:T(8,128)(2,1)S(1)}, u32[]{:S(2)}, u32[]{:S(2)}) collective-permute-start(bf16[64,1024]{1,0:T(8,128)(2,1)S(1)} %total.5.a_ref), channel_id=1, source_target_pairs={{0,32},{16,48},{32,0},{48,16},{1,33},{17,49},{33,1},{49,17},{2,34}... | collective-permute-start | bytes 393224 | tf_op jit(solution)/shard_map/ppermute | solution.py:18
  107.7 2.9 %collective-permute-done.30.b_ref = bf16[64,1024]{1,0:T(8,128)(2,1)S(1)} collective-permute-done((bf16[64,1024]{1,0:T(8,128)(2,1)S(1)}, bf16[64,1024]{1,0:T(8,128)(2,1)S(1)}, u32[]{:S(2)}, u32[]{:S(2)}) %collective-permute-start.30) | collective-permute-done | bytes 131104 | tf_op jit(solution)/shard_map/ppermute | solution.py:18
  110.6 5.7 %collective-permute-done.31.c_ref = bf16[64,1024]{1,0:T(8,128)(2,1)S(1)} collective-permute-done((bf16[64,1024]{1,0:T(8,128)(2,1)S(1)}, bf16[64,1024]{1,0:T(8,128)(2,1)S(1)}, u32[]{:S(2)}, u32[]{:S(2)}) %collective-permute-start.31) | collective-permute-done | bytes 131104 | tf_op jit(solution)/shard_map/ppermute | solution.py:18
  116.2 3.1 %collective-permute-done.32.d_ref = bf16[64,1024]{1,0:T(8,128)(2,1)S(1)} collective-permute-done((bf16[64,1024]{1,0:T(8,128)(2,1)S(1)}, bf16[64,1024]{1,0:T(8,128)(2,1)S(1)}, u32[]{:S(2)}, u32[]{:S(2)}) %collective-permute-start.32) | collective-permute-done | bytes 131104 | tf_op jit(solution)/shard_map/ppermute | solution.py:18
  120.2 3.4 %collective-permute-start.35 = (bf16[64,1024]{1,0:T(8,128)(2,1)S(1)}, bf16[64,1024]{1,0:T(8,128)(2,1)S(1)}, u32[]{:S(2)}, u32[]{:S(2)}) collective-permute-start(bf16[64,1024]{1,0:T(8,128)(2,1)S(1)} %finish.1.refs_0_), channel_id=1, source_target_pairs={{0,192},{64,128},{128,64},{192,0},{1,193},{65,129},{129,65},{193,1... | collective-permute-start | bytes 393224 | tf_op jit(solution)/shard_map/ppermute | solution.py:18
  124.3 2.5 %collective-permute-done.33.refs_1_ = bf16[64,1024]{1,0:T(8,128)(2,1)S(1)} collective-permute-done((bf16[64,1024]{1,0:T(8,128)(2,1)S(1)}, bf16[64,1024]{1,0:T(8,128)(2,1)S(1)}, u32[]{:S(2)}, u32[]{:S(2)}) %collective-permute-start.33) | collective-permute-done | bytes 131104 | tf_op jit(solution)/shard_map/ppermute | solution.py:18
  (76 shorter events, 44.3 us)
Async XLA Ops:
  29.8 36.1 %collective-permute-start.15 = (bf16[256,1024]{1,0:T(8,128)(2,1)S(1)}, bf16[256,1024]{1,0:T(8,128)(2,1)S(1)}, u32[]{:S(2)}, u32[]{:S(2)}) collective-permute-start(bf16[256,1024]{1,0:T(8,128)(2,1)S(1)} %copy-done.4), channel_id=1, source_target_pairs={{0,1},{1,0},{2,3},{3,2},{4,5},{5,4},{6,7},{7,6},{8,9},{9,8},{10,11... | collective-permute-start | bytes 1572872 | tf_op jit(solution)/shard_map/ppermute | solution.py:18
  32.9 7.9 %collective-permute-start.11 = (bf16[64,1024]{1,0:T(8,128)(2,1)S(1)}, bf16[64,1024]{1,0:T(8,128)(2,1)S(1)}, u32[]{:S(2)}, u32[]{:S(2)}) collective-permute-start(bf16[64,1024]{1,0:T(8,128)(2,1)S(1)} %get-tuple-element.26), channel_id=1, source_target_pairs={{0,8},{4,12},{8,0},{12,4},{1,9},{5,13},{9,1},{13,5},{2,10},{6,14},... | collective-permute-start | bytes 393224 | tf_op jit(solution)/shard_map/ppermute | solution.py:18
  36.0 7.7 %collective-permute-start.12 = (bf16[64,1024]{1,0:T(8,128)(2,1)S(1)}, bf16[64,1024]{1,0:T(8,128)(2,1)S(1)}, u32[]{:S(2)}, u32[]{:S(2)}) collective-permute-start(bf16[64,1024]{1,0:T(8,128)(2,1)S(1)} %get-tuple-element.27), channel_id=1, source_target_pairs={{0,4},{4,0},{8,12},{12,8},{1,5},{5,1},{9,13},{13,9},{2,6},{6,2},{1... | collective-permute-start | bytes 393224 | tf_op jit(solution)/shard_map/ppermute | solution.py:18
  36.6 9.1 %collective-permute-start.13 = (bf16[64,1024]{1,0:T(8,128)(2,1)S(1)}, bf16[64,1024]{1,0:T(8,128)(2,1)S(1)}, u32[]{:S(2)}, u32[]{:S(2)}) collective-permute-start(bf16[64,1024]{1,0:T(8,128)(2,1)S(1)} %get-tuple-element.28), channel_id=1, source_target_pairs={{0,12},{4,8},{8,4},{12,0},{1,13},{5,9},{9,5},{13,1},{2,14},{6,10},... | collective-permute-start | bytes 393224 | tf_op jit(solution)/shard_map/ppermute | solution.py:18
  37.1 15.0 %collective-permute-start.7 = (bf16[64,1024]{1,0:T(8,128)(2,1)S(1)}, bf16[64,1024]{1,0:T(8,128)(2,1)S(1)}, u32[]{:S(2)}, u32[]{:S(2)}) collective-permute-start(bf16[64,1024]{1,0:T(8,128)(2,1)S(1)} %get-tuple-element.22), channel_id=1, source_target_pairs={{0,8},{4,12},{8,0},{12,4},{1,9},{5,13},{9,1},{13,5},{2,10},{6,14},... | collective-permute-start | bytes 393224 | tf_op jit(solution)/shard_map/ppermute | solution.py:18
  40.8 11.3 %collective-permute-start.8 = (bf16[64,1024]{1,0:T(8,128)(2,1)S(1)}, bf16[64,1024]{1,0:T(8,128)(2,1)S(1)}, u32[]{:S(2)}, u32[]{:S(2)}) collective-permute-start(bf16[64,1024]{1,0:T(8,128)(2,1)S(1)} %get-tuple-element.23), channel_id=1, source_target_pairs={{0,4},{4,0},{8,12},{12,8},{1,5},{5,1},{9,13},{13,9},{2,6},{6,2},{1... | collective-permute-start | bytes 393224 | tf_op jit(solution)/shard_map/ppermute | solution.py:18
  43.7 8.5 %collective-permute-start.9 = (bf16[64,1024]{1,0:T(8,128)(2,1)S(1)}, bf16[64,1024]{1,0:T(8,128)(2,1)S(1)}, u32[]{:S(2)}, u32[]{:S(2)}) collective-permute-start(bf16[64,1024]{1,0:T(8,128)(2,1)S(1)} %get-tuple-element.24), channel_id=1, source_target_pairs={{0,12},{4,8},{8,4},{12,0},{1,13},{5,9},{9,5},{13,1},{2,14},{6,10},... | collective-permute-start | bytes 393224 | tf_op jit(solution)/shard_map/ppermute | solution.py:18
  45.7 10.6 %collective-permute-start.14 = (bf16[64,1024]{1,0:T(8,128)(2,1)S(1)}, bf16[64,1024]{1,0:T(8,128)(2,1)S(1)}, u32[]{:S(2)}, u32[]{:S(2)}) collective-permute-start(bf16[64,1024]{1,0:T(8,128)(2,1)S(1)} %total.4.part_ref), channel_id=1, source_target_pairs={{0,2},{2,0},{1,3},{3,1},{4,6},{6,4},{5,7},{7,5},{8,10},{10,8},{9,1... | collective-permute-start | bytes 393224 | tf_op jit(solution)/shard_map/ppermute | solution.py:18
  52.2 11.1 %collective-permute-start.10 = (bf16[64,1024]{1,0:T(8,128)(2,1)S(1)}, bf16[64,1024]{1,0:T(8,128)(2,1)S(1)}, u32[]{:S(2)}, u32[]{:S(2)}) collective-permute-start(bf16[64,1024]{1,0:T(8,128)(2,1)S(1)} %total.3.part_ref), channel_id=1, source_target_pairs={{0,2},{2,0},{1,3},{3,1},{4,6},{6,4},{5,7},{7,5},{8,10},{10,8},{9,1... | collective-permute-start | bytes 393224 | tf_op jit(solution)/shard_map/ppermute | solution.py:18
  56.6 11.1 %collective-permute-start.19 = (bf16[64,1024]{1,0:T(8,128)(2,1)S(1)}, bf16[64,1024]{1,0:T(8,128)(2,1)S(1)}, u32[]{:S(2)}, u32[]{:S(2)}) collective-permute-start(bf16[64,1024]{1,0:T(8,128)(2,1)S(1)} %new_rows.3.b_ref.refs_4_), channel_id=1, source_target_pairs={{0,8},{4,12},{8,0},{12,4},{1,9},{5,13},{9,1},{13,5},{2,10},{6,14},... | collective-permute-start | bytes 393224 | tf_op jit(solution)/shard_map/ppermute | solution.py:18
  61.4 7.8 %collective-permute-start.20 = (bf16[64,1024]{1,0:T(8,128)(2,1)S(1)}, bf16[64,1024]{1,0:T(8,128)(2,1)S(1)}, u32[]{:S(2)}, u32[]{:S(2)}) collective-permute-start(bf16[64,1024]{1,0:T(8,128)(2,1)S(1)} %new_rows.3.b_ref.refs_4_), channel_id=1, source_target_pairs={{0,4},{4,0},{8,12},{12,8},{1,5},{5,1},{9,13},{13,9},{2,6},{6,2},{1... | collective-permute-start | bytes 393224 | tf_op jit(solution)/shard_map/ppermute | solution.py:18
  63.3 8.8 %collective-permute-start.21 = (bf16[64,1024]{1,0:T(8,128)(2,1)S(1)}, bf16[64,1024]{1,0:T(8,128)(2,1)S(1)}, u32[]{:S(2)}, u32[]{:S(2)}) collective-permute-start(bf16[64,1024]{1,0:T(8,128)(2,1)S(1)} %new_rows.3.b_ref.refs_4_), channel_id=1, source_target_pairs={{0,12},{4,8},{8,4},{12,0},{1,13},{5,9},{9,5},{13,1},{2,14},{6,10},... | collective-permute-start | bytes 393224 | tf_op jit(solution)/shard_map/ppermute | solution.py:18
  63.6 8.5 %collective-permute-start.16 = (bf16[64,1024]{1,0:T(8,128)(2,1)S(1)}, bf16[64,1024]{1,0:T(8,128)(2,1)S(1)}, u32[]{:S(2)}, u32[]{:S(2)}) collective-permute-start(bf16[64,1024]{1,0:T(8,128)(2,1)S(1)} %new_rows.2.a_ref.refs_0_), channel_id=1, source_target_pairs={{0,8},{4,12},{8,0},{12,4},{1,9},{5,13},{9,1},{13,5},{2,10},{6,14},... | collective-permute-start | bytes 393224 | tf_op jit(solution)/shard_map/ppermute | solution.py:18
  65.9 7.4 %collective-permute-start.17 = (bf16[64,1024]{1,0:T(8,128)(2,1)S(1)}, bf16[64,1024]{1,0:T(8,128)(2,1)S(1)}, u32[]{:S(2)}, u32[]{:S(2)}) collective-permute-start(bf16[64,1024]{1,0:T(8,128)(2,1)S(1)} %new_rows.2.a_ref.refs_0_), channel_id=1, source_target_pairs={{0,4},{4,0},{8,12},{12,8},{1,5},{5,1},{9,13},{13,9},{2,6},{6,2},{1... | collective-permute-start | bytes 393224 | tf_op jit(solution)/shard_map/ppermute | solution.py:18
  82.8 8.8 %collective-permute-start.25 = (f32[2,512]{1,0:T(2,128)S(1)}, f32[2,512]{1,0:T(2,128)S(1)}, u32[]{:S(2)}, u32[]{:S(2)}) collective-permute-start(f32[2,512]{1,0:T(2,128)S(1)} %merge_stats.3.refs_0_), channel_id=1, source_target_pairs={{0,2},{2,0},{1,3},{3,1},{4,6},{6,4},{5,7},{7,5},{8,10},{10,8},{9,1... | collective-permute-start | bytes 12296 | tf_op jit(solution)/shard_map/ppermute | solution.py:18
  94.1 7.9 %collective-permute-start.27 = (bf16[64,1024]{1,0:T(8,128)(2,1)S(1)}, bf16[64,1024]{1,0:T(8,128)(2,1)S(1)}, u32[]{:S(2)}, u32[]{:S(2)}) collective-permute-start(bf16[64,1024]{1,0:T(8,128)(2,1)S(1)} %get-tuple-element.33), channel_id=1, source_target_pairs={{0,128},{64,192},{128,0},{192,64},{1,129},{65,193},{129,1},{193,65... | collective-permute-start | bytes 393224 | tf_op jit(solution)/shard_map/ppermute | solution.py:18
  94.9 7.2 %collective-permute-start.28 = (bf16[64,1024]{1,0:T(8,128)(2,1)S(1)}, bf16[64,1024]{1,0:T(8,128)(2,1)S(1)}, u32[]{:S(2)}, u32[]{:S(2)}) collective-permute-start(bf16[64,1024]{1,0:T(8,128)(2,1)S(1)} %get-tuple-element.34), channel_id=1, source_target_pairs={{0,64},{64,0},{128,192},{192,128},{1,65},{65,1},{129,193},{193,129... | collective-permute-start | bytes 393224 | tf_op jit(solution)/shard_map/ppermute | solution.py:18
  95.4 8.6 %collective-permute-start.29 = (bf16[64,1024]{1,0:T(8,128)(2,1)S(1)}, bf16[64,1024]{1,0:T(8,128)(2,1)S(1)}, u32[]{:S(2)}, u32[]{:S(2)}) collective-permute-start(bf16[64,1024]{1,0:T(8,128)(2,1)S(1)} %get-tuple-element.35), channel_id=1, source_target_pairs={{0,192},{64,128},{128,64},{192,0},{1,193},{65,129},{129,65},{193,1... | collective-permute-start | bytes 393224 | tf_op jit(solution)/shard_map/ppermute | solution.py:18
  104.1 6.4 %collective-permute-start.30 = (bf16[64,1024]{1,0:T(8,128)(2,1)S(1)}, bf16[64,1024]{1,0:T(8,128)(2,1)S(1)}, u32[]{:S(2)}, u32[]{:S(2)}) collective-permute-start(bf16[64,1024]{1,0:T(8,128)(2,1)S(1)} %total.5.a_ref), channel_id=1, source_target_pairs={{0,16},{16,0},{32,48},{48,32},{1,17},{17,1},{33,49},{49,33},{2,18}... | collective-permute-start | bytes 393224 | tf_op jit(solution)/shard_map/ppermute | solution.py:18
  104.2 12.0 %collective-permute-start.31 = (bf16[64,1024]{1,0:T(8,128)(2,1)S(1)}, bf16[64,1024]{1,0:T(8,128)(2,1)S(1)}, u32[]{:S(2)}, u32[]{:S(2)}) collective-permute-start(bf16[64,1024]{1,0:T(8,128)(2,1)S(1)} %total.5.a_ref), channel_id=1, source_target_pairs={{0,32},{16,48},{32,0},{48,16},{1,33},{17,49},{33,1},{49,17},{2,34}... | collective-permute-start | bytes 393224 | tf_op jit(solution)/shard_map/ppermute | solution.py:18
  106.8 12.5 %collective-permute-start.32 = (bf16[64,1024]{1,0:T(8,128)(2,1)S(1)}, bf16[64,1024]{1,0:T(8,128)(2,1)S(1)}, u32[]{:S(2)}, u32[]{:S(2)}) collective-permute-start(bf16[64,1024]{1,0:T(8,128)(2,1)S(1)} %total.5.a_ref), channel_id=1, source_target_pairs={{0,48},{16,32},{32,16},{48,0},{1,49},{17,33},{33,17},{49,1},{2,50}... | collective-permute-start | bytes 393224 | tf_op jit(solution)/shard_map/ppermute | solution.py:18
  119.5 7.4 %collective-permute-start.33 = (bf16[64,1024]{1,0:T(8,128)(2,1)S(1)}, bf16[64,1024]{1,0:T(8,128)(2,1)S(1)}, u32[]{:S(2)}, u32[]{:S(2)}) collective-permute-start(bf16[64,1024]{1,0:T(8,128)(2,1)S(1)} %finish.1.refs_0_), channel_id=1, source_target_pairs={{0,128},{64,192},{128,0},{192,64},{1,129},{65,193},{129,1},{193,65... | collective-permute-start | bytes 393224 | tf_op jit(solution)/shard_map/ppermute | solution.py:18
  119.7 7.1 %collective-permute-start.34 = (bf16[64,1024]{1,0:T(8,128)(2,1)S(1)}, bf16[64,1024]{1,0:T(8,128)(2,1)S(1)}, u32[]{:S(2)}, u32[]{:S(2)}) collective-permute-start(bf16[64,1024]{1,0:T(8,128)(2,1)S(1)} %finish.1.refs_0_), channel_id=1, source_target_pairs={{0,64},{64,0},{128,192},{192,128},{1,65},{65,1},{129,193},{193,129... | collective-permute-start | bytes 393224 | tf_op jit(solution)/shard_map/ppermute | solution.py:18
  120.2 7.9 %collective-permute-start.35 = (bf16[64,1024]{1,0:T(8,128)(2,1)S(1)}, bf16[64,1024]{1,0:T(8,128)(2,1)S(1)}, u32[]{:S(2)}, u32[]{:S(2)}) collective-permute-start(bf16[64,1024]{1,0:T(8,128)(2,1)S(1)} %finish.1.refs_0_), channel_id=1, source_target_pairs={{0,192},{64,128},{128,64},{192,0},{1,193},{65,129},{129,65},{193,1... | collective-permute-start | bytes 393224 | tf_op jit(solution)/shard_map/ppermute | solution.py:18
  (17 other events, 85.4 us)

commit v4 on v3

--- a/solution.py
+++ b/solution.py
@@ -9,6 +9,7 @@
 from jax.sharding import PartitionSpec as P
 
 sharpness_coefficient = 100.0
+LOG2_E = 1.4426950408889634
 AXES = ("y", "zl", "x", "zh", "core")
 MIB = 1024 * 1024
 VMEM = pl.BlockSpec(memory_space=pltpu.VMEM)
@@ -85,7 +86,7 @@
         columns = slice(start, start + step)
         raw = times_rows(center_ref[...], point_ref[columns, :])
         peak = jnp.max(raw, axis=0, keepdims=True)
-        powers = jnp.exp((raw - peak) * scale)
+        powers = jnp.exp2((raw - peak) * (scale * LOG2_E))
         stat_ref[0:1, columns] = peak * scale
         stat_ref[1:2, columns] = jnp.sum(powers, axis=0, keepdims=True)
         power_ref[:, columns] = bf16(powers)
@@ -105,29 +106,27 @@
     )(center, points)
 
 
-def sums_kernel(near, other_core, local_ref, *refs):
+def sums_kernel(near, other_core, half, local_ref, *refs):
     stat_refs, power_ref, point_ref, out_ref = refs[:near], refs[near], refs[near + 1], refs[-1]
-    nx, nh, _, owned, count = power_ref.shape
     peak, total = merge([ref[...] for ref in stat_refs])
     factor = jnp.exp(local_ref[0:1, :] - peak) / total
     core = lax.axis_index("core") ^ int(other_core)
-    for k in range(nx):
-        powers = power_ref[lax.axis_index("x") ^ k, :, core].reshape(nh * owned, count)
-        weight = bf16(f32(powers) * factor)
-        sums = jnp.dot(weight, point_ref[...], preferred_element_type=jnp.float32)
-        out_ref[k] = sums.astype(out_ref.dtype).reshape(nh, owned, -1)
-
-
-def level_one_sums(other_core, local, stats, powers, points, dtype):
-    nx, nh, _, owned, count = powers.shape
+    blocks = [power_ref[lax.axis_index("x") ^ k, half, core] for k in range(power_ref.shape[0])]
+    weight = bf16(f32(jnp.concatenate(blocks)) * factor)
+    sums = jnp.dot(weight, point_ref[...], preferred_element_type=jnp.float32)
+    out_ref[...] = sums.astype(out_ref.dtype).reshape(out_ref.shape)
+
+
+def level_one_sums(other_core, half, local, stats, powers, points, dtype):
+    nx, _, _, owned, count = powers.shape
     depth = points.shape[1]
     return kernel_call(
-        functools.partial(sums_kernel, len(stats), other_core),
+        functools.partial(sums_kernel, len(stats), other_core, half),
         "level_one_sums",
-        2 * nx * nh * owned * count * depth,
+        2 * nx * owned * count * depth,
         [VMEM] * (3 + len(stats)),
         VMEM,
-        shape((nx, nh, owned, depth), dtype),
+        shape((nx, 1, owned, depth), dtype),
     )(local, *stats, powers, points)
 
 
@@ -299,13 +298,14 @@
     near = merge_stats([local] + from_others(local, "y"))
     powers = powers.reshape(nx, nh, nc, owned, -1)
     stats = [near] + from_others(near, "zl")
-    sent = level_one_sums(True, local, stats, powers, points, jnp.bfloat16)
-    got = swapped(sent, "core")
-    kept = level_one_sums(False, local, stats, powers, points, jnp.float32)
 
     centers = center_one.reshape(nx, nh, nc, owned, depth)
     rows = []
-    for half, part in enumerate(axis_sums(kept, got, "x")):
+    for half in range(nh):
+        sent = level_one_sums(True, half, local, stats, powers, points, jnp.bfloat16)
+        got = swapped(sent, "core")
+        kept = level_one_sums(False, half, local, stats, powers, points, jnp.float32)
+        (part,) = axis_sums(kept, got, "x")
         rows.append(new_rows(half, part, swapped(part, "zh"), centers))
     level_one = own_rows(*rows)
 

time: 129 us -> 128 us (level)
    ppermute x36 -> x37, waiting for transfers between devices: 42.9 us -> 42.1 us  [swapped(): lax.ppermute(value, axis, [(i, i ^ mask) for i in range(lax.axis_size(axi...]
    pallas_call x2 -> x4, Pallas kernels: 4.7 us -> 4.98 us  [level_one_sums(): kernel_call(functools.partial(sums_kernel, len(stats), other_core, half),...]
    ppermute x36 -> x37, starting transfers between devices: 65.2 us -> 65 us  [swapped(): lax.ppermute(value, axis, [(i, i ^ mask) for i in range(lax.axis_size(axi...]
    unnamed x10 -> x8, local copies, waits for them, and re-layouts: 3.79 us -> 3.78 us
  transfers between devices with their start and end apart: 36 -> 37, of which waited for: 22 -> 22; matrix products, arithmetic and copies ran while one was open for 0% -> 0% of each run, Pallas kernels for 3% -> 5%
where the time goes in v4:
time: 128 us
  starting transfers between devices  65 us (51%)
  waiting for transfers between devices  42.1 us (33%)
  Pallas kernels  15.8 us (12%)
  local copies, waits for them, and re-layouts  3.78 us (3%)
    ppermute x37, starting transfers between devices, swapped(): lax.ppermute(value, axis, [(i, i ^ mask) for i in range(lax.axis_size(axi...  65 us
    ppermute x37, waiting for transfers between devices, swapped(): lax.ppermute(value, axis, [(i, i ^ mask) for i in range(lax.axis_size(axi...  42.1 us
    pallas_call x1, Pallas kernels, level_one_powers(): kernel_call(functools.partial(powers_kernel, scale, 512), 'level_one_powe...  6.03 us
    pallas_call x4, Pallas kernels, level_one_sums(): kernel_call(functools.partial(sums_kernel, len(stats), other_core, half),...  4.98 us
    unnamed x8, local copies, waits for them, and re-layouts  3.78 us
  transfers between devices with their start and end apart: 37, of which 22 were waited for; matrix products, arithmetic and copies ran while one was open for 0% of the time, Pallas kernels for 5%

profile of v4, /device:TPU:32, one launch (start us, length us, event | category | flops | bytes accessed | tf_op | source)
XLA Modules:
  0.0 127.8 jit_solution(2151733875165073074)
XLA Ops:
  0.6 2.2 %copy-done = bf16[2048,1024]{1,0:T(8,128)(2,1)S(1)} copy-done((bf16[2048,1024]{1,0:T(8,128)(2,1)S(1)}, bf16[2048,1024]{1,0:T(8,128)(2,1)}, u32[]{:S(2)}) %copy-start) | copy-done | bytes 4194328
  4.4 6.0 %level_one_powers.1 = (bf16[1024,2048]{1,0:T(8,128)(2,1)S(1)}, f32[2,2048]{1,0:T(2,128)S(1)}) custom-call(bf16[1024,1024]{1,0:T(8,128)(2,1)S(1)} %copy-done.1, bf16[2048,1024]{1,0:T(8,128)(2,1)S(1)} %copy-done), custom_call_target="tpu_custom_call" | custom-call | flops 4294967296 | bytes 1024 | tf_op jit(solution)/shard_map/level_one_powers/pallas_call | solution.py:98
  10.4 3.3 %collective-permute-start = (f32[2,2048]{1,0:T(2,128)S(1)}, f32[2,2048]{1,0:T(2,128)S(1)}, u32[]{:S(2)}, u32[]{:S(2)}) collective-permute-start(f32[2,2048]{1,0:T(2,128)S(1)} %get-tuple-element.19.refs_0_.local_ref), channel_id=1, source_target_pairs={{0,128},{64,192},{128,0},{192,64},{1,129},{65,193},{129,1},{193,65... | collective-permute-start | bytes 49160 | tf_op jit(solution)/shard_map/ppermute | solution.py:19
  17.5 1.9 %collective-permute-done.2.refs_3_ = f32[2,2048]{1,0:T(2,128)S(1)} collective-permute-done((f32[2,2048]{1,0:T(2,128)S(1)}, f32[2,2048]{1,0:T(2,128)S(1)}, u32[]{:S(2)}, u32[]{:S(2)}) %collective-permute-start.2) | collective-permute-done | bytes 16416 | tf_op jit(solution)/shard_map/ppermute | solution.py:19
  19.4 2.0 %collective-permute-start.3 = (f32[2,2048]{1,0:T(2,128)S(1)}, f32[2,2048]{1,0:T(2,128)S(1)}, u32[]{:S(2)}, u32[]{:S(2)}) collective-permute-start(f32[2,2048]{1,0:T(2,128)S(1)} %merge_stats.2.refs_0_), channel_id=1, source_target_pairs={{0,48},{16,32},{32,16},{48,0},{1,49},{17,33},{33,17},{49,1},{2,50}... | collective-permute-start | bytes 49160 | tf_op jit(solution)/shard_map/ppermute | solution.py:19
  24.2 1.8 %collective-permute-done.4.refs_2_ = f32[2,2048]{1,0:T(2,128)S(1)} collective-permute-done((f32[2,2048]{1,0:T(2,128)S(1)}, f32[2,2048]{1,0:T(2,128)S(1)}, u32[]{:S(2)}, u32[]{:S(2)}) %collective-permute-start.4) | collective-permute-done | bytes 16416 | tf_op jit(solution)/shard_map/ppermute | solution.py:19
  31.4 3.1 %collective-permute-start.12 = (bf16[64,1024]{1,0:T(8,128)(2,1)S(1)}, bf16[64,1024]{1,0:T(8,128)(2,1)S(1)}, u32[]{:S(2)}, u32[]{:S(2)}) collective-permute-start(bf16[64,1024]{1,0:T(8,128)(2,1)S(1)} %get-tuple-element.26), channel_id=1, source_target_pairs={{0,8},{4,12},{8,0},{12,4},{1,9},{5,13},{9,1},{13,5},{2,10},{6,14},... | collective-permute-start | bytes 393224 | tf_op jit(solution)/shard_map/ppermute | solution.py:19
  37.0 3.0 %collective-permute-start.7 = (bf16[64,1024]{1,0:T(8,128)(2,1)S(1)}, bf16[64,1024]{1,0:T(8,128)(2,1)S(1)}, u32[]{:S(2)}, u32[]{:S(2)}) collective-permute-start(bf16[64,1024]{1,0:T(8,128)(2,1)S(1)} %get-tuple-element.22), channel_id=1, source_target_pairs={{0,8},{4,12},{8,0},{12,4},{1,9},{5,13},{9,1},{13,5},{2,10},{6,14},... | collective-permute-start | bytes 393224 | tf_op jit(solution)/shard_map/ppermute | solution.py:19
  44.2 6.4 %collective-permute-start.15 = (bf16[64,1024]{1,0:T(8,128)(2,1)S(1)}, bf16[64,1024]{1,0:T(8,128)(2,1)S(1)}, u32[]{:S(2)}, u32[]{:S(2)}) collective-permute-start(bf16[64,1024]{1,0:T(8,128)(2,1)S(1)} %total.4.part_ref), channel_id=1, source_target_pairs={{0,2},{2,0},{1,3},{3,1},{4,6},{6,4},{5,7},{7,5},{8,10},{10,8},{9,1... | collective-permute-start | bytes 393224 | tf_op jit(solution)/shard_map/ppermute | solution.py:19
  50.6 4.3 %collective-permute-start.10 = (bf16[64,1024]{1,0:T(8,128)(2,1)S(1)}, bf16[64,1024]{1,0:T(8,128)(2,1)S(1)}, u32[]{:S(2)}, u32[]{:S(2)}) collective-permute-start(bf16[64,1024]{1,0:T(8,128)(2,1)S(1)} %total.3.part_ref), channel_id=1, source_target_pairs={{0,2},{2,0},{1,3},{3,1},{4,6},{6,4},{5,7},{7,5},{8,10},{10,8},{9,1... | collective-permute-start | bytes 393224 | tf_op jit(solution)/shard_map/ppermute | solution.py:19
  55.2 6.0 %collective-permute-start.20 = (bf16[64,1024]{1,0:T(8,128)(2,1)S(1)}, bf16[64,1024]{1,0:T(8,128)(2,1)S(1)}, u32[]{:S(2)}, u32[]{:S(2)}) collective-permute-start(bf16[64,1024]{1,0:T(8,128)(2,1)S(1)} %new_rows.3.b_ref.refs_4_), channel_id=1, source_target_pairs={{0,8},{4,12},{8,0},{12,4},{1,9},{5,13},{9,1},{13,5},{2,10},{6,14},... | collective-permute-start | bytes 393224 | tf_op jit(solution)/shard_map/ppermute | solution.py:19
  62.2 3.5 %collective-permute-start.17 = (bf16[64,1024]{1,0:T(8,128)(2,1)S(1)}, bf16[64,1024]{1,0:T(8,128)(2,1)S(1)}, u32[]{:S(2)}, u32[]{:S(2)}) collective-permute-start(bf16[64,1024]{1,0:T(8,128)(2,1)S(1)} %new_rows.2.a_ref.refs_0_), channel_id=1, source_target_pairs={{0,8},{4,12},{8,0},{12,4},{1,9},{5,13},{9,1},{13,5},{2,10},{6,14},... | collective-permute-start | bytes 393224 | tf_op jit(solution)/shard_map/ppermute | solution.py:19
  67.7 3.0 %collective-permute-done.22.refs_7_ = bf16[64,1024]{1,0:T(8,128)(2,1)S(1)} collective-permute-done((bf16[64,1024]{1,0:T(8,128)(2,1)S(1)}, bf16[64,1024]{1,0:T(8,128)(2,1)S(1)}, u32[]{:S(2)}, u32[]{:S(2)}) %collective-permute-start.22) | collective-permute-done | bytes 131104 | tf_op jit(solution)/shard_map/ppermute | solution.py:19
  73.6 2.3 %collective-permute-start.23 = (f32[2,512]{1,0:T(2,128)S(1)}, f32[2,512]{1,0:T(2,128)S(1)}, u32[]{:S(2)}, u32[]{:S(2)}) collective-permute-start(f32[2,512]{1,0:T(2,128)S(1)} %get-tuple-element.29.refs_0_.local_ref), channel_id=1, source_target_pairs={{0,8},{4,12},{8,0},{12,4},{1,9},{5,13},{9,1},{13,5},{2,10},{6,14},... | collective-permute-start | bytes 12296 | tf_op jit(solution)/shard_map/ppermute | solution.py:19
  81.3 7.2 %collective-permute-start.26 = (f32[2,512]{1,0:T(2,128)S(1)}, f32[2,512]{1,0:T(2,128)S(1)}, u32[]{:S(2)}, u32[]{:S(2)}) collective-permute-start(f32[2,512]{1,0:T(2,128)S(1)} %merge_stats.3.refs_0_), channel_id=1, source_target_pairs={{0,2},{2,0},{1,3},{3,1},{4,6},{6,4},{5,7},{7,5},{8,10},{10,8},{9,1... | collective-permute-start | bytes 12296 | tf_op jit(solution)/shard_map/ppermute | solution.py:19
  94.0 2.9 %collective-permute-start.30 = (bf16[64,1024]{1,0:T(8,128)(2,1)S(1)}, bf16[64,1024]{1,0:T(8,128)(2,1)S(1)}, u32[]{:S(2)}, u32[]{:S(2)}) collective-permute-start(bf16[64,1024]{1,0:T(8,128)(2,1)S(1)} %get-tuple-element.35), channel_id=1, source_target_pairs={{0,192},{64,128},{128,64},{192,0},{1,193},{65,129},{129,65},{193,1... | collective-permute-start | bytes 393224 | tf_op jit(solution)/shard_map/ppermute | solution.py:19
  96.9 3.8 %collective-permute-done.28.refs_0_ = bf16[64,1024]{1,0:T(8,128)(2,1)S(1)} collective-permute-done((bf16[64,1024]{1,0:T(8,128)(2,1)S(1)}, bf16[64,1024]{1,0:T(8,128)(2,1)S(1)}, u32[]{:S(2)}, u32[]{:S(2)}) %collective-permute-start.28) | collective-permute-done | bytes 131104 | tf_op jit(solution)/shard_map/ppermute | solution.py:19
  100.7 2.0 %collective-permute-done.30.refs_2_ = bf16[64,1024]{1,0:T(8,128)(2,1)S(1)} collective-permute-done((bf16[64,1024]{1,0:T(8,128)(2,1)S(1)}, bf16[64,1024]{1,0:T(8,128)(2,1)S(1)}, u32[]{:S(2)}, u32[]{:S(2)}) %collective-permute-start.30) | collective-permute-done | bytes 131104 | tf_op jit(solution)/shard_map/ppermute | solution.py:19
  102.8 2.5 %collective-permute-start.32 = (bf16[64,1024]{1,0:T(8,128)(2,1)S(1)}, bf16[64,1024]{1,0:T(8,128)(2,1)S(1)}, u32[]{:S(2)}, u32[]{:S(2)}) collective-permute-start(bf16[64,1024]{1,0:T(8,128)(2,1)S(1)} %total.5.a_ref), channel_id=1, source_target_pairs={{0,32},{16,48},{32,0},{48,16},{1,33},{17,49},{33,1},{49,17},{2,34}... | collective-permute-start | bytes 393224 | tf_op jit(solution)/shard_map/ppermute | solution.py:19
  106.3 2.9 %collective-permute-done.31.b_ref = bf16[64,1024]{1,0:T(8,128)(2,1)S(1)} collective-permute-done((bf16[64,1024]{1,0:T(8,128)(2,1)S(1)}, bf16[64,1024]{1,0:T(8,128)(2,1)S(1)}, u32[]{:S(2)}, u32[]{:S(2)}) %collective-permute-start.31) | collective-permute-done | bytes 131104 | tf_op jit(solution)/shard_map/ppermute | solution.py:19
  109.1 5.7 %collective-permute-done.32.c_ref = bf16[64,1024]{1,0:T(8,128)(2,1)S(1)} collective-permute-done((bf16[64,1024]{1,0:T(8,128)(2,1)S(1)}, bf16[64,1024]{1,0:T(8,128)(2,1)S(1)}, u32[]{:S(2)}, u32[]{:S(2)}) %collective-permute-start.32) | collective-permute-done | bytes 131104 | tf_op jit(solution)/shard_map/ppermute | solution.py:19
  114.8 3.1 %collective-permute-done.33.d_ref = bf16[64,1024]{1,0:T(8,128)(2,1)S(1)} collective-permute-done((bf16[64,1024]{1,0:T(8,128)(2,1)S(1)}, bf16[64,1024]{1,0:T(8,128)(2,1)S(1)}, u32[]{:S(2)}, u32[]{:S(2)}) %collective-permute-start.33) | collective-permute-done | bytes 131104 | tf_op jit(solution)/shard_map/ppermute | solution.py:19
  118.8 3.4 %collective-permute-start.36 = (bf16[64,1024]{1,0:T(8,128)(2,1)S(1)}, bf16[64,1024]{1,0:T(8,128)(2,1)S(1)}, u32[]{:S(2)}, u32[]{:S(2)}) collective-permute-start(bf16[64,1024]{1,0:T(8,128)(2,1)S(1)} %finish.1.refs_0_), channel_id=1, source_target_pairs={{0,192},{64,128},{128,64},{192,0},{1,193},{65,129},{129,65},{193,1... | collective-permute-start | bytes 393224 | tf_op jit(solution)/shard_map/ppermute | solution.py:19
  122.9 2.5 %collective-permute-done.34.refs_1_ = bf16[64,1024]{1,0:T(8,128)(2,1)S(1)} collective-permute-done((bf16[64,1024]{1,0:T(8,128)(2,1)S(1)}, bf16[64,1024]{1,0:T(8,128)(2,1)S(1)}, u32[]{:S(2)}, u32[]{:S(2)}) %collective-permute-start.34) | collective-permute-done | bytes 131104 | tf_op jit(solution)/shard_map/ppermute | solution.py:19
  (79 shorter events, 42.0 us)
Async XLA Ops:
  29.2 7.7 %collective-permute-start.6 = (bf16[4,1,64,1024]{3,2,1,0:T(8,128)(2,1)S(1)}, bf16[4,1,64,1024]{3,2,1,0:T(8,128)(2,1)S(1)}, u32[]{:S(2)}, u32[]{:S(2)}) collective-permute-start(bf16[4,1,64,1024]{3,2,1,0:T(8,128)(2,1)S(1)} %level_one_sums.5), channel_id=1, source_target_pairs={{0,1},{1,0},{2,3},{3,2},{4,5},{5,4},{6,7},{7,6},{8,9},{9,8},{10,11... | collective-permute-start | bytes 1572872 | tf_op jit(solution)/shard_map/ppermute | solution.py:19
  29.8 36.0 %collective-permute-start.16 = (bf16[256,1024]{1,0:T(8,128)(2,1)S(1)}, bf16[256,1024]{1,0:T(8,128)(2,1)S(1)}, u32[]{:S(2)}, u32[]{:S(2)}) collective-permute-start(bf16[256,1024]{1,0:T(8,128)(2,1)S(1)} %copy-done.3), channel_id=1, source_target_pairs={{0,1},{1,0},{2,3},{3,2},{4,5},{5,4},{6,7},{7,6},{8,9},{9,8},{10,11... | collective-permute-start | bytes 1572872 | tf_op jit(solution)/shard_map/ppermute | solution.py:19
  31.4 8.7 %collective-permute-start.12 = (bf16[64,1024]{1,0:T(8,128)(2,1)S(1)}, bf16[64,1024]{1,0:T(8,128)(2,1)S(1)}, u32[]{:S(2)}, u32[]{:S(2)}) collective-permute-start(bf16[64,1024]{1,0:T(8,128)(2,1)S(1)} %get-tuple-element.26), channel_id=1, source_target_pairs={{0,8},{4,12},{8,0},{12,4},{1,9},{5,13},{9,1},{13,5},{2,10},{6,14},... | collective-permute-start | bytes 393224 | tf_op jit(solution)/shard_map/ppermute | solution.py:19
  34.5 7.7 %collective-permute-start.13 = (bf16[64,1024]{1,0:T(8,128)(2,1)S(1)}, bf16[64,1024]{1,0:T(8,128)(2,1)S(1)}, u32[]{:S(2)}, u32[]{:S(2)}) collective-permute-start(bf16[64,1024]{1,0:T(8,128)(2,1)S(1)} %get-tuple-element.27), channel_id=1, source_target_pairs={{0,4},{4,0},{8,12},{12,8},{1,5},{5,1},{9,13},{13,9},{2,6},{6,2},{1... | collective-permute-start | bytes 393224 | tf_op jit(solution)/shard_map/ppermute | solution.py:19
  35.1 9.0 %collective-permute-start.14 = (bf16[64,1024]{1,0:T(8,128)(2,1)S(1)}, bf16[64,1024]{1,0:T(8,128)(2,1)S(1)}, u32[]{:S(2)}, u32[]{:S(2)}) collective-permute-start(bf16[64,1024]{1,0:T(8,128)(2,1)S(1)} %get-tuple-element.28), channel_id=1, source_target_pairs={{0,12},{4,8},{8,4},{12,0},{1,13},{5,9},{9,5},{13,1},{2,14},{6,10},... | collective-permute-start | bytes 393224 | tf_op jit(solution)/shard_map/ppermute | solution.py:19
  37.0 13.5 %collective-permute-start.7 = (bf16[64,1024]{1,0:T(8,128)(2,1)S(1)}, bf16[64,1024]{1,0:T(8,128)(2,1)S(1)}, u32[]{:S(2)}, u32[]{:S(2)}) collective-permute-start(bf16[64,1024]{1,0:T(8,128)(2,1)S(1)} %get-tuple-element.22), channel_id=1, source_target_pairs={{0,8},{4,12},{8,0},{12,4},{1,9},{5,13},{9,1},{13,5},{2,10},{6,14},... | collective-permute-start | bytes 393224 | tf_op jit(solution)/shard_map/ppermute | solution.py:19
  40.1 10.5 %collective-permute-start.8 = (bf16[64,1024]{1,0:T(8,128)(2,1)S(1)}, bf16[64,1024]{1,0:T(8,128)(2,1)S(1)}, u32[]{:S(2)}, u32[]{:S(2)}) collective-permute-start(bf16[64,1024]{1,0:T(8,128)(2,1)S(1)} %get-tuple-element.23), channel_id=1, source_target_pairs={{0,4},{4,0},{8,12},{12,8},{1,5},{5,1},{9,13},{13,9},{2,6},{6,2},{1... | collective-permute-start | bytes 393224 | tf_op jit(solution)/shard_map/ppermute | solution.py:19
  42.3 8.3 %collective-permute-start.9 = (bf16[64,1024]{1,0:T(8,128)(2,1)S(1)}, bf16[64,1024]{1,0:T(8,128)(2,1)S(1)}, u32[]{:S(2)}, u32[]{:S(2)}) collective-permute-start(bf16[64,1024]{1,0:T(8,128)(2,1)S(1)} %get-tuple-element.24), channel_id=1, source_target_pairs={{0,12},{4,8},{8,4},{12,0},{1,13},{5,9},{9,5},{13,1},{2,14},{6,10},... | collective-permute-start | bytes 393224 | tf_op jit(solution)/shard_map/ppermute | solution.py:19
  44.2 10.7 %collective-permute-start.15 = (bf16[64,1024]{1,0:T(8,128)(2,1)S(1)}, bf16[64,1024]{1,0:T(8,128)(2,1)S(1)}, u32[]{:S(2)}, u32[]{:S(2)}) collective-permute-start(bf16[64,1024]{1,0:T(8,128)(2,1)S(1)} %total.4.part_ref), channel_id=1, source_target_pairs={{0,2},{2,0},{1,3},{3,1},{4,6},{6,4},{5,7},{7,5},{8,10},{10,8},{9,1... | collective-permute-start | bytes 393224 | tf_op jit(solution)/shard_map/ppermute | solution.py:19
  50.6 11.3 %collective-permute-start.10 = (bf16[64,1024]{1,0:T(8,128)(2,1)S(1)}, bf16[64,1024]{1,0:T(8,128)(2,1)S(1)}, u32[]{:S(2)}, u32[]{:S(2)}) collective-permute-start(bf16[64,1024]{1,0:T(8,128)(2,1)S(1)} %total.3.part_ref), channel_id=1, source_target_pairs={{0,2},{2,0},{1,3},{3,1},{4,6},{6,4},{5,7},{7,5},{8,10},{10,8},{9,1... | collective-permute-start | bytes 393224 | tf_op jit(solution)/shard_map/ppermute | solution.py:19
  55.2 11.1 %collective-permute-start.20 = (bf16[64,1024]{1,0:T(8,128)(2,1)S(1)}, bf16[64,1024]{1,0:T(8,128)(2,1)S(1)}, u32[]{:S(2)}, u32[]{:S(2)}) collective-permute-start(bf16[64,1024]{1,0:T(8,128)(2,1)S(1)} %new_rows.3.b_ref.refs_4_), channel_id=1, source_target_pairs={{0,8},{4,12},{8,0},{12,4},{1,9},{5,13},{9,1},{13,5},{2,10},{6,14},... | collective-permute-start | bytes 393224 | tf_op jit(solution)/shard_map/ppermute | solution.py:19
  61.2 6.4 %collective-permute-start.21 = (bf16[64,1024]{1,0:T(8,128)(2,1)S(1)}, bf16[64,1024]{1,0:T(8,128)(2,1)S(1)}, u32[]{:S(2)}, u32[]{:S(2)}) collective-permute-start(bf16[64,1024]{1,0:T(8,128)(2,1)S(1)} %new_rows.3.b_ref.refs_4_), channel_id=1, source_target_pairs={{0,4},{4,0},{8,12},{12,8},{1,5},{5,1},{9,13},{13,9},{2,6},{6,2},{1... | collective-permute-start | bytes 393224 | tf_op jit(solution)/shard_map/ppermute | solution.py:19
  61.8 8.9 %collective-permute-start.22 = (bf16[64,1024]{1,0:T(8,128)(2,1)S(1)}, bf16[64,1024]{1,0:T(8,128)(2,1)S(1)}, u32[]{:S(2)}, u32[]{:S(2)}) collective-permute-start(bf16[64,1024]{1,0:T(8,128)(2,1)S(1)} %new_rows.3.b_ref.refs_4_), channel_id=1, source_target_pairs={{0,12},{4,8},{8,4},{12,0},{1,13},{5,9},{9,5},{13,1},{2,14},{6,10},... | collective-permute-start | bytes 393224 | tf_op jit(solution)/shard_map/ppermute | solution.py:19
  62.2 8.5 %collective-permute-start.17 = (bf16[64,1024]{1,0:T(8,128)(2,1)S(1)}, bf16[64,1024]{1,0:T(8,128)(2,1)S(1)}, u32[]{:S(2)}, u32[]{:S(2)}) collective-permute-start(bf16[64,1024]{1,0:T(8,128)(2,1)S(1)} %new_rows.2.a_ref.refs_0_), channel_id=1, source_target_pairs={{0,8},{4,12},{8,0},{12,4},{1,9},{5,13},{9,1},{13,5},{2,10},{6,14},... | collective-permute-start | bytes 393224 | tf_op jit(solution)/shard_map/ppermute | solution.py:19
  81.3 8.8 %collective-permute-start.26 = (f32[2,512]{1,0:T(2,128)S(1)}, f32[2,512]{1,0:T(2,128)S(1)}, u32[]{:S(2)}, u32[]{:S(2)}) collective-permute-start(f32[2,512]{1,0:T(2,128)S(1)} %merge_stats.3.refs_0_), channel_id=1, source_target_pairs={{0,2},{2,0},{1,3},{3,1},{4,6},{6,4},{5,7},{7,5},{8,10},{10,8},{9,1... | collective-permute-start | bytes 12296 | tf_op jit(solution)/shard_map/ppermute | solution.py:19
  92.7 7.9 %collective-permute-start.28 = (bf16[64,1024]{1,0:T(8,128)(2,1)S(1)}, bf16[64,1024]{1,0:T(8,128)(2,1)S(1)}, u32[]{:S(2)}, u32[]{:S(2)}) collective-permute-start(bf16[64,1024]{1,0:T(8,128)(2,1)S(1)} %get-tuple-element.33), channel_id=1, source_target_pairs={{0,128},{64,192},{128,0},{192,64},{1,129},{65,193},{129,1},{193,65... | collective-permute-start | bytes 393224 | tf_op jit(solution)/shard_map/ppermute | solution.py:19
  93.4 7.2 %collective-permute-start.29 = (bf16[64,1024]{1,0:T(8,128)(2,1)S(1)}, bf16[64,1024]{1,0:T(8,128)(2,1)S(1)}, u32[]{:S(2)}, u32[]{:S(2)}) collective-permute-start(bf16[64,1024]{1,0:T(8,128)(2,1)S(1)} %get-tuple-element.34), channel_id=1, source_target_pairs={{0,64},{64,0},{128,192},{192,128},{1,65},{65,1},{129,193},{193,129... | collective-permute-start | bytes 393224 | tf_op jit(solution)/shard_map/ppermute | solution.py:19
  94.0 8.6 %collective-permute-start.30 = (bf16[64,1024]{1,0:T(8,128)(2,1)S(1)}, bf16[64,1024]{1,0:T(8,128)(2,1)S(1)}, u32[]{:S(2)}, u32[]{:S(2)}) collective-permute-start(bf16[64,1024]{1,0:T(8,128)(2,1)S(1)} %get-tuple-element.35), channel_id=1, source_target_pairs={{0,192},{64,128},{128,64},{192,0},{1,193},{65,129},{129,65},{193,1... | collective-permute-start | bytes 393224 | tf_op jit(solution)/shard_map/ppermute | solution.py:19
  102.7 6.4 %collective-permute-start.31 = (bf16[64,1024]{1,0:T(8,128)(2,1)S(1)}, bf16[64,1024]{1,0:T(8,128)(2,1)S(1)}, u32[]{:S(2)}, u32[]{:S(2)}) collective-permute-start(bf16[64,1024]{1,0:T(8,128)(2,1)S(1)} %total.5.a_ref), channel_id=1, source_target_pairs={{0,16},{16,0},{32,48},{48,32},{1,17},{17,1},{33,49},{49,33},{2,18}... | collective-permute-start | bytes 393224 | tf_op jit(solution)/shard_map/ppermute | solution.py:19
  102.8 12.0 %collective-permute-start.32 = (bf16[64,1024]{1,0:T(8,128)(2,1)S(1)}, bf16[64,1024]{1,0:T(8,128)(2,1)S(1)}, u32[]{:S(2)}, u32[]{:S(2)}) collective-permute-start(bf16[64,1024]{1,0:T(8,128)(2,1)S(1)} %total.5.a_ref), channel_id=1, source_target_pairs={{0,32},{16,48},{32,0},{48,16},{1,33},{17,49},{33,1},{49,17},{2,34}... | collective-permute-start | bytes 393224 | tf_op jit(solution)/shard_map/ppermute | solution.py:19
  105.3 12.5 %collective-permute-start.33 = (bf16[64,1024]{1,0:T(8,128)(2,1)S(1)}, bf16[64,1024]{1,0:T(8,128)(2,1)S(1)}, u32[]{:S(2)}, u32[]{:S(2)}) collective-permute-start(bf16[64,1024]{1,0:T(8,128)(2,1)S(1)} %total.5.a_ref), channel_id=1, source_target_pairs={{0,48},{16,32},{32,16},{48,0},{1,49},{17,33},{33,17},{49,1},{2,50}... | collective-permute-start | bytes 393224 | tf_op jit(solution)/shard_map/ppermute | solution.py:19
  118.0 7.4 %collective-permute-start.34 = (bf16[64,1024]{1,0:T(8,128)(2,1)S(1)}, bf16[64,1024]{1,0:T(8,128)(2,1)S(1)}, u32[]{:S(2)}, u32[]{:S(2)}) collective-permute-start(bf16[64,1024]{1,0:T(8,128)(2,1)S(1)} %finish.1.refs_0_), channel_id=1, source_target_pairs={{0,128},{64,192},{128,0},{192,64},{1,129},{65,193},{129,1},{193,65... | collective-permute-start | bytes 393224 | tf_op jit(solution)/shard_map/ppermute | solution.py:19
  118.3 7.1 %collective-permute-start.35 = (bf16[64,1024]{1,0:T(8,128)(2,1)S(1)}, bf16[64,1024]{1,0:T(8,128)(2,1)S(1)}, u32[]{:S(2)}, u32[]{:S(2)}) collective-permute-start(bf16[64,1024]{1,0:T(8,128)(2,1)S(1)} %finish.1.refs_0_), channel_id=1, source_target_pairs={{0,64},{64,0},{128,192},{192,128},{1,65},{65,1},{129,193},{193,129... | collective-permute-start | bytes 393224 | tf_op jit(solution)/shard_map/ppermute | solution.py:19
  118.8 7.9 %collective-permute-start.36 = (bf16[64,1024]{1,0:T(8,128)(2,1)S(1)}, bf16[64,1024]{1,0:T(8,128)(2,1)S(1)}, u32[]{:S(2)}, u32[]{:S(2)}) collective-permute-start(bf16[64,1024]{1,0:T(8,128)(2,1)S(1)} %finish.1.refs_0_), channel_id=1, source_target_pairs={{0,192},{64,128},{128,64},{192,0},{1,193},{65,129},{129,65},{193,1... | collective-permute-start | bytes 393224 | tf_op jit(solution)/shard_map/ppermute | solution.py:19
  (17 other events, 84.0 us)

commit v5 on v4

--- a/solution.py
+++ b/solution.py
@@ -207,7 +207,7 @@
         row_ref[pl.ds(pl.multiple_of(first, size), size), :] = ref[...]
     raw = times_rows(center_ref[...], row_ref[...])
     peak = jnp.max(raw, axis=0, keepdims=True)
-    powers = jnp.exp((raw - peak) * scale)
+    powers = jnp.exp2((raw - peak) * (scale * LOG2_E))
     stat_ref[0:1, :] = peak * scale
     stat_ref[1:2, :] = jnp.sum(powers, axis=0, keepdims=True)
     power_ref[...] = bf16(powers)
@@ -312,8 +312,8 @@
     two_core = swapped(center_two, "core")
     pieces = [piece for half in rows for piece in [half] + from_others(half, "x")]
     rows, powers, local = level_two_powers(center_two, two_core, pieces, ny, scale)
-    near = merge_stats([local] + from_others(local, "x"))
-    stats = [near, swapped(near, "zh")]
+    near = merge_stats([local, swapped(local, "zh")])
+    stats = [near] + from_others(near, "x")
     sent = level_two_sums(True, local, stats, powers, rows, ny, jnp.bfloat16)
     got = swapped(sent, "core")
     kept = level_two_sums(False, local, stats, powers, rows, ny, jnp.float32)

time: 128 us -> 128 us (level)
  no operation moved by 1% of the time
where the time goes in v5:
time: 128 us
  starting transfers between devices  64.4 us (50%)
  waiting for transfers between devices  42.7 us (33%)
  Pallas kernels  15.8 us (12%)
  local copies, waits for them, and re-layouts  3.78 us (3%)
    ppermute x37, starting transfers between devices, swapped(): lax.ppermute(value, axis, [(i, i ^ mask) for i in range(lax.axis_size(axi...  64.4 us
    ppermute x37, waiting for transfers between devices, swapped(): lax.ppermute(value, axis, [(i, i ^ mask) for i in range(lax.axis_size(axi...  42.7 us
    pallas_call x1, Pallas kernels, level_one_powers(): kernel_call(functools.partial(powers_kernel, scale, 512), 'level_one_powe...  6.03 us
    pallas_call x4, Pallas kernels, level_one_sums(): kernel_call(functools.partial(sums_kernel, len(stats), other_core, half),...  4.98 us
    unnamed x8, local copies, waits for them, and re-layouts  3.78 us
  transfers between devices with their start and end apart: 37, of which 22 were waited for; matrix products, arithmetic and copies ran while one was open for 0% of the time, Pallas kernels for 5%

profile of v5, /device:TPU:32, one launch (start us, length us, event | category | flops | bytes accessed | tf_op | source)
XLA Modules:
  0.0 127.7 jit_solution(77659519768760154)
XLA Ops:
  0.6 2.2 %copy-done = bf16[2048,1024]{1,0:T(8,128)(2,1)S(1)} copy-done((bf16[2048,1024]{1,0:T(8,128)(2,1)S(1)}, bf16[2048,1024]{1,0:T(8,128)(2,1)}, u32[]{:S(2)}) %copy-start) | copy-done | bytes 4194328
  4.4 6.0 %level_one_powers.1 = (bf16[1024,2048]{1,0:T(8,128)(2,1)S(1)}, f32[2,2048]{1,0:T(2,128)S(1)}) custom-call(bf16[1024,1024]{1,0:T(8,128)(2,1)S(1)} %copy-done.1, bf16[2048,1024]{1,0:T(8,128)(2,1)S(1)} %copy-done), custom_call_target="tpu_custom_call" | custom-call | flops 4294967296 | bytes 1024 | tf_op jit(solution)/shard_map/level_one_powers/pallas_call | solution.py:98
  10.4 3.3 %collective-permute-start = (f32[2,2048]{1,0:T(2,128)S(1)}, f32[2,2048]{1,0:T(2,128)S(1)}, u32[]{:S(2)}, u32[]{:S(2)}) collective-permute-start(f32[2,2048]{1,0:T(2,128)S(1)} %get-tuple-element.19.refs_0_.local_ref), channel_id=1, source_target_pairs={{0,128},{64,192},{128,0},{192,64},{1,129},{65,193},{129,1},{193,65... | collective-permute-start | bytes 49160 | tf_op jit(solution)/shard_map/ppermute | solution.py:19
  17.5 1.9 %collective-permute-done.2.refs_3_ = f32[2,2048]{1,0:T(2,128)S(1)} collective-permute-done((f32[2,2048]{1,0:T(2,128)S(1)}, f32[2,2048]{1,0:T(2,128)S(1)}, u32[]{:S(2)}, u32[]{:S(2)}) %collective-permute-start.2) | collective-permute-done | bytes 16416 | tf_op jit(solution)/shard_map/ppermute | solution.py:19
  19.4 2.0 %collective-permute-start.3 = (f32[2,2048]{1,0:T(2,128)S(1)}, f32[2,2048]{1,0:T(2,128)S(1)}, u32[]{:S(2)}, u32[]{:S(2)}) collective-permute-start(f32[2,2048]{1,0:T(2,128)S(1)} %merge_stats.2.refs_0_), channel_id=1, source_target_pairs={{0,48},{16,32},{32,16},{48,0},{1,49},{17,33},{33,17},{49,1},{2,50}... | collective-permute-start | bytes 49160 | tf_op jit(solution)/shard_map/ppermute | solution.py:19
  31.4 3.1 %collective-permute-start.12 = (bf16[64,1024]{1,0:T(8,128)(2,1)S(1)}, bf16[64,1024]{1,0:T(8,128)(2,1)S(1)}, u32[]{:S(2)}, u32[]{:S(2)}) collective-permute-start(bf16[64,1024]{1,0:T(8,128)(2,1)S(1)} %get-tuple-element.26), channel_id=1, source_target_pairs={{0,8},{4,12},{8,0},{12,4},{1,9},{5,13},{9,1},{13,5},{2,10},{6,14},... | collective-permute-start | bytes 393224 | tf_op jit(solution)/shard_map/ppermute | solution.py:19
  37.0 3.0 %collective-permute-start.7 = (bf16[64,1024]{1,0:T(8,128)(2,1)S(1)}, bf16[64,1024]{1,0:T(8,128)(2,1)S(1)}, u32[]{:S(2)}, u32[]{:S(2)}) collective-permute-start(bf16[64,1024]{1,0:T(8,128)(2,1)S(1)} %get-tuple-element.22), channel_id=1, source_target_pairs={{0,8},{4,12},{8,0},{12,4},{1,9},{5,13},{9,1},{13,5},{2,10},{6,14},... | collective-permute-start | bytes 393224 | tf_op jit(solution)/shard_map/ppermute | solution.py:19
  44.2 6.4 %collective-permute-start.15 = (bf16[64,1024]{1,0:T(8,128)(2,1)S(1)}, bf16[64,1024]{1,0:T(8,128)(2,1)S(1)}, u32[]{:S(2)}, u32[]{:S(2)}) collective-permute-start(bf16[64,1024]{1,0:T(8,128)(2,1)S(1)} %total.4.part_ref), channel_id=1, source_target_pairs={{0,2},{2,0},{1,3},{3,1},{4,6},{6,4},{5,7},{7,5},{8,10},{10,8},{9,1... | collective-permute-start | bytes 393224 | tf_op jit(solution)/shard_map/ppermute | solution.py:19
  50.6 4.3 %collective-permute-start.10 = (bf16[64,1024]{1,0:T(8,128)(2,1)S(1)}, bf16[64,1024]{1,0:T(8,128)(2,1)S(1)}, u32[]{:S(2)}, u32[]{:S(2)}) collective-permute-start(bf16[64,1024]{1,0:T(8,128)(2,1)S(1)} %total.3.part_ref), channel_id=1, source_target_pairs={{0,2},{2,0},{1,3},{3,1},{4,6},{6,4},{5,7},{7,5},{8,10},{10,8},{9,1... | collective-permute-start | bytes 393224 | tf_op jit(solution)/shard_map/ppermute | solution.py:19
  55.2 6.0 %collective-permute-start.20 = (bf16[64,1024]{1,0:T(8,128)(2,1)S(1)}, bf16[64,1024]{1,0:T(8,128)(2,1)S(1)}, u32[]{:S(2)}, u32[]{:S(2)}) collective-permute-start(bf16[64,1024]{1,0:T(8,128)(2,1)S(1)} %new_rows.3.b_ref.refs_4_), channel_id=1, source_target_pairs={{0,8},{4,12},{8,0},{12,4},{1,9},{5,13},{9,1},{13,5},{2,10},{6,14},... | collective-permute-start | bytes 393224 | tf_op jit(solution)/shard_map/ppermute | solution.py:19
  62.2 3.5 %collective-permute-start.17 = (bf16[64,1024]{1,0:T(8,128)(2,1)S(1)}, bf16[64,1024]{1,0:T(8,128)(2,1)S(1)}, u32[]{:S(2)}, u32[]{:S(2)}) collective-permute-start(bf16[64,1024]{1,0:T(8,128)(2,1)S(1)} %new_rows.2.a_ref.refs_0_), channel_id=1, source_target_pairs={{0,8},{4,12},{8,0},{12,4},{1,9},{5,13},{9,1},{13,5},{2,10},{6,14},... | collective-permute-start | bytes 393224 | tf_op jit(solution)/shard_map/ppermute | solution.py:19
  67.7 3.0 %collective-permute-done.22.refs_7_ = bf16[64,1024]{1,0:T(8,128)(2,1)S(1)} collective-permute-done((bf16[64,1024]{1,0:T(8,128)(2,1)S(1)}, bf16[64,1024]{1,0:T(8,128)(2,1)S(1)}, u32[]{:S(2)}, u32[]{:S(2)}) %collective-permute-start.22) | collective-permute-done | bytes 131104 | tf_op jit(solution)/shard_map/ppermute | solution.py:19
  73.6 6.6 %collective-permute-start.23 = (f32[2,512]{1,0:T(2,128)S(1)}, f32[2,512]{1,0:T(2,128)S(1)}, u32[]{:S(2)}, u32[]{:S(2)}) collective-permute-start(f32[2,512]{1,0:T(2,128)S(1)} %get-tuple-element.29.refs_0_.local_ref), channel_id=1, source_target_pairs={{0,2},{2,0},{1,3},{3,1},{4,6},{6,4},{5,7},{7,5},{8,10},{10,8},{9,1... | collective-permute-start | bytes 12296 | tf_op jit(solution)/shard_map/ppermute | solution.py:19
  81.8 2.2 %collective-permute-start.24 = (f32[2,512]{1,0:T(2,128)S(1)}, f32[2,512]{1,0:T(2,128)S(1)}, u32[]{:S(2)}, u32[]{:S(2)}) collective-permute-start(f32[2,512]{1,0:T(2,128)S(1)} %merge_stats.3.refs_0_), channel_id=1, source_target_pairs={{0,8},{4,12},{8,0},{12,4},{1,9},{5,13},{9,1},{13,5},{2,10},{6,14},... | collective-permute-start | bytes 12296 | tf_op jit(solution)/shard_map/ppermute | solution.py:19
  87.6 2.5 %collective-permute-done.26.refs_3_ = f32[2,512]{1,0:T(2,128)S(1)} collective-permute-done((f32[2,512]{1,0:T(2,128)S(1)}, f32[2,512]{1,0:T(2,128)S(1)}, u32[]{:S(2)}, u32[]{:S(2)}) %collective-permute-start.26) | collective-permute-done | bytes 4128 | tf_op jit(solution)/shard_map/ppermute | solution.py:19
  94.0 2.9 %collective-permute-start.30 = (bf16[64,1024]{1,0:T(8,128)(2,1)S(1)}, bf16[64,1024]{1,0:T(8,128)(2,1)S(1)}, u32[]{:S(2)}, u32[]{:S(2)}) collective-permute-start(bf16[64,1024]{1,0:T(8,128)(2,1)S(1)} %get-tuple-element.35), channel_id=1, source_target_pairs={{0,192},{64,128},{128,64},{192,0},{1,193},{65,129},{129,65},{193,1... | collective-permute-start | bytes 393224 | tf_op jit(solution)/shard_map/ppermute | solution.py:19
  96.8 3.8 %collective-permute-done.28.refs_0_ = bf16[64,1024]{1,0:T(8,128)(2,1)S(1)} collective-permute-done((bf16[64,1024]{1,0:T(8,128)(2,1)S(1)}, bf16[64,1024]{1,0:T(8,128)(2,1)S(1)}, u32[]{:S(2)}, u32[]{:S(2)}) %collective-permute-start.28) | collective-permute-done | bytes 131104 | tf_op jit(solution)/shard_map/ppermute | solution.py:19
  100.6 2.0 %collective-permute-done.30.refs_2_ = bf16[64,1024]{1,0:T(8,128)(2,1)S(1)} collective-permute-done((bf16[64,1024]{1,0:T(8,128)(2,1)S(1)}, bf16[64,1024]{1,0:T(8,128)(2,1)S(1)}, u32[]{:S(2)}, u32[]{:S(2)}) %collective-permute-start.30) | collective-permute-done | bytes 131104 | tf_op jit(solution)/shard_map/ppermute | solution.py:19
  102.8 2.5 %collective-permute-start.32 = (bf16[64,1024]{1,0:T(8,128)(2,1)S(1)}, bf16[64,1024]{1,0:T(8,128)(2,1)S(1)}, u32[]{:S(2)}, u32[]{:S(2)}) collective-permute-start(bf16[64,1024]{1,0:T(8,128)(2,1)S(1)} %total.5.a_ref), channel_id=1, source_target_pairs={{0,32},{16,48},{32,0},{48,16},{1,33},{17,49},{33,1},{49,17},{2,34}... | collective-permute-start | bytes 393224 | tf_op jit(solution)/shard_map/ppermute | solution.py:19
  106.2 2.9 %collective-permute-done.31.b_ref = bf16[64,1024]{1,0:T(8,128)(2,1)S(1)} collective-permute-done((bf16[64,1024]{1,0:T(8,128)(2,1)S(1)}, bf16[64,1024]{1,0:T(8,128)(2,1)S(1)}, u32[]{:S(2)}, u32[]{:S(2)}) %collective-permute-start.31) | collective-permute-done | bytes 131104 | tf_op jit(solution)/shard_map/ppermute | solution.py:19
  109.1 5.7 %collective-permute-done.32.c_ref = bf16[64,1024]{1,0:T(8,128)(2,1)S(1)} collective-permute-done((bf16[64,1024]{1,0:T(8,128)(2,1)S(1)}, bf16[64,1024]{1,0:T(8,128)(2,1)S(1)}, u32[]{:S(2)}, u32[]{:S(2)}) %collective-permute-start.32) | collective-permute-done | bytes 131104 | tf_op jit(solution)/shard_map/ppermute | solution.py:19
  114.8 3.1 %collective-permute-done.33.d_ref = bf16[64,1024]{1,0:T(8,128)(2,1)S(1)} collective-permute-done((bf16[64,1024]{1,0:T(8,128)(2,1)S(1)}, bf16[64,1024]{1,0:T(8,128)(2,1)S(1)}, u32[]{:S(2)}, u32[]{:S(2)}) %collective-permute-start.33) | collective-permute-done | bytes 131104 | tf_op jit(solution)/shard_map/ppermute | solution.py:19
  118.8 3.4 %collective-permute-start.36 = (bf16[64,1024]{1,0:T(8,128)(2,1)S(1)}, bf16[64,1024]{1,0:T(8,128)(2,1)S(1)}, u32[]{:S(2)}, u32[]{:S(2)}) collective-permute-start(bf16[64,1024]{1,0:T(8,128)(2,1)S(1)} %finish.1.refs_0_), channel_id=1, source_target_pairs={{0,192},{64,128},{128,64},{192,0},{1,193},{65,129},{129,65},{193,1... | collective-permute-start | bytes 393224 | tf_op jit(solution)/shard_map/ppermute | solution.py:19
  122.9 2.5 %collective-permute-done.34.refs_1_ = bf16[64,1024]{1,0:T(8,128)(2,1)S(1)} collective-permute-done((bf16[64,1024]{1,0:T(8,128)(2,1)S(1)}, bf16[64,1024]{1,0:T(8,128)(2,1)S(1)}, u32[]{:S(2)}, u32[]{:S(2)}) %collective-permute-start.34) | collective-permute-done | bytes 131104 | tf_op jit(solution)/shard_map/ppermute | solution.py:19
  (79 shorter events, 42.0 us)
Async XLA Ops:
  29.2 7.7 %collective-permute-start.6 = (bf16[4,1,64,1024]{3,2,1,0:T(8,128)(2,1)S(1)}, bf16[4,1,64,1024]{3,2,1,0:T(8,128)(2,1)S(1)}, u32[]{:S(2)}, u32[]{:S(2)}) collective-permute-start(bf16[4,1,64,1024]{3,2,1,0:T(8,128)(2,1)S(1)} %level_one_sums.5), channel_id=1, source_target_pairs={{0,1},{1,0},{2,3},{3,2},{4,5},{5,4},{6,7},{7,6},{8,9},{9,8},{10,11... | collective-permute-start | bytes 1572872 | tf_op jit(solution)/shard_map/ppermute | solution.py:19
  29.8 36.0 %collective-permute-start.16 = (bf16[256,1024]{1,0:T(8,128)(2,1)S(1)}, bf16[256,1024]{1,0:T(8,128)(2,1)S(1)}, u32[]{:S(2)}, u32[]{:S(2)}) collective-permute-start(bf16[256,1024]{1,0:T(8,128)(2,1)S(1)} %copy-done.3), channel_id=1, source_target_pairs={{0,1},{1,0},{2,3},{3,2},{4,5},{5,4},{6,7},{7,6},{8,9},{9,8},{10,11... | collective-permute-start | bytes 1572872 | tf_op jit(solution)/shard_map/ppermute | solution.py:19
  31.4 8.7 %collective-permute-start.12 = (bf16[64,1024]{1,0:T(8,128)(2,1)S(1)}, bf16[64,1024]{1,0:T(8,128)(2,1)S(1)}, u32[]{:S(2)}, u32[]{:S(2)}) collective-permute-start(bf16[64,1024]{1,0:T(8,128)(2,1)S(1)} %get-tuple-element.26), channel_id=1, source_target_pairs={{0,8},{4,12},{8,0},{12,4},{1,9},{5,13},{9,1},{13,5},{2,10},{6,14},... | collective-permute-start | bytes 393224 | tf_op jit(solution)/shard_map/ppermute | solution.py:19
  34.5 7.7 %collective-permute-start.13 = (bf16[64,1024]{1,0:T(8,128)(2,1)S(1)}, bf16[64,1024]{1,0:T(8,128)(2,1)S(1)}, u32[]{:S(2)}, u32[]{:S(2)}) collective-permute-start(bf16[64,1024]{1,0:T(8,128)(2,1)S(1)} %get-tuple-element.27), channel_id=1, source_target_pairs={{0,4},{4,0},{8,12},{12,8},{1,5},{5,1},{9,13},{13,9},{2,6},{6,2},{1... | collective-permute-start | bytes 393224 | tf_op jit(solution)/shard_map/ppermute | solution.py:19
  35.1 9.0 %collective-permute-start.14 = (bf16[64,1024]{1,0:T(8,128)(2,1)S(1)}, bf16[64,1024]{1,0:T(8,128)(2,1)S(1)}, u32[]{:S(2)}, u32[]{:S(2)}) collective-permute-start(bf16[64,1024]{1,0:T(8,128)(2,1)S(1)} %get-tuple-element.28), channel_id=1, source_target_pairs={{0,12},{4,8},{8,4},{12,0},{1,13},{5,9},{9,5},{13,1},{2,14},{6,10},... | collective-permute-start | bytes 393224 | tf_op jit(solution)/shard_map/ppermute | solution.py:19
  37.0 13.5 %collective-permute-start.7 = (bf16[64,1024]{1,0:T(8,128)(2,1)S(1)}, bf16[64,1024]{1,0:T(8,128)(2,1)S(1)}, u32[]{:S(2)}, u32[]{:S(2)}) collective-permute-start(bf16[64,1024]{1,0:T(8,128)(2,1)S(1)} %get-tuple-element.22), channel_id=1, source_target_pairs={{0,8},{4,12},{8,0},{12,4},{1,9},{5,13},{9,1},{13,5},{2,10},{6,14},... | collective-permute-start | bytes 393224 | tf_op jit(solution)/shard_map/ppermute | solution.py:19
  40.1 10.5 %collective-permute-start.8 = (bf16[64,1024]{1,0:T(8,128)(2,1)S(1)}, bf16[64,1024]{1,0:T(8,128)(2,1)S(1)}, u32[]{:S(2)}, u32[]{:S(2)}) collective-permute-start(bf16[64,1024]{1,0:T(8,128)(2,1)S(1)} %get-tuple-element.23), channel_id=1, source_target_pairs={{0,4},{4,0},{8,12},{12,8},{1,5},{5,1},{9,13},{13,9},{2,6},{6,2},{1... | collective-permute-start | bytes 393224 | tf_op jit(solution)/shard_map/ppermute | solution.py:19
  42.3 8.3 %collective-permute-start.9 = (bf16[64,1024]{1,0:T(8,128)(2,1)S(1)}, bf16[64,1024]{1,0:T(8,128)(2,1)S(1)}, u32[]{:S(2)}, u32[]{:S(2)}) collective-permute-start(bf16[64,1024]{1,0:T(8,128)(2,1)S(1)} %get-tuple-element.24), channel_id=1, source_target_pairs={{0,12},{4,8},{8,4},{12,0},{1,13},{5,9},{9,5},{13,1},{2,14},{6,10},... | collective-permute-start | bytes 393224 | tf_op jit(solution)/shard_map/ppermute | solution.py:19
  44.2 10.7 %collective-permute-start.15 = (bf16[64,1024]{1,0:T(8,128)(2,1)S(1)}, bf16[64,1024]{1,0:T(8,128)(2,1)S(1)}, u32[]{:S(2)}, u32[]{:S(2)}) collective-permute-start(bf16[64,1024]{1,0:T(8,128)(2,1)S(1)} %total.4.part_ref), channel_id=1, source_target_pairs={{0,2},{2,0},{1,3},{3,1},{4,6},{6,4},{5,7},{7,5},{8,10},{10,8},{9,1... | collective-permute-start | bytes 393224 | tf_op jit(solution)/shard_map/ppermute | solution.py:19
  50.6 11.3 %collective-permute-start.10 = (bf16[64,1024]{1,0:T(8,128)(2,1)S(1)}, bf16[64,1024]{1,0:T(8,128)(2,1)S(1)}, u32[]{:S(2)}, u32[]{:S(2)}) collective-permute-start(bf16[64,1024]{1,0:T(8,128)(2,1)S(1)} %total.3.part_ref), channel_id=1, source_target_pairs={{0,2},{2,0},{1,3},{3,1},{4,6},{6,4},{5,7},{7,5},{8,10},{10,8},{9,1... | collective-permute-start | bytes 393224 | tf_op jit(solution)/shard_map/ppermute | solution.py:19
  55.2 11.1 %collective-permute-start.20 = (bf16[64,1024]{1,0:T(8,128)(2,1)S(1)}, bf16[64,1024]{1,0:T(8,128)(2,1)S(1)}, u32[]{:S(2)}, u32[]{:S(2)}) collective-permute-start(bf16[64,1024]{1,0:T(8,128)(2,1)S(1)} %new_rows.3.b_ref.refs_4_), channel_id=1, source_target_pairs={{0,8},{4,12},{8,0},{12,4},{1,9},{5,13},{9,1},{13,5},{2,10},{6,14},... | collective-permute-start | bytes 393224 | tf_op jit(solution)/shard_map/ppermute | solution.py:19
  61.2 6.4 %collective-permute-start.21 = (bf16[64,1024]{1,0:T(8,128)(2,1)S(1)}, bf16[64,1024]{1,0:T(8,128)(2,1)S(1)}, u32[]{:S(2)}, u32[]{:S(2)}) collective-permute-start(bf16[64,1024]{1,0:T(8,128)(2,1)S(1)} %new_rows.3.b_ref.refs_4_), channel_id=1, source_target_pairs={{0,4},{4,0},{8,12},{12,8},{1,5},{5,1},{9,13},{13,9},{2,6},{6,2},{1... | collective-permute-start | bytes 393224 | tf_op jit(solution)/shard_map/ppermute | solution.py:19
  61.8 8.9 %collective-permute-start.22 = (bf16[64,1024]{1,0:T(8,128)(2,1)S(1)}, bf16[64,1024]{1,0:T(8,128)(2,1)S(1)}, u32[]{:S(2)}, u32[]{:S(2)}) collective-permute-start(bf16[64,1024]{1,0:T(8,128)(2,1)S(1)} %new_rows.3.b_ref.refs_4_), channel_id=1, source_target_pairs={{0,12},{4,8},{8,4},{12,0},{1,13},{5,9},{9,5},{13,1},{2,14},{6,10},... | collective-permute-start | bytes 393224 | tf_op jit(solution)/shard_map/ppermute | solution.py:19
  62.2 8.5 %collective-permute-start.17 = (bf16[64,1024]{1,0:T(8,128)(2,1)S(1)}, bf16[64,1024]{1,0:T(8,128)(2,1)S(1)}, u32[]{:S(2)}, u32[]{:S(2)}) collective-permute-start(bf16[64,1024]{1,0:T(8,128)(2,1)S(1)} %new_rows.2.a_ref.refs_0_), channel_id=1, source_target_pairs={{0,8},{4,12},{8,0},{12,4},{1,9},{5,13},{9,1},{13,5},{2,10},{6,14},... | collective-permute-start | bytes 393224 | tf_op jit(solution)/shard_map/ppermute | solution.py:19
  73.6 8.2 %collective-permute-start.23 = (f32[2,512]{1,0:T(2,128)S(1)}, f32[2,512]{1,0:T(2,128)S(1)}, u32[]{:S(2)}, u32[]{:S(2)}) collective-permute-start(f32[2,512]{1,0:T(2,128)S(1)} %get-tuple-element.29.refs_0_.local_ref), channel_id=1, source_target_pairs={{0,2},{2,0},{1,3},{3,1},{4,6},{6,4},{5,7},{7,5},{8,10},{10,8},{9,1... | collective-permute-start | bytes 12296 | tf_op jit(solution)/shard_map/ppermute | solution.py:19
  92.7 7.9 %collective-permute-start.28 = (bf16[64,1024]{1,0:T(8,128)(2,1)S(1)}, bf16[64,1024]{1,0:T(8,128)(2,1)S(1)}, u32[]{:S(2)}, u32[]{:S(2)}) collective-permute-start(bf16[64,1024]{1,0:T(8,128)(2,1)S(1)} %get-tuple-element.33), channel_id=1, source_target_pairs={{0,128},{64,192},{128,0},{192,64},{1,129},{65,193},{129,1},{193,65... | collective-permute-start | bytes 393224 | tf_op jit(solution)/shard_map/ppermute | solution.py:19
  93.4 7.2 %collective-permute-start.29 = (bf16[64,1024]{1,0:T(8,128)(2,1)S(1)}, bf16[64,1024]{1,0:T(8,128)(2,1)S(1)}, u32[]{:S(2)}, u32[]{:S(2)}) collective-permute-start(bf16[64,1024]{1,0:T(8,128)(2,1)S(1)} %get-tuple-element.34), channel_id=1, source_target_pairs={{0,64},{64,0},{128,192},{192,128},{1,65},{65,1},{129,193},{193,129... | collective-permute-start | bytes 393224 | tf_op jit(solution)/shard_map/ppermute | solution.py:19
  94.0 8.6 %collective-permute-start.30 = (bf16[64,1024]{1,0:T(8,128)(2,1)S(1)}, bf16[64,1024]{1,0:T(8,128)(2,1)S(1)}, u32[]{:S(2)}, u32[]{:S(2)}) collective-permute-start(bf16[64,1024]{1,0:T(8,128)(2,1)S(1)} %get-tuple-element.35), channel_id=1, source_target_pairs={{0,192},{64,128},{128,64},{192,0},{1,193},{65,129},{129,65},{193,1... | collective-permute-start | bytes 393224 | tf_op jit(solution)/shard_map/ppermute | solution.py:19
  102.7 6.4 %collective-permute-start.31 = (bf16[64,1024]{1,0:T(8,128)(2,1)S(1)}, bf16[64,1024]{1,0:T(8,128)(2,1)S(1)}, u32[]{:S(2)}, u32[]{:S(2)}) collective-permute-start(bf16[64,1024]{1,0:T(8,128)(2,1)S(1)} %total.5.a_ref), channel_id=1, source_target_pairs={{0,16},{16,0},{32,48},{48,32},{1,17},{17,1},{33,49},{49,33},{2,18}... | collective-permute-start | bytes 393224 | tf_op jit(solution)/shard_map/ppermute | solution.py:19
  102.8 12.0 %collective-permute-start.32 = (bf16[64,1024]{1,0:T(8,128)(2,1)S(1)}, bf16[64,1024]{1,0:T(8,128)(2,1)S(1)}, u32[]{:S(2)}, u32[]{:S(2)}) collective-permute-start(bf16[64,1024]{1,0:T(8,128)(2,1)S(1)} %total.5.a_ref), channel_id=1, source_target_pairs={{0,32},{16,48},{32,0},{48,16},{1,33},{17,49},{33,1},{49,17},{2,34}... | collective-permute-start | bytes 393224 | tf_op jit(solution)/shard_map/ppermute | solution.py:19
  105.3 12.5 %collective-permute-start.33 = (bf16[64,1024]{1,0:T(8,128)(2,1)S(1)}, bf16[64,1024]{1,0:T(8,128)(2,1)S(1)}, u32[]{:S(2)}, u32[]{:S(2)}) collective-permute-start(bf16[64,1024]{1,0:T(8,128)(2,1)S(1)} %total.5.a_ref), channel_id=1, source_target_pairs={{0,48},{16,32},{32,16},{48,0},{1,49},{17,33},{33,17},{49,1},{2,50}... | collective-permute-start | bytes 393224 | tf_op jit(solution)/shard_map/ppermute | solution.py:19
  118.0 7.4 %collective-permute-start.34 = (bf16[64,1024]{1,0:T(8,128)(2,1)S(1)}, bf16[64,1024]{1,0:T(8,128)(2,1)S(1)}, u32[]{:S(2)}, u32[]{:S(2)}) collective-permute-start(bf16[64,1024]{1,0:T(8,128)(2,1)S(1)} %finish.1.refs_0_), channel_id=1, source_target_pairs={{0,128},{64,192},{128,0},{192,64},{1,129},{65,193},{129,1},{193,65... | collective-permute-start | bytes 393224 | tf_op jit(solution)/shard_map/ppermute | solution.py:19
  118.2 7.1 %collective-permute-start.35 = (bf16[64,1024]{1,0:T(8,128)(2,1)S(1)}, bf16[64,1024]{1,0:T(8,128)(2,1)S(1)}, u32[]{:S(2)}, u32[]{:S(2)}) collective-permute-start(bf16[64,1024]{1,0:T(8,128)(2,1)S(1)} %finish.1.refs_0_), channel_id=1, source_target_pairs={{0,64},{64,0},{128,192},{192,128},{1,65},{65,1},{129,193},{193,129... | collective-permute-start | bytes 393224 | tf_op jit(solution)/shard_map/ppermute | solution.py:19
  118.8 7.9 %collective-permute-start.36 = (bf16[64,1024]{1,0:T(8,128)(2,1)S(1)}, bf16[64,1024]{1,0:T(8,128)(2,1)S(1)}, u32[]{:S(2)}, u32[]{:S(2)}) collective-permute-start(bf16[64,1024]{1,0:T(8,128)(2,1)S(1)} %finish.1.refs_0_), channel_id=1, source_target_pairs={{0,192},{64,128},{128,64},{192,0},{1,193},{65,129},{129,65},{193,1... | collective-permute-start | bytes 393224 | tf_op jit(solution)/shard_map/ppermute | solution.py:19
  (17 other events, 84.0 us)

commit v6 on v4

--- a/solution.py
+++ b/solution.py
@@ -96,13 +96,13 @@
     held, depth = center.shape
     count = points.shape[0]
     return kernel_call(
-        functools.partial(powers_kernel, scale, 512),
+        functools.partial(powers_kernel, scale, 1024),
         "level_one_powers",
         2 * held * count * depth,
         [VMEM] * 2,
         [VMEM] * 2,
         [shape((held, count)), shape((2, count), jnp.float32)],
-        vmem=20,
+        vmem=28,
     )(center, points)
 
 

time: 128 us -> 128 us (level)
    unnamed x8 -> x6, local copies, waits for them, and re-layouts: 3.78 us -> 3.78 us
where the time goes in v6:
time: 128 us
  starting transfers between devices  65 us (51%)
  waiting for transfers between devices  42.1 us (33%)
  Pallas kernels  15.8 us (12%)
  local copies, waits for them, and re-layouts  3.78 us (3%)
    ppermute x37, starting transfers between devices, swapped(): lax.ppermute(value, axis, [(i, i ^ mask) for i in range(lax.axis_size(axi...  65 us
    ppermute x37, waiting for transfers between devices, swapped(): lax.ppermute(value, axis, [(i, i ^ mask) for i in range(lax.axis_size(axi...  42.1 us
    pallas_call x1, Pallas kernels, level_one_powers(): kernel_call(functools.partial(powers_kernel, scale, 1024), 'level_one_pow...  5.95 us
    pallas_call x4, Pallas kernels, level_one_sums(): kernel_call(functools.partial(sums_kernel, len(stats), other_core, half),...  4.98 us
    unnamed x6, local copies, waits for them, and re-layouts  3.78 us
  transfers between devices with their start and end apart: 37, of which 22 were waited for; matrix products, arithmetic and copies ran while one was open for 0% of the time, Pallas kernels for 5%

profile of v6, /device:TPU:32, one launch (start us, length us, event | category | flops | bytes accessed | tf_op | source)
XLA Modules:
  0.0 127.7 jit_solution(112310847107079931)
XLA Ops:
  0.6 2.2 %copy-done = bf16[2048,1024]{1,0:T(8,128)(2,1)S(1)} copy-done((bf16[2048,1024]{1,0:T(8,128)(2,1)S(1)}, bf16[2048,1024]{1,0:T(8,128)(2,1)}, u32[]{:S(2)}) %copy-start) | copy-done | bytes 4194328
  4.4 5.9 %level_one_powers.1 = (bf16[1024,2048]{1,0:T(8,128)(2,1)S(1)}, f32[2,2048]{1,0:T(2,128)S(1)}) custom-call(bf16[1024,1024]{1,0:T(8,128)(2,1)S(1)} %copy-done.1, bf16[2048,1024]{1,0:T(8,128)(2,1)S(1)} %copy-done), custom_call_target="tpu_custom_call" | custom-call | flops 4294967296 | bytes 1024 | tf_op jit(solution)/shard_map/level_one_powers/pallas_call | solution.py:98
  10.4 3.3 %collective-permute-start = (f32[2,2048]{1,0:T(2,128)S(1)}, f32[2,2048]{1,0:T(2,128)S(1)}, u32[]{:S(2)}, u32[]{:S(2)}) collective-permute-start(f32[2,2048]{1,0:T(2,128)S(1)} %get-tuple-element.19.refs_0_.local_ref), channel_id=1, source_target_pairs={{0,128},{64,192},{128,0},{192,64},{1,129},{65,193},{129,1},{193,65... | collective-permute-start | bytes 49160 | tf_op jit(solution)/shard_map/ppermute | solution.py:19
  17.4 1.9 %collective-permute-done.2.refs_3_ = f32[2,2048]{1,0:T(2,128)S(1)} collective-permute-done((f32[2,2048]{1,0:T(2,128)S(1)}, f32[2,2048]{1,0:T(2,128)S(1)}, u32[]{:S(2)}, u32[]{:S(2)}) %collective-permute-start.2) | collective-permute-done | bytes 16416 | tf_op jit(solution)/shard_map/ppermute | solution.py:19
  19.3 2.0 %collective-permute-start.3 = (f32[2,2048]{1,0:T(2,128)S(1)}, f32[2,2048]{1,0:T(2,128)S(1)}, u32[]{:S(2)}, u32[]{:S(2)}) collective-permute-start(f32[2,2048]{1,0:T(2,128)S(1)} %merge_stats.2.refs_0_), channel_id=1, source_target_pairs={{0,48},{16,32},{32,16},{48,0},{1,49},{17,33},{33,17},{49,1},{2,50}... | collective-permute-start | bytes 49160 | tf_op jit(solution)/shard_map/ppermute | solution.py:19
  24.1 1.8 %collective-permute-done.4.refs_2_ = f32[2,2048]{1,0:T(2,128)S(1)} collective-permute-done((f32[2,2048]{1,0:T(2,128)S(1)}, f32[2,2048]{1,0:T(2,128)S(1)}, u32[]{:S(2)}, u32[]{:S(2)}) %collective-permute-start.4) | collective-permute-done | bytes 16416 | tf_op jit(solution)/shard_map/ppermute | solution.py:19
  31.4 3.1 %collective-permute-start.12 = (bf16[64,1024]{1,0:T(8,128)(2,1)S(1)}, bf16[64,1024]{1,0:T(8,128)(2,1)S(1)}, u32[]{:S(2)}, u32[]{:S(2)}) collective-permute-start(bf16[64,1024]{1,0:T(8,128)(2,1)S(1)} %get-tuple-element.26), channel_id=1, source_target_pairs={{0,8},{4,12},{8,0},{12,4},{1,9},{5,13},{9,1},{13,5},{2,10},{6,14},... | collective-permute-start | bytes 393224 | tf_op jit(solution)/shard_map/ppermute | solution.py:19
  37.0 3.0 %collective-permute-start.7 = (bf16[64,1024]{1,0:T(8,128)(2,1)S(1)}, bf16[64,1024]{1,0:T(8,128)(2,1)S(1)}, u32[]{:S(2)}, u32[]{:S(2)}) collective-permute-start(bf16[64,1024]{1,0:T(8,128)(2,1)S(1)} %get-tuple-element.22), channel_id=1, source_target_pairs={{0,8},{4,12},{8,0},{12,4},{1,9},{5,13},{9,1},{13,5},{2,10},{6,14},... | collective-permute-start | bytes 393224 | tf_op jit(solution)/shard_map/ppermute | solution.py:19
  44.1 6.4 %collective-permute-start.15 = (bf16[64,1024]{1,0:T(8,128)(2,1)S(1)}, bf16[64,1024]{1,0:T(8,128)(2,1)S(1)}, u32[]{:S(2)}, u32[]{:S(2)}) collective-permute-start(bf16[64,1024]{1,0:T(8,128)(2,1)S(1)} %total.4.part_ref), channel_id=1, source_target_pairs={{0,2},{2,0},{1,3},{3,1},{4,6},{6,4},{5,7},{7,5},{8,10},{10,8},{9,1... | collective-permute-start | bytes 393224 | tf_op jit(solution)/shard_map/ppermute | solution.py:19
  50.5 4.3 %collective-permute-start.10 = (bf16[64,1024]{1,0:T(8,128)(2,1)S(1)}, bf16[64,1024]{1,0:T(8,128)(2,1)S(1)}, u32[]{:S(2)}, u32[]{:S(2)}) collective-permute-start(bf16[64,1024]{1,0:T(8,128)(2,1)S(1)} %total.3.part_ref), channel_id=1, source_target_pairs={{0,2},{2,0},{1,3},{3,1},{4,6},{6,4},{5,7},{7,5},{8,10},{10,8},{9,1... | collective-permute-start | bytes 393224 | tf_op jit(solution)/shard_map/ppermute | solution.py:19
  55.1 6.0 %collective-permute-start.20 = (bf16[64,1024]{1,0:T(8,128)(2,1)S(1)}, bf16[64,1024]{1,0:T(8,128)(2,1)S(1)}, u32[]{:S(2)}, u32[]{:S(2)}) collective-permute-start(bf16[64,1024]{1,0:T(8,128)(2,1)S(1)} %new_rows.3.b_ref.refs_4_), channel_id=1, source_target_pairs={{0,8},{4,12},{8,0},{12,4},{1,9},{5,13},{9,1},{13,5},{2,10},{6,14},... | collective-permute-start | bytes 393224 | tf_op jit(solution)/shard_map/ppermute | solution.py:19
  62.1 3.5 %collective-permute-start.17 = (bf16[64,1024]{1,0:T(8,128)(2,1)S(1)}, bf16[64,1024]{1,0:T(8,128)(2,1)S(1)}, u32[]{:S(2)}, u32[]{:S(2)}) collective-permute-start(bf16[64,1024]{1,0:T(8,128)(2,1)S(1)} %new_rows.2.a_ref.refs_0_), channel_id=1, source_target_pairs={{0,8},{4,12},{8,0},{12,4},{1,9},{5,13},{9,1},{13,5},{2,10},{6,14},... | collective-permute-start | bytes 393224 | tf_op jit(solution)/shard_map/ppermute | solution.py:19
  67.6 3.1 %collective-permute-done.22.refs_7_ = bf16[64,1024]{1,0:T(8,128)(2,1)S(1)} collective-permute-done((bf16[64,1024]{1,0:T(8,128)(2,1)S(1)}, bf16[64,1024]{1,0:T(8,128)(2,1)S(1)}, u32[]{:S(2)}, u32[]{:S(2)}) %collective-permute-start.22) | collective-permute-done | bytes 131104 | tf_op jit(solution)/shard_map/ppermute | solution.py:19
  73.5 2.3 %collective-permute-start.23 = (f32[2,512]{1,0:T(2,128)S(1)}, f32[2,512]{1,0:T(2,128)S(1)}, u32[]{:S(2)}, u32[]{:S(2)}) collective-permute-start(f32[2,512]{1,0:T(2,128)S(1)} %get-tuple-element.29.refs_0_.local_ref), channel_id=1, source_target_pairs={{0,8},{4,12},{8,0},{12,4},{1,9},{5,13},{9,1},{13,5},{2,10},{6,14},... | collective-permute-start | bytes 12296 | tf_op jit(solution)/shard_map/ppermute | solution.py:19
  81.2 7.2 %collective-permute-start.26 = (f32[2,512]{1,0:T(2,128)S(1)}, f32[2,512]{1,0:T(2,128)S(1)}, u32[]{:S(2)}, u32[]{:S(2)}) collective-permute-start(f32[2,512]{1,0:T(2,128)S(1)} %merge_stats.3.refs_0_), channel_id=1, source_target_pairs={{0,2},{2,0},{1,3},{3,1},{4,6},{6,4},{5,7},{7,5},{8,10},{10,8},{9,1... | collective-permute-start | bytes 12296 | tf_op jit(solution)/shard_map/ppermute | solution.py:19
  94.0 2.9 %collective-permute-start.30 = (bf16[64,1024]{1,0:T(8,128)(2,1)S(1)}, bf16[64,1024]{1,0:T(8,128)(2,1)S(1)}, u32[]{:S(2)}, u32[]{:S(2)}) collective-permute-start(bf16[64,1024]{1,0:T(8,128)(2,1)S(1)} %get-tuple-element.35), channel_id=1, source_target_pairs={{0,192},{64,128},{128,64},{192,0},{1,193},{65,129},{129,65},{193,1... | collective-permute-start | bytes 393224 | tf_op jit(solution)/shard_map/ppermute | solution.py:19
  96.8 3.8 %collective-permute-done.28.refs_0_ = bf16[64,1024]{1,0:T(8,128)(2,1)S(1)} collective-permute-done((bf16[64,1024]{1,0:T(8,128)(2,1)S(1)}, bf16[64,1024]{1,0:T(8,128)(2,1)S(1)}, u32[]{:S(2)}, u32[]{:S(2)}) %collective-permute-start.28) | collective-permute-done | bytes 131104 | tf_op jit(solution)/shard_map/ppermute | solution.py:19
  100.6 2.0 %collective-permute-done.30.refs_2_ = bf16[64,1024]{1,0:T(8,128)(2,1)S(1)} collective-permute-done((bf16[64,1024]{1,0:T(8,128)(2,1)S(1)}, bf16[64,1024]{1,0:T(8,128)(2,1)S(1)}, u32[]{:S(2)}, u32[]{:S(2)}) %collective-permute-start.30) | collective-permute-done | bytes 131104 | tf_op jit(solution)/shard_map/ppermute | solution.py:19
  102.7 2.5 %collective-permute-start.32 = (bf16[64,1024]{1,0:T(8,128)(2,1)S(1)}, bf16[64,1024]{1,0:T(8,128)(2,1)S(1)}, u32[]{:S(2)}, u32[]{:S(2)}) collective-permute-start(bf16[64,1024]{1,0:T(8,128)(2,1)S(1)} %total.5.a_ref), channel_id=1, source_target_pairs={{0,32},{16,48},{32,0},{48,16},{1,33},{17,49},{33,1},{49,17},{2,34}... | collective-permute-start | bytes 393224 | tf_op jit(solution)/shard_map/ppermute | solution.py:19
  106.2 2.9 %collective-permute-done.31.b_ref = bf16[64,1024]{1,0:T(8,128)(2,1)S(1)} collective-permute-done((bf16[64,1024]{1,0:T(8,128)(2,1)S(1)}, bf16[64,1024]{1,0:T(8,128)(2,1)S(1)}, u32[]{:S(2)}, u32[]{:S(2)}) %collective-permute-start.31) | collective-permute-done | bytes 131104 | tf_op jit(solution)/shard_map/ppermute | solution.py:19
  109.1 5.6 %collective-permute-done.32.c_ref = bf16[64,1024]{1,0:T(8,128)(2,1)S(1)} collective-permute-done((bf16[64,1024]{1,0:T(8,128)(2,1)S(1)}, bf16[64,1024]{1,0:T(8,128)(2,1)S(1)}, u32[]{:S(2)}, u32[]{:S(2)}) %collective-permute-start.32) | collective-permute-done | bytes 131104 | tf_op jit(solution)/shard_map/ppermute | solution.py:19
  114.7 3.1 %collective-permute-done.33.d_ref = bf16[64,1024]{1,0:T(8,128)(2,1)S(1)} collective-permute-done((bf16[64,1024]{1,0:T(8,128)(2,1)S(1)}, bf16[64,1024]{1,0:T(8,128)(2,1)S(1)}, u32[]{:S(2)}, u32[]{:S(2)}) %collective-permute-start.33) | collective-permute-done | bytes 131104 | tf_op jit(solution)/shard_map/ppermute | solution.py:19
  118.7 3.4 %collective-permute-start.36 = (bf16[64,1024]{1,0:T(8,128)(2,1)S(1)}, bf16[64,1024]{1,0:T(8,128)(2,1)S(1)}, u32[]{:S(2)}, u32[]{:S(2)}) collective-permute-start(bf16[64,1024]{1,0:T(8,128)(2,1)S(1)} %finish.1.refs_0_), channel_id=1, source_target_pairs={{0,192},{64,128},{128,64},{192,0},{1,193},{65,129},{129,65},{193,1... | collective-permute-start | bytes 393224 | tf_op jit(solution)/shard_map/ppermute | solution.py:19
  122.8 2.5 %collective-permute-done.34.refs_1_ = bf16[64,1024]{1,0:T(8,128)(2,1)S(1)} collective-permute-done((bf16[64,1024]{1,0:T(8,128)(2,1)S(1)}, bf16[64,1024]{1,0:T(8,128)(2,1)S(1)}, u32[]{:S(2)}, u32[]{:S(2)}) %collective-permute-start.34) | collective-permute-done | bytes 131104 | tf_op jit(solution)/shard_map/ppermute | solution.py:19
  (77 shorter events, 42.0 us)
Async XLA Ops:
  29.1 7.8 %collective-permute-start.6 = (bf16[4,1,64,1024]{3,2,1,0:T(8,128)(2,1)S(1)}, bf16[4,1,64,1024]{3,2,1,0:T(8,128)(2,1)S(1)}, u32[]{:S(2)}, u32[]{:S(2)}) collective-permute-start(bf16[4,1,64,1024]{3,2,1,0:T(8,128)(2,1)S(1)} %level_one_sums.5), channel_id=1, source_target_pairs={{0,1},{1,0},{2,3},{3,2},{4,5},{5,4},{6,7},{7,6},{8,9},{9,8},{10,11... | collective-permute-start | bytes 1572872 | tf_op jit(solution)/shard_map/ppermute | solution.py:19
  29.7 36.0 %collective-permute-start.16 = (bf16[256,1024]{1,0:T(8,128)(2,1)S(1)}, bf16[256,1024]{1,0:T(8,128)(2,1)S(1)}, u32[]{:S(2)}, u32[]{:S(2)}) collective-permute-start(bf16[256,1024]{1,0:T(8,128)(2,1)S(1)} %copy-done.2), channel_id=1, source_target_pairs={{0,1},{1,0},{2,3},{3,2},{4,5},{5,4},{6,7},{7,6},{8,9},{9,8},{10,11... | collective-permute-start | bytes 1572872 | tf_op jit(solution)/shard_map/ppermute | solution.py:19
  31.4 8.7 %collective-permute-start.12 = (bf16[64,1024]{1,0:T(8,128)(2,1)S(1)}, bf16[64,1024]{1,0:T(8,128)(2,1)S(1)}, u32[]{:S(2)}, u32[]{:S(2)}) collective-permute-start(bf16[64,1024]{1,0:T(8,128)(2,1)S(1)} %get-tuple-element.26), channel_id=1, source_target_pairs={{0,8},{4,12},{8,0},{12,4},{1,9},{5,13},{9,1},{13,5},{2,10},{6,14},... | collective-permute-start | bytes 393224 | tf_op jit(solution)/shard_map/ppermute | solution.py:19
  34.5 7.7 %collective-permute-start.13 = (bf16[64,1024]{1,0:T(8,128)(2,1)S(1)}, bf16[64,1024]{1,0:T(8,128)(2,1)S(1)}, u32[]{:S(2)}, u32[]{:S(2)}) collective-permute-start(bf16[64,1024]{1,0:T(8,128)(2,1)S(1)} %get-tuple-element.27), channel_id=1, source_target_pairs={{0,4},{4,0},{8,12},{12,8},{1,5},{5,1},{9,13},{13,9},{2,6},{6,2},{1... | collective-permute-start | bytes 393224 | tf_op jit(solution)/shard_map/ppermute | solution.py:19
  35.1 8.9 %collective-permute-start.14 = (bf16[64,1024]{1,0:T(8,128)(2,1)S(1)}, bf16[64,1024]{1,0:T(8,128)(2,1)S(1)}, u32[]{:S(2)}, u32[]{:S(2)}) collective-permute-start(bf16[64,1024]{1,0:T(8,128)(2,1)S(1)} %get-tuple-element.28), channel_id=1, source_target_pairs={{0,12},{4,8},{8,4},{12,0},{1,13},{5,9},{9,5},{13,1},{2,14},{6,10},... | collective-permute-start | bytes 393224 | tf_op jit(solution)/shard_map/ppermute | solution.py:19
  37.0 13.4 %collective-permute-start.7 = (bf16[64,1024]{1,0:T(8,128)(2,1)S(1)}, bf16[64,1024]{1,0:T(8,128)(2,1)S(1)}, u32[]{:S(2)}, u32[]{:S(2)}) collective-permute-start(bf16[64,1024]{1,0:T(8,128)(2,1)S(1)} %get-tuple-element.22), channel_id=1, source_target_pairs={{0,8},{4,12},{8,0},{12,4},{1,9},{5,13},{9,1},{13,5},{2,10},{6,14},... | collective-permute-start | bytes 393224 | tf_op jit(solution)/shard_map/ppermute | solution.py:19
  40.0 10.4 %collective-permute-start.8 = (bf16[64,1024]{1,0:T(8,128)(2,1)S(1)}, bf16[64,1024]{1,0:T(8,128)(2,1)S(1)}, u32[]{:S(2)}, u32[]{:S(2)}) collective-permute-start(bf16[64,1024]{1,0:T(8,128)(2,1)S(1)} %get-tuple-element.23), channel_id=1, source_target_pairs={{0,4},{4,0},{8,12},{12,8},{1,5},{5,1},{9,13},{13,9},{2,6},{6,2},{1... | collective-permute-start | bytes 393224 | tf_op jit(solution)/shard_map/ppermute | solution.py:19
  42.2 8.3 %collective-permute-start.9 = (bf16[64,1024]{1,0:T(8,128)(2,1)S(1)}, bf16[64,1024]{1,0:T(8,128)(2,1)S(1)}, u32[]{:S(2)}, u32[]{:S(2)}) collective-permute-start(bf16[64,1024]{1,0:T(8,128)(2,1)S(1)} %get-tuple-element.24), channel_id=1, source_target_pairs={{0,12},{4,8},{8,4},{12,0},{1,13},{5,9},{9,5},{13,1},{2,14},{6,10},... | collective-permute-start | bytes 393224 | tf_op jit(solution)/shard_map/ppermute | solution.py:19
  44.1 10.7 %collective-permute-start.15 = (bf16[64,1024]{1,0:T(8,128)(2,1)S(1)}, bf16[64,1024]{1,0:T(8,128)(2,1)S(1)}, u32[]{:S(2)}, u32[]{:S(2)}) collective-permute-start(bf16[64,1024]{1,0:T(8,128)(2,1)S(1)} %total.4.part_ref), channel_id=1, source_target_pairs={{0,2},{2,0},{1,3},{3,1},{4,6},{6,4},{5,7},{7,5},{8,10},{10,8},{9,1... | collective-permute-start | bytes 393224 | tf_op jit(solution)/shard_map/ppermute | solution.py:19
  50.5 11.3 %collective-permute-start.10 = (bf16[64,1024]{1,0:T(8,128)(2,1)S(1)}, bf16[64,1024]{1,0:T(8,128)(2,1)S(1)}, u32[]{:S(2)}, u32[]{:S(2)}) collective-permute-start(bf16[64,1024]{1,0:T(8,128)(2,1)S(1)} %total.3.part_ref), channel_id=1, source_target_pairs={{0,2},{2,0},{1,3},{3,1},{4,6},{6,4},{5,7},{7,5},{8,10},{10,8},{9,1... | collective-permute-start | bytes 393224 | tf_op jit(solution)/shard_map/ppermute | solution.py:19
  55.1 11.1 %collective-permute-start.20 = (bf16[64,1024]{1,0:T(8,128)(2,1)S(1)}, bf16[64,1024]{1,0:T(8,128)(2,1)S(1)}, u32[]{:S(2)}, u32[]{:S(2)}) collective-permute-start(bf16[64,1024]{1,0:T(8,128)(2,1)S(1)} %new_rows.3.b_ref.refs_4_), channel_id=1, source_target_pairs={{0,8},{4,12},{8,0},{12,4},{1,9},{5,13},{9,1},{13,5},{2,10},{6,14},... | collective-permute-start | bytes 393224 | tf_op jit(solution)/shard_map/ppermute | solution.py:19
  61.1 6.4 %collective-permute-start.21 = (bf16[64,1024]{1,0:T(8,128)(2,1)S(1)}, bf16[64,1024]{1,0:T(8,128)(2,1)S(1)}, u32[]{:S(2)}, u32[]{:S(2)}) collective-permute-start(bf16[64,1024]{1,0:T(8,128)(2,1)S(1)} %new_rows.3.b_ref.refs_4_), channel_id=1, source_target_pairs={{0,4},{4,0},{8,12},{12,8},{1,5},{5,1},{9,13},{13,9},{2,6},{6,2},{1... | collective-permute-start | bytes 393224 | tf_op jit(solution)/shard_map/ppermute | solution.py:19
  61.7 8.9 %collective-permute-start.22 = (bf16[64,1024]{1,0:T(8,128)(2,1)S(1)}, bf16[64,1024]{1,0:T(8,128)(2,1)S(1)}, u32[]{:S(2)}, u32[]{:S(2)}) collective-permute-start(bf16[64,1024]{1,0:T(8,128)(2,1)S(1)} %new_rows.3.b_ref.refs_4_), channel_id=1, source_target_pairs={{0,12},{4,8},{8,4},{12,0},{1,13},{5,9},{9,5},{13,1},{2,14},{6,10},... | collective-permute-start | bytes 393224 | tf_op jit(solution)/shard_map/ppermute | solution.py:19
  62.1 8.5 %collective-permute-start.17 = (bf16[64,1024]{1,0:T(8,128)(2,1)S(1)}, bf16[64,1024]{1,0:T(8,128)(2,1)S(1)}, u32[]{:S(2)}, u32[]{:S(2)}) collective-permute-start(bf16[64,1024]{1,0:T(8,128)(2,1)S(1)} %new_rows.2.a_ref.refs_0_), channel_id=1, source_target_pairs={{0,8},{4,12},{8,0},{12,4},{1,9},{5,13},{9,1},{13,5},{2,10},{6,14},... | collective-permute-start | bytes 393224 | tf_op jit(solution)/shard_map/ppermute | solution.py:19
  81.2 8.8 %collective-permute-start.26 = (f32[2,512]{1,0:T(2,128)S(1)}, f32[2,512]{1,0:T(2,128)S(1)}, u32[]{:S(2)}, u32[]{:S(2)}) collective-permute-start(f32[2,512]{1,0:T(2,128)S(1)} %merge_stats.3.refs_0_), channel_id=1, source_target_pairs={{0,2},{2,0},{1,3},{3,1},{4,6},{6,4},{5,7},{7,5},{8,10},{10,8},{9,1... | collective-permute-start | bytes 12296 | tf_op jit(solution)/shard_map/ppermute | solution.py:19
  92.6 7.9 %collective-permute-start.28 = (bf16[64,1024]{1,0:T(8,128)(2,1)S(1)}, bf16[64,1024]{1,0:T(8,128)(2,1)S(1)}, u32[]{:S(2)}, u32[]{:S(2)}) collective-permute-start(bf16[64,1024]{1,0:T(8,128)(2,1)S(1)} %get-tuple-element.33), channel_id=1, source_target_pairs={{0,128},{64,192},{128,0},{192,64},{1,129},{65,193},{129,1},{193,65... | collective-permute-start | bytes 393224 | tf_op jit(solution)/shard_map/ppermute | solution.py:19
  93.4 7.2 %collective-permute-start.29 = (bf16[64,1024]{1,0:T(8,128)(2,1)S(1)}, bf16[64,1024]{1,0:T(8,128)(2,1)S(1)}, u32[]{:S(2)}, u32[]{:S(2)}) collective-permute-start(bf16[64,1024]{1,0:T(8,128)(2,1)S(1)} %get-tuple-element.34), channel_id=1, source_target_pairs={{0,64},{64,0},{128,192},{192,128},{1,65},{65,1},{129,193},{193,129... | collective-permute-start | bytes 393224 | tf_op jit(solution)/shard_map/ppermute | solution.py:19
  94.0 8.6 %collective-permute-start.30 = (bf16[64,1024]{1,0:T(8,128)(2,1)S(1)}, bf16[64,1024]{1,0:T(8,128)(2,1)S(1)}, u32[]{:S(2)}, u32[]{:S(2)}) collective-permute-start(bf16[64,1024]{1,0:T(8,128)(2,1)S(1)} %get-tuple-element.35), channel_id=1, source_target_pairs={{0,192},{64,128},{128,64},{192,0},{1,193},{65,129},{129,65},{193,1... | collective-permute-start | bytes 393224 | tf_op jit(solution)/shard_map/ppermute | solution.py:19
  102.6 6.4 %collective-permute-start.31 = (bf16[64,1024]{1,0:T(8,128)(2,1)S(1)}, bf16[64,1024]{1,0:T(8,128)(2,1)S(1)}, u32[]{:S(2)}, u32[]{:S(2)}) collective-permute-start(bf16[64,1024]{1,0:T(8,128)(2,1)S(1)} %total.5.a_ref), channel_id=1, source_target_pairs={{0,16},{16,0},{32,48},{48,32},{1,17},{17,1},{33,49},{49,33},{2,18}... | collective-permute-start | bytes 393224 | tf_op jit(solution)/shard_map/ppermute | solution.py:19
  102.7 12.0 %collective-permute-start.32 = (bf16[64,1024]{1,0:T(8,128)(2,1)S(1)}, bf16[64,1024]{1,0:T(8,128)(2,1)S(1)}, u32[]{:S(2)}, u32[]{:S(2)}) collective-permute-start(bf16[64,1024]{1,0:T(8,128)(2,1)S(1)} %total.5.a_ref), channel_id=1, source_target_pairs={{0,32},{16,48},{32,0},{48,16},{1,33},{17,49},{33,1},{49,17},{2,34}... | collective-permute-start | bytes 393224 | tf_op jit(solution)/shard_map/ppermute | solution.py:19
  105.3 12.5 %collective-permute-start.33 = (bf16[64,1024]{1,0:T(8,128)(2,1)S(1)}, bf16[64,1024]{1,0:T(8,128)(2,1)S(1)}, u32[]{:S(2)}, u32[]{:S(2)}) collective-permute-start(bf16[64,1024]{1,0:T(8,128)(2,1)S(1)} %total.5.a_ref), channel_id=1, source_target_pairs={{0,48},{16,32},{32,16},{48,0},{1,49},{17,33},{33,17},{49,1},{2,50}... | collective-permute-start | bytes 393224 | tf_op jit(solution)/shard_map/ppermute | solution.py:19
  118.0 7.4 %collective-permute-start.34 = (bf16[64,1024]{1,0:T(8,128)(2,1)S(1)}, bf16[64,1024]{1,0:T(8,128)(2,1)S(1)}, u32[]{:S(2)}, u32[]{:S(2)}) collective-permute-start(bf16[64,1024]{1,0:T(8,128)(2,1)S(1)} %finish.1.refs_0_), channel_id=1, source_target_pairs={{0,128},{64,192},{128,0},{192,64},{1,129},{65,193},{129,1},{193,65... | collective-permute-start | bytes 393224 | tf_op jit(solution)/shard_map/ppermute | solution.py:19
  118.2 7.1 %collective-permute-start.35 = (bf16[64,1024]{1,0:T(8,128)(2,1)S(1)}, bf16[64,1024]{1,0:T(8,128)(2,1)S(1)}, u32[]{:S(2)}, u32[]{:S(2)}) collective-permute-start(bf16[64,1024]{1,0:T(8,128)(2,1)S(1)} %finish.1.refs_0_), channel_id=1, source_target_pairs={{0,64},{64,0},{128,192},{192,128},{1,65},{65,1},{129,193},{193,129... | collective-permute-start | bytes 393224 | tf_op jit(solution)/shard_map/ppermute | solution.py:19
  118.7 7.9 %collective-permute-start.36 = (bf16[64,1024]{1,0:T(8,128)(2,1)S(1)}, bf16[64,1024]{1,0:T(8,128)(2,1)S(1)}, u32[]{:S(2)}, u32[]{:S(2)}) collective-permute-start(bf16[64,1024]{1,0:T(8,128)(2,1)S(1)} %finish.1.refs_0_), channel_id=1, source_target_pairs={{0,192},{64,128},{128,64},{192,0},{1,193},{65,129},{129,65},{193,1... | collective-permute-start | bytes 393224 | tf_op jit(solution)/shard_map/ppermute | solution.py:19
  (16 other events, 64.3 us)
